TPU v7x, 32 devices: a whole 2x2x4 slice. The times are simulated.
32 devices in a mesh: sib: 4 (over z), ctx: 2 (over x), head: 4 (over y, core).
Axes of the slice: x: 2, y: 2, z: 4, core: 2. Of those that a mesh axis runs over, the one named last changes fastest.
Arguments:
- queries: bfloat16 [4, 1024, 4, 1536], P('sib', 'ctx', 'head'), may hold values from -8 to 8
- suffix_kv: bfloat16 [4, 1024, 4, 320], P('sib', 'ctx', 'head'), may hold values from -6 to 6
- prefix_kv: bfloat16 [16384, 4, 320], P(('sib', 'ctx'), 'head'), may hold values from -6 to 6
- pooling: float32 [2, 64], replicated, may hold values from 0.03 to 0.3
- gate_logits: float32 [4, 1024, 4, 24], P('sib', 'ctx', 'head'), may hold values from -6 to 6
- selected: int32 [4, 16, 4, 16], P('sib', 'ctx', 'head'), may hold values from 0 to 255, as said below
- lengths: int32 [4], P('sib'), may hold values from 128 to 1024, as said below
- w_out: bfloat16 [4096, 2560], P('head'), may hold values from -0.375 to 0.375
Outputs:
- layer_out: bfloat16 [4, 1024, 2560], P('sib', ('ctx', 'head'))
Inputs may be any that keep to these rules, and one draw needn't show every extreme that they name: For each sibling and group, the 16 indices of a query block are distinct, and the query blocks of one index of ctx (8 aligned query blocks) select together at most 24 blocks, counted with repeats, among any aligned range of 32 prefix blocks; some range is selected exactly 24 times in every such run. `lengths`: some sibling has the full length 1024 and some the length 128.
All inputs are finite; a program needn't handle non-finite values.
Results may differ from a plain program's by a relative error of at most 0.0096.
Values may be sent and summed in bfloat16 or wider, within the bound.
No kernel may reach another device: no remote copies, remote signals or barrier semaphores. Data moves between devices by JAX's collectives and lax.ppermute only.
A program may use at most 192 MiB of HBM per device.

v0:
```python
import jax
import jax.numpy as jnp
from jax import lax
from jax.sharding import PartitionSpec as P

DK = 192
DV = 128
HQ = 8
DM = 2560
BLK = 64
W = 512


def passed_along(value, axis, steps):
    count = lax.axis_size(axis)
    first, last = (max(0, -steps), min(count, count - steps))
    return lax.ppermute(value, axis, [(source, source + steps) for source in range(first, last)])


def earlier_rows(own_kv, distance):
    return passed_along(own_kv, "ctx", distance)


def softmax_parts(scores):
    row_max = jnp.max(scores, axis=-1, keepdims=True)
    weights = jnp.exp(scores - row_max)
    return (weights.astype(jnp.bfloat16), jnp.sum(weights, axis=-1, keepdims=True))


def shards(queries, suffix_kv, prefix_kv, pooling, gate_logits, selected, lengths, w_out):
    row_count = queries.shape[1]
    score_scale = DK ** (-0.5)
    query_rows = queries.reshape(row_count, HQ, DK)
    owned_blocks = prefix_kv.reshape(-1, BLK, DK + DV)
    block_count = owned_blocks.shape[0]
    owned_float = owned_blocks.astype(jnp.float32)
    comp_keys = jnp.einsum(
        "bjd,j->bd", owned_float[:, :, :DK], pooling[0], precision=lax.Precision.HIGHEST
    )
    comp_values = jnp.einsum(
        "bjd,j->bd", owned_float[:, :, DK:], pooling[1], precision=lax.Precision.HIGHEST
    )
    compressed = jnp.concatenate([comp_keys, comp_values], axis=-1).astype(jnp.bfloat16)
    segment = lax.all_gather(compressed, ("sib", "ctx"), axis=0, tiled=True)
    row_max = jnp.full((row_count, HQ), -1e30, jnp.float32)
    scores = (
        jnp.einsum("rhd,kd->rhk", query_rows, segment[:, :DK], preferred_element_type=jnp.float32)
        * score_scale
    )
    new_max = jnp.maximum(row_max, jnp.max(scores, axis=-1))
    weights = jnp.exp(scores - new_max[:, :, None])
    row_total = jnp.sum(weights, axis=-1)
    accumulated = jnp.einsum(
        "rhk,kd->rhd",
        weights.astype(jnp.bfloat16),
        segment[:, DK:],
        preferred_element_type=jnp.float32,
    )
    row_max, row_total, accumulated = (new_max, row_total, accumulated)
    comp_out = accumulated / row_total[:, :, None]
    own_kv = suffix_kv.reshape(row_count, DK + DV)
    window_reach = -(-W // row_count)
    near_parts = [earlier_rows(own_kv, 1)]
    near_kv = jnp.concatenate(near_parts + [own_kv], axis=0)
    row_begin = lax.axis_index("ctx") * row_count
    query_pos = row_begin + jnp.arange(row_count, dtype=jnp.int32)
    key_pos = (
        row_begin
        - window_reach * row_count
        + jnp.arange((window_reach + 1) * row_count, dtype=jnp.int32)
    )
    visible = (
        (key_pos[None, :] <= query_pos[:, None])
        & (key_pos[None, :] > query_pos[:, None] - W)
        & (key_pos[None, :] >= 0)
    )
    scores = (
        jnp.einsum("rhd,kd->rhk", query_rows, near_kv[:, :DK], preferred_element_type=jnp.float32)
        * score_scale
    )
    scores = jnp.where(visible[:, None, :], scores, -jnp.inf)
    weights, window_total = softmax_parts(scores)
    win_out = (
        jnp.einsum("rhk,kd->rhd", weights, near_kv[:, DK:], preferred_element_type=jnp.float32)
        / window_total
    )
    slot_ids = selected.reshape(-1)
    slot_count = slot_ids.shape[0]
    owner_count = lax.axis_size("sib") * lax.axis_size("ctx")
    capacity = max(2, (slot_count * 3 // 2 + owner_count - 1) // owner_count)
    slot_owner = slot_ids // block_count
    slot_local = slot_ids % block_count
    owner_match = (slot_owner[:, None] == jnp.arange(owner_count, dtype=jnp.int32)[None, :]).astype(
        jnp.int32
    )
    slot_rank = jnp.sum((jnp.cumsum(owner_match, axis=0) - 1) * owner_match, axis=1)
    slot_place = slot_owner * capacity + slot_rank
    place_match = (
        slot_place[:, None] == jnp.arange(owner_count * capacity, dtype=jnp.int32)[None, :]
    ).astype(jnp.int32)
    requests = (jnp.sum(place_match * (slot_local[:, None] + 1), axis=0) - 1).reshape(
        owner_count, capacity
    )
    wanted = lax.all_to_all(requests, ("sib", "ctx"), split_axis=0, concat_axis=0, tiled=True)
    served = jnp.take(owned_blocks, jnp.maximum(wanted, 0), axis=0)
    received = lax.all_to_all(served, ("sib", "ctx"), split_axis=0, concat_axis=0, tiled=True)
    picked = jnp.take(received.reshape(owner_count * capacity, BLK, DK + DV), slot_place, axis=0)
    blocks_here = row_count // BLK
    picked = picked.reshape(blocks_here, -1, DK + DV)
    query_blocks = query_rows.reshape(blocks_here, BLK, HQ, DK)
    scores = (
        jnp.einsum(
            "qthd,qkd->qhtk", query_blocks, picked[:, :, :DK], preferred_element_type=jnp.float32
        )
        * score_scale
    )
    weights, selected_total = softmax_parts(scores)
    sel_out = (
        jnp.einsum("qhtk,qkd->qhtd", weights, picked[:, :, DK:], preferred_element_type=jnp.float32)
        / selected_total
    )
    sel_out = jnp.transpose(sel_out, (0, 2, 1, 3)).reshape(row_count, HQ, DV)
    gate_values = jax.nn.sigmoid(gate_logits.reshape(row_count, 3, HQ))
    head_out = (
        gate_values[:, 0, :, None] * comp_out
        + gate_values[:, 1, :, None] * sel_out
        + gate_values[:, 2, :, None] * win_out
    )
    head_out = jnp.where((query_pos < lengths[0])[:, None, None], head_out, 0.0)
    head_flat = head_out.astype(jnp.bfloat16).reshape(row_count, HQ * DV)
    summed = lax.psum_scatter(
        jnp.dot(head_flat, w_out, preferred_element_type=jnp.float32),
        "head",
        scatter_dimension=0,
        tiled=True,
    )
    return summed.astype(jnp.bfloat16).reshape(1, -1, DM)


def solution(mesh):
    return jax.shard_map(
        shards,
        mesh=mesh,
        in_specs=(
            P("sib", "ctx", "head", None),
            P("sib", "ctx", "head", None),
            P(("sib", "ctx"), "head", None),
            P(),
            P("sib", "ctx", "head", None),
            P("sib", "ctx", "head", None),
            P("sib"),
            P("head", None),
        ),
        out_specs=P("sib", ("ctx", "head"), None),
        check_vma=False,
    )
```

profile of v0, /device:TPU:0, one launch (start us, length us, event | category | flops | bytes accessed | tf_op | source)
XLA Modules:
  0.0 415.6 jit_solution(11768520194902839958)
XLA Ops:
  6.5 0.5 broadcast.381
  7.0 1.3 reduce.5
  8.4 0.1 reshape.313
  8.5 0.1 fusion.37
  8.6 0.2 reduce_window_sum.11
  8.8 0.2 select_reduce_fusion.1
  8.9 0.1 select_reduce_fusion
  9.1 0.7 sub.57
  9.8 7.3 %all-to-all-start = ((s32[8,1,24]{2,1,0:T(1,128)}), s32[8,1,24]{2,1,0:T(1,128)S(1)}, u32[]{:S(2)}, u32[]{:S(2)}) async-start(s32[8,1,24]{2,1,0:T(1,128)} %sub.57), calls=%async_computation | async-start | bytes 8192 | tf_op jit(solution)/shard_map/all_to_all | solution.py:104
  17.0 1.8 copy.48
  18.8 4.6 %all-to-all-done = s32[8,1,24]{2,1,0:T(1,128)S(1)} async-done(((s32[8,1,24]{2,1,0:T(1,128)}), s32[8,1,24]{2,1,0:T(1,128)S(1)}, u32[]{:S(2)}, u32[]{:S(2)}) %all-to-all-start) | async-done | bytes 800 | tf_op jit(solution)/shard_map/all_to_all | solution.py:104
  23.4 0.1 reshape.322
  23.5 10.0 %gather_fusion = bf16[192,64,320]{2,1,0:T(8,128)(2,1)} fusion(bf16[32,64,320]{2,1,0:T(8,128)(2,1)S(1)} %bitcast.124, s32[1024]{0:T(1024)S(1)} %pad_clamp_fusion.1), kind=kCustom, calls=%fused_computation | custom fusion | bytes 15729408 | tf_op jit(solution)/shard_map/jit(_take)/gather | solution.py:105
  33.5 8.4 %broadcast_select_fusion = bf16[8,24,64,320]{3,2,1,0:T(8,128)(2,1)} fusion(bf16[8,24,64,320]{3,2,1,0:T(8,128)(2,1)} %bitcast.127, pred[8,24]{1,0:T(8,128)(4,1)S(1)} %compare_bitcast_fusion), kind=kLoop, calls=%fused_computation.12 | loop fusion | flops 3932160 | bytes 15728832 | tf_op jit(solution)/shard_map/jit(_take)/select_n | solution.py:105
  41.9 5.2 %all-to-all-start.1 = ((bf16[8,24,64,320]{3,2,1,0:T(8,128)(2,1)}), bf16[8,24,64,320]{3,2,1,0:T(8,128)(2,1)}, u32[]{:S(2)}, u32[]{:S(2)}) async-start(bf16[8,24,64,320]{3,2,1,0:T(8,128)(2,1)} %broadcast_select_fusion), calls=%async_computation.1 | async-start | bytes 18874368 | tf_op jit(solution)/shard_map/all_to_all | solution.py:106
  47.1 0.0 reduce-scatter.2.cloned.1.call-start
  47.2 0.0 copy-done.8
  47.2 4.5 %collective-permute-start = (bf16[512,320]{0,1:T(8,128)(2,1)S(1)}, bf16[512,320]{0,1:T(8,128)(2,1)}, u32[]{:S(2)}, u32[]{:S(2)}) collective-permute-start(bf16[512,320]{0,1:T(8,128)(2,1)S(1)} %bitcast.143), channel_id=1, source_target_pairs={{0,4},{1,5},{2,6},{3,7},{8,12},{9,13},{10,14},{11,15},{16,20},{17,... | collective-permute-start | bytes 983048 | tf_op jit(solution)/shard_map/ppermute | solution.py:17
  51.7 0.1 reduce_sum.51
  51.8 0.0 copy-done.6
  51.8 0.1 reshape.315
  51.8 0.0 copy-done.2
  51.8 1.6 copy.50
  53.4 0.0 copy-done.7
  53.4 0.5 fusion.24
  54.0 0.5 fusion.28
  55.1 0.1 pad_maximum_fusion.1
  55.2 216.6 %all_gather.3 = bf16[256,320]{1,0:T(8,128)(2,1)S(1)} all-gather(bf16[32,320]{1,0:T(8,128)(2,1)S(1)} %pad_maximum_fusion.1), channel_id=1, replica_groups=mesh['sib'=4,'ctx'=2,'head'=4] {'sib','ctx'}, dimensions={0}, use_global_device_ids=true | all-gather | bytes 184320 | tf_op jit(solution)/shard_map/all_gather | solution.py:44
  271.8 2.1 bitcast_reduce_fusion.1
  274.0 0.0 copy-start
  274.0 0.0 copy-done.5
  274.1 1.0 and_and_fusion
  275.1 0.0 copy-start.4
  275.1 0.8 copy-done
  275.9 2.3 fusion.17
  278.2 0.6 fusion.43
  278.8 3.3 reshape_reshape.3
  282.1 0.1 broadcast_in_dim.71
  282.2 0.1 broadcast_in_dim.72
  282.3 0.0 copy-start.3
  282.3 3.0 fusion.14
  285.3 0.0 collective-permute-done
  285.3 0.0 copy-done.3
  285.4 8.2 %fusion.5 = (f32[512,8]{0,1:T(8,128)S(1)}, f32[1024,512,8]{1,0,2:T(8,128)}) fusion(pred[512,1024]{0,1:T(8,128)(4,1)S(1)} %and_and_fusion, bf16[512,8,192]{0,2,1:T(8,128)(2,1)S(1)} %bitcast.133, bf16[512,320]{0,1:T(8,128)(2,1)S(1)} %bitcast.144, bf16[512,320]{0,1:T(8,128)(2,1)} %collective-permute-done), kind=kOutput, calls=%fused_computation.11 | convolution fusion | flops 1623977984 | bytes 19546112 | tf_op jit(solution)/shard_map/rhd,kd->rhk/dot_general | solution.py:78
  293.6 0.0 copy-done.4
  293.6 9.2 %fusion.1 = f32[512,8]{0,1:T(8,128)S(1)} fusion(f32[1024,512,8]{1,0,2:T(8,128)} %get-tuple-element.15, f32[512,8]{0,1:T(8,128)S(1)} %get-tuple-element.14, pred[512,1024]{0,1:T(8,128)(4,1)S(1)} %and_and_fusion), kind=kLoop, calls=%fused_computation.7 | loop fusion | flops 16773120 | bytes 17334272 | tf_op jit(solution)/shard_map/reduce_sum | solution.py:27
  302.8 0.0 all-to-all-done.1
  302.8 7.8 %gather_fusion.1 = bf16[128,64,320]{2,1,0:T(8,128)(2,1)} fusion(bf16[192,64,320]{2,1,0:T(8,128)(2,1)} %bitcast.20, s32[1024]{0:T(1024)S(1)} %pad_clamp_fusion), kind=kCustom, calls=%fused_computation.1 | custom fusion | bytes 10486272 | tf_op jit(solution)/shard_map/jit(_take)/gather | solution.py:107
  310.6 8.2 %copy.54 = bf16[8,1024,320]{1,2,0:T(8,128)(2,1)} copy(bf16[8,1024,320]{2,1,0:T(8,128)(2,1)} %bitcast.128) | data formatting | bytes 10485760 | tf_op jit(solution)/shard_map/jit(_take)/gather | solution.py:107
  318.8 5.3 %broadcast_select_fusion.1 = bf16[8,1024,320]{1,2,0:T(8,128)(2,1)} fusion(bf16[8,1024,320]{1,2,0:T(8,128)(2,1)} %copy.54, pred[8,1024]{1,0:T(8,128)(4,1)S(1)} %broadcast_in_dim.72), kind=kLoop, calls=%fused_computation.18 | loop fusion | flops 2621440 | bytes 10493952 | tf_op jit(solution)/shard_map/jit(_take)/select_n | solution.py:107
  324.0 4.1 bitcast_reduce_fusion
  328.2 0.0 copy-start.1
  328.2 3.7 fusion.3
  331.9 0.0 copy-done.1
  331.9 4.8 %bitcast_divide_fusion = f32[8,64,8,128]{3,1,2,0:T(8,128)} fusion(bf16[8,1024,320]{1,2,0:T(8,128)(2,1)S(1)} %copy-done.1, f32[8,1024,64,8]{1,2,3,0:T(8,128)S(1)} %get-tuple-element.11, f32[8,8,64]{2,1,0:T(8,128)S(1)} %get-tuple-element.10, f32[8,64,8]{1,2,0:T(8,128)S(1)} %bitcast.141), kind=kOutput, calls=%fused_computation.28 | convolution fusion | flops 1086849024 | bytes 21037056 | tf_op jit(solution)/shard_map/qhtk,qkd->qhtd/dot_general | solution.py:119
  336.7 2.8 copy.57
  339.5 0.0 slice-start
  339.5 1.9 copy.58
  341.4 0.0 copy-done.9
  341.4 9.7 %select_convert_fusion = bf16[512,8,128]{0,2,1:T(8,128)(2,1)S(1)} fusion(f32[512,8,128]{0,2,1:T(8,128)} %copy.58, f32[512,8,128]{0,2,1:T(8,128)} %fusion.17, f32[512,8]{0,1:T(8,128)S(1)} %fusion.1, f32[512,8]{0,1:T(8,128)S(1)} %get-tuple-element.6, f32[512,8]{0,1:T(8,128)S(1)} %get-tuple-element.7, f32[512,8]{0,1:T(8,128)S(1)} %fusion.14, ...), kind=kOutput, calls=%fused_computation.30 | convolution fusion | flops 1095761920 | bytes 23298560 | tf_op jit(solution)/shard_map/rhk,kd->rhd/dot_general | solution.py:84
  351.2 4.7 %fusion.56 = f32[512,2560]{1,0:T(8,128)} fusion(bf16[512,1024]{0,1:T(8,128)(2,1)S(1)} %bitcast.134, bf16[1024,2560]{1,0:T(8,128)(2,1)S(1)} %bitcast.131), kind=kOutput, calls=%fused_computation.106 | convolution fusion | flops 2684354560 | bytes 11534336 | tf_op jit(solution)/shard_map/dot_general | solution.py:132
  355.9 0.0 reduce-scatter.2.cloned.1.call-update
  355.9 50.7 %reduce-scatter.2.cloned.1.call-done = f32[128,2560]{1,0:T(8,128)} async-done(((f32[512,2560]{1,0:T(8,128)}), f32[128,2560]{1,0:T(8,128)}) %reduce-scatter.2.cloned.1.call-update) | async-done | bytes 1310736 | tf_op jit(solution)/shard_map/reduce_scatter | solution.py:131
  406.6 2.2 convert_bitcast_fusion
  (27 shorter events, 0.2 us)
Async XLA Ops:
  9.8 13.6 %all-to-all-start = ((s32[8,1,24]{2,1,0:T(1,128)}), s32[8,1,24]{2,1,0:T(1,128)S(1)}, u32[]{:S(2)}, u32[]{:S(2)}) async-start(s32[8,1,24]{2,1,0:T(1,128)} %sub.57), calls=%async_computation | async-start | bytes 8192 | tf_op jit(solution)/shard_map/all_to_all | solution.py:104
  41.9 5.2 %copy-start.8 = (bf16[1,512,1,320]{1,3,2,0:T(8,128)(2,1)S(1)}, bf16[1,512,1,320]{1,3,2,0:T(8,128)(2,1)}, u32[]{:S(2)}) copy-start(bf16[1,512,1,320]{1,3,2,0:T(8,128)(2,1)} %param.9) | copy-start | bytes 983044
  41.9 9.8 %copy-start.6 = (s32[1,8,1,16]{3,2,1,0:T(1,128)S(1)}, s32[1,8,1,16]{3,2,1,0:T(1,128)}, u32[]{:S(2)}) copy-start(s32[1,8,1,16]{3,2,1,0:T(1,128)} %param.13) | copy-start | bytes 1540
  41.9 9.9 %copy-start.2 = (bf16[1,512,1,1536]{3,1,2,0:T(8,128)(2,1)S(1)}, bf16[1,512,1,1536]{3,1,2,0:T(8,128)(2,1)}, u32[]{:S(2)}) copy-start(bf16[1,512,1,1536]{3,1,2,0:T(8,128)(2,1)} %param.8) | copy-start | bytes 4718596
  41.9 11.5 %copy-start.7 = (f32[2,64]{1,0:T(2,128)S(1)}, f32[2,64]{1,0:T(2,128)}, u32[]{:S(2)}) copy-start(f32[2,64]{1,0:T(2,128)} %param.11) | copy-start | bytes 1540
  41.9 260.9 %all-to-all-start.1 = ((bf16[8,24,64,320]{3,2,1,0:T(8,128)(2,1)}), bf16[8,24,64,320]{3,2,1,0:T(8,128)(2,1)}, u32[]{:S(2)}, u32[]{:S(2)}) async-start(bf16[8,24,64,320]{3,2,1,0:T(8,128)(2,1)} %broadcast_select_fusion), calls=%async_computation.1 | async-start | bytes 18874368 | tf_op jit(solution)/shard_map/all_to_all | solution.py:106
  47.1 359.5 %reduce-scatter.2.cloned.1.call-start = ((), (), s32[]{:S(2)}) async-start(), calls=%async_computation.3 | async-start | bytes 6553600 | tf_op jit(solution)/shard_map/reduce_scatter | solution.py:131
  47.2 238.2 %collective-permute-start = (bf16[512,320]{0,1:T(8,128)(2,1)S(1)}, bf16[512,320]{0,1:T(8,128)(2,1)}, u32[]{:S(2)}, u32[]{:S(2)}) collective-permute-start(bf16[512,320]{0,1:T(8,128)(2,1)S(1)} %bitcast.143), channel_id=1, source_target_pairs={{0,4},{1,5},{2,6},{3,7},{8,12},{9,13},{10,14},{11,15},{16,20},{17,... | collective-permute-start | bytes 983048 | tf_op jit(solution)/shard_map/ppermute | solution.py:17
  53.4 220.6 %copy-start.5 = (f32[1,512,1,24]{1,3,2,0:T(8,128)S(1)}, f32[1,512,1,24]{1,3,2,0:T(8,128)}, u32[]{:S(2)}) copy-start(f32[1,512,1,24]{1,3,2,0:T(8,128)} %param.12) | copy-start | bytes 147460
  274.0 1.9 copy-start
  275.1 18.5 %copy-start.4 = (pred[512,1024]{0,1:T(8,128)(4,1)}, pred[512,1024]{0,1:T(8,128)(4,1)S(1)}, u32[]{:S(2)}) copy-start(pred[512,1024]{0,1:T(8,128)(4,1)S(1)} %and_and_fusion) | copy-start | bytes 1572868
  282.3 3.0 copy-start.3
  328.2 3.7 copy-start.1
  336.7 4.7 %copy-start.9 = (pred[512]{0:T(512)(128)(4,1)S(1)}, pred[512]{0:T(512)(128)(4,1)}, u32[]{:S(2)}) copy-start(pred[512]{0:T(512)(128)(4,1)} %fusion.43) | copy-start | bytes 1540
  339.5 11.7 %slice-start = ((s8[5242880]{0:T(1024)(128)(4,1)}), s8[1048576]{0:T(1024)(128)(4,1)S(1)}, s32[]{:S(2)}) async-start(s8[5242880]{0:T(1024)(128)(4,1)} %bitcast.130), calls=%async_computation.4 | async-start | bytes 2097152
  341.4 9.7 %slice-start.1 = ((s8[5242880]{0:T(1024)(128)(4,1)}), s8[4194304]{0:T(1024)(128)(4,1)S(1)}, s32[]{:S(2)}) async-start(s8[5242880]{0:T(1024)(128)(4,1)} %bitcast.130), calls=%async_computation.5 | async-start | bytes 8388608
Sparse Core Ops, SparseCore 0:
  356.0 50.5 reduce-scatter.1
where the time goes:
time: 416 us
  blocking collectives  217 us (52%)
  waiting for transfers between devices  55.3 us (13%)
  local copies, waits for them, and re-layouts  40 us (10%)
  matrix products  37 us (9%)
  other arithmetic  35.5 us (9%)
  starting transfers between devices  17 us (4%)
  between operations  14.4 us (3%)
    all_gather x1, blocking collectives, shards(): segment = lax.all_gather(compressed, ('sib', 'ctx'), axis=0, tiled=True)  217 us
    reduce_scatter x1, waiting for transfers between devices, shards(): lax.psum_scatter(jnp.dot(head_flat, w_out, preferred_element_type=jnp.flo...  50.7 us
    gather x2, local copies, waits for them, and re-layouts, shards(): jnp.take(received.reshape(owner_count * capacity, BLK, DK + DV), slot_pla...  16 us
    reduce_sum x2, other arithmetic, softmax_parts(): jnp.sum(weights, axis=-1, keepdims=True)  12.8 us
    gather x1, local copies, waits for them, and re-layouts, shards(): served = jnp.take(owned_blocks, jnp.maximum(wanted, 0), axis=0)  10 us
    dot_general x1, matrix products, shards(): jnp.einsum('rhk,kd->rhd', weights, near_kv[:, DK:], preferred_element_typ...  9.72 us
    select_n x1, other arithmetic, shards(): served = jnp.take(owned_blocks, jnp.maximum(wanted, 0), axis=0)  8.4 us
  transfers between devices with their start and end apart: 4, of which 2 were waited for; matrix products, arithmetic and copies ran while one was open for 8% of the time, Pallas kernels for 0%

commit v1 on v0

v1 whole, which is shorter than its diff:
```python
import functools

import jax
import jax.numpy as jnp
from jax import lax
from jax.experimental import pallas as pl
from jax.experimental.pallas import tpu as pltpu
from jax.sharding import PartitionSpec as P

DK = 192
DV = 128
HQ = 8
DM = 2560
BLK = 64
W = 512
LANES = 128
TAIL = DK - LANES
EXT = 2 * LANES
ROWS = BLK + BLK // 2 + BLK
QUAD = 4
SCALE = DK ** (-0.5)
LOW = -1e30
VMEM = 56 * 1024 * 1024
BF = jnp.bfloat16
F32 = jnp.float32


def params(**more):
    return pltpu.CompilerParams(vmem_limit_bytes=VMEM, **more)


def cost(microseconds):
    return pl.CostEstimate(flops=int(microseconds * 1e9), bytes_accessed=0, transcendentals=0)


def lane_is_low(shape):
    return lax.broadcasted_iota(jnp.int32, shape, len(shape) - 1) < TAIL


def pack_kernel(kv_ref, pool_ref, packed_ref, comp_ref):
    tokens = kv_ref.shape[1]
    pool = pool_ref[...]
    pool_key = jnp.broadcast_to(pool[:, 0:1], (BLK, LANES))
    pool_value = jnp.broadcast_to(pool[:, 1:2], (BLK, LANES))
    half = BLK // 2
    pool_tail = jnp.where(lane_is_low((half, LANES)), pool_key[:half], pool_key[half:])
    rows = []
    for tile in range(tokens // LANES):
        part = kv_ref[:, tile * LANES : (tile + 1) * LANES].astype(F32)
        keys = part[:LANES].T
        ends = part[LANES:DK]
        ends = jnp.concatenate([ends, pltpu.roll(ends, LANES - half, 1)], axis=0).T
        values = part[DK:].T
        for sub in range(LANES // BLK):
            base = (tile * (LANES // BLK) + sub) * ROWS
            at = sub * BLK
            key, end, value = keys[at : at + BLK], ends[at : at + half], values[at : at + BLK]
            packed_ref[base : base + BLK] = key.astype(BF)
            packed_ref[base + BLK : base + BLK + half] = end.astype(BF)
            packed_ref[base + BLK + half : base + ROWS] = value.astype(BF)
            comp_key = jnp.sum(key * pool_key, axis=0, keepdims=True)
            comp_end = jnp.sum(end * pool_tail, axis=0, keepdims=True)
            comp_end = comp_end + pltpu.roll(comp_end, TAIL, 1)
            comp_end = jnp.where(lane_is_low((1, LANES)), comp_end, 0.0)
            comp_value = jnp.sum(value * pool_value, axis=0, keepdims=True)
            rows.append(jnp.concatenate([comp_key, comp_end, comp_value], axis=1))
    comp_ref[...] = jnp.concatenate(rows, axis=0).astype(BF)


def pack(kv_t, pooling):
    blocks = kv_t.shape[1] // BLK
    return pl.pallas_call(
        pack_kernel,
        out_shape=(
            jax.ShapeDtypeStruct((blocks * ROWS, LANES), BF),
            jax.ShapeDtypeStruct((blocks, EXT + DV), BF),
        ),
        compiler_params=params(),
        cost_estimate=cost(5),
        name="pack",
    )(kv_t, pooling.T)


def wide_queries_kernel(q_ref, out_ref):
    low = lane_is_low((BLK, LANES))
    for pair in range(HQ // 2):
        at = pair * 2 * DK
        first, middle, last = (
            q_ref[:, at + k * LANES : at + (k + 1) * LANES].astype(F32) for k in range(3)
        )
        middle_swap = pltpu.roll(middle, TAIL, 1)
        last_swap = pltpu.roll(last, TAIL, 1)
        top = pair * 2 * BLK
        out_ref[0, top : top + BLK, :LANES] = first.astype(BF)
        out_ref[0, top : top + BLK, LANES:] = jnp.where(low, middle, middle_swap).astype(BF)
        top += BLK
        out_ref[0, top : top + BLK, :LANES] = jnp.where(low, middle_swap, last_swap).astype(BF)
        out_ref[0, top : top + BLK, LANES:] = jnp.where(low, last_swap, last).astype(BF)


def wide_queries(queries):
    rows = queries.shape[0]
    return pl.pallas_call(
        wide_queries_kernel,
        grid=(rows // BLK,),
        in_specs=[pl.BlockSpec((BLK, HQ * DK), lambda i: (i, 0))],
        out_specs=pl.BlockSpec((1, HQ * BLK, EXT), lambda i: (i, 0, 0)),
        out_shape=jax.ShapeDtypeStruct((rows // BLK, HQ * BLK, EXT), BF),
        compiler_params=params(),
        cost_estimate=cost(6),
        name="wide_queries",
    )(queries)


def scores_of(keys, queries):
    return lax.dot_general(keys, queries, (((1,), (1,)), ((), ())), preferred_element_type=F32)


def near_kernel(begin_ref, q_ref, far_ref, own_ref, comp_ref, gate_ref, out_ref, key_ref, value_ref):
    step = pl.program_id(0)
    rows = own_ref.shape[1]

    @pl.when(step == 0)
    def _():
        zeros = jnp.zeros((LANES, TAIL), BF)
        for source, top in ((far_ref, 0), (own_ref, rows)):
            for at in range(0, rows, LANES):
                part = source[:DK, at : at + LANES].astype(F32)
                key_ref[top + at : top + at + LANES, :LANES] = part[:LANES].T.astype(BF)
                end = jnp.concatenate([part[LANES:], jnp.zeros((TAIL, LANES), F32)], axis=0)
                key_ref[top + at : top + at + LANES, LANES:] = end.T.astype(BF)
            value_ref[:, top : top + rows] = source[DK:, :]

    queries = q_ref[0]
    gates = gate_ref[0]
    total_lanes = queries.shape[0]
    scores = scores_of(comp_ref[:, :EXT], queries)
    top = jnp.max(scores, axis=0, keepdims=True)
    weights = jnp.exp((scores - top) * SCALE)
    total = jnp.sum(weights, axis=0, keepdims=True)
    comp_out = lax.dot_general(
        comp_ref[:, EXT:], weights.astype(BF), (((0,), (0,)), ((), ())), preferred_element_type=F32
    )
    out = comp_out * (gates[0:1] / total)

    span = W + LANES
    start = pl.multiple_of((step // 2) * LANES + rows - W, LANES)
    scores = scores_of(key_ref[pl.ds(start, span), :], queries)
    key_pos = start - rows + lax.broadcasted_iota(jnp.int32, (span, total_lanes), 0)
    query_pos = step * BLK + (lax.broadcasted_iota(jnp.int32, (span, total_lanes), 1) & (BLK - 1))
    visible = (key_pos <= query_pos) & (key_pos > query_pos - W) & (key_pos + begin_ref[0] >= 0)
    scores = jnp.where(visible, scores, LOW)
    top = jnp.max(scores, axis=0, keepdims=True)
    weights = jnp.exp((scores - top) * SCALE)
    total = jnp.sum(weights, axis=0, keepdims=True)
    window_out = jnp.dot(
        value_ref[:, pl.ds(start, span)], weights.astype(BF), preferred_element_type=F32
    )
    out_ref[0] = out + window_out * (gates[2:3] / total)


def near_parts(begin, wide, far_t, own_t, comp, gates):
    steps, lanes, _ = wide.shape
    rows = own_t.shape[1]
    whole = lambda array: pl.BlockSpec(array.shape, lambda i, *_: (0,) * array.ndim)
    return pl.pallas_call(
        near_kernel,
        grid_spec=pltpu.PrefetchScalarGridSpec(
            num_scalar_prefetch=1,
            grid=(steps,),
            in_specs=[
                pl.BlockSpec((1, lanes, EXT), lambda i, *_: (i, 0, 0)),
                whole(far_t),
                whole(own_t),
                whole(comp),
                pl.BlockSpec((1, 3, lanes), lambda i, *_: (i, 0, 0)),
            ],
            out_specs=pl.BlockSpec((1, DV, lanes), lambda i, *_: (i, 0, 0)),
            scratch_shapes=[pltpu.VMEM((2 * rows, EXT), BF), pltpu.VMEM((DV, 2 * rows), BF)],
        ),
        out_shape=jax.ShapeDtypeStruct((steps, DV, lanes), F32),
        compiler_params=params(),
        cost_estimate=cost(14),
        name="near",
    )(begin, wide, far_t, own_t, comp, gates)


def selected_step(block, ids_ref, owner_ref, q_ref, kv_refs, state, list_ref, key_ref, value_ref):
    top_k = ids_ref.shape[1]
    held = kv_refs[0].shape[0] // ROWS
    count = jnp.int32(0)
    for slot in range(top_k):
        index = ids_ref[block, slot]
        owner = index // held
        entry = jnp.int32(-1)
        for place in range(len(kv_refs)):
            entry = jnp.where(owner == owner_ref[place], place * held + index % held, entry)
        list_ref[count] = entry
        count = count + (entry >= 0).astype(jnp.int32)
    half = BLK // 2
    low = lane_is_low((half, LANES))

    def quad(step, state):
        top, total, acc = state
        for k in range(QUAD):
            entry = list_ref[jnp.minimum(step * QUAD + k, count - 1)]
            place, base = entry // held, pl.multiple_of((entry % held) * ROWS, 16)
            for at, kv_ref in enumerate(kv_refs):

                @pl.when(place == at)
                def _():
                    to = k * BLK
                    key_ref[to : to + BLK, :LANES] = kv_ref[pl.ds(base, BLK), :]
                    end = kv_ref[pl.ds(base + BLK, half), :]
                    zero = jnp.zeros_like(end)
                    key_ref[to : to + half, LANES:] = jnp.where(low, end, zero)
                    key_ref[to + half : to + BLK, LANES:] = jnp.where(low, zero, end)
                    value_ref[to : to + BLK, :] = kv_ref[pl.ds(base + BLK + half, BLK), :]

        scores = scores_of(key_ref[...], q_ref[0])
        row = lax.broadcasted_iota(jnp.int32, scores.shape, 0)
        scores = jnp.where(row < (count - step * QUAD) * BLK, scores, LOW)
        new_top = jnp.maximum(top, jnp.max(scores, axis=0, keepdims=True))
        weights = jnp.exp((scores - new_top) * SCALE)
        keep = jnp.exp((top - new_top) * SCALE)
        total = total * keep + jnp.sum(weights, axis=0, keepdims=True)
        acc = acc * keep + lax.dot_general(
            value_ref[...], weights.astype(BF), (((0,), (0,)), ((), ())), preferred_element_type=F32
        )
        return new_top, total, acc

    return lax.fori_loop(0, (count + QUAD - 1) // QUAD, quad, state)


def stage_kernel(first, n_kv, ids_ref, owner_ref, q_ref, *refs):
    kv_refs, refs = refs[:n_kv], refs[n_kv:]
    if first:
        state_out, acc_out, list_ref, key_ref, value_ref = refs
        lanes = q_ref.shape[1]
        state = (
            jnp.full((1, lanes), LOW, F32),
            jnp.zeros((1, lanes), F32),
            jnp.zeros((DV, lanes), F32),
        )
    else:
        state_in, acc_in, state_out, acc_out, list_ref, key_ref, value_ref = refs
        state = (state_in[0, 0:1], state_in[0, 1:2], acc_in[0])
    top, total, acc = selected_step(
        pl.program_id(0), ids_ref, owner_ref, q_ref, kv_refs, state, list_ref, key_ref, value_ref
    )
    state_out[0, 0:1] = top
    state_out[0, 1:2] = total
    acc_out[0] = acc


def scratch():
    return [
        pltpu.SMEM((64,), jnp.int32),
        pltpu.VMEM((QUAD * BLK, EXT), BF),
        pltpu.VMEM((QUAD * BLK, DV), BF),
    ]


def stage(ids, owners, wide, kvs, state):
    steps, lanes, _ = wide.shape
    row = pl.BlockSpec((1, 2, lanes), lambda i, *_: (i, 0, 0))
    wide_row = pl.BlockSpec((1, DV, lanes), lambda i, *_: (i, 0, 0))
    in_specs = [pl.BlockSpec((1, lanes, EXT), lambda i, *_: (i, 0, 0))]
    in_specs += [pl.BlockSpec(kv.shape, lambda i, *_: (0, 0)) for kv in kvs]
    first = state is None
    aliases = {}
    if not first:
        in_specs += [row, wide_row]
        aliases = {3 + len(kvs): 0, 4 + len(kvs): 1}
    return pl.pallas_call(
        functools.partial(stage_kernel, first, len(kvs)),
        grid_spec=pltpu.PrefetchScalarGridSpec(
            num_scalar_prefetch=2,
            grid=(steps,),
            in_specs=in_specs,
            out_specs=[row, wide_row],
            scratch_shapes=scratch(),
        ),
        out_shape=(
            jax.ShapeDtypeStruct((steps, 2, lanes), F32),
            jax.ShapeDtypeStruct((steps, DV, lanes), F32),
        ),
        input_output_aliases=aliases,
        compiler_params=params(),
        cost_estimate=cost(12),
        name="stage",
    )(ids, owners, wide, *kvs, *(() if first else state))


def last_kernel(n_kv, order_ref, ids_ref, owner_ref, q_ref, *refs):
    kv_refs, refs = refs[:n_kv], refs[n_kv:]
    state_in, acc_in, near_ref, gate_ref, out_ref, list_ref, key_ref, value_ref = refs
    state = (state_in[0, 0:1], state_in[0, 1:2], acc_in[0])
    block = order_ref[pl.program_id(0)]
    _, total, acc = selected_step(
        block, ids_ref, owner_ref, q_ref, kv_refs, state, list_ref, key_ref, value_ref
    )
    out = near_ref[0] + acc * (gate_ref[0, 1:2] / total)
    for head in range(0, HQ, 2):
        pair = out[:, head * BLK : (head + 2) * BLK].T.astype(BF)
        out_ref[:, head * DV : (head + 1) * DV] = pair[:BLK]
        out_ref[:, (head + 1) * DV : (head + 2) * DV] = pair[BLK:]


def last_stage(order, ids, owners, wide, kvs, state, near, gates):
    _, lanes, _ = wide.shape
    (steps,) = order.shape
    at = lambda i, order, *_: (order[i], 0, 0)
    return pl.pallas_call(
        functools.partial(last_kernel, len(kvs)),
        grid_spec=pltpu.PrefetchScalarGridSpec(
            num_scalar_prefetch=3,
            grid=(steps,),
            in_specs=[pl.BlockSpec((1, lanes, EXT), at)]
            + [pl.BlockSpec(kv.shape, lambda i, *_: (0, 0)) for kv in kvs]
            + [
                pl.BlockSpec((1, 2, lanes), at),
                pl.BlockSpec((1, DV, lanes), at),
                pl.BlockSpec((1, DV, lanes), at),
                pl.BlockSpec((1, 3, lanes), at),
            ],
            out_specs=pl.BlockSpec((BLK, HQ * DV), lambda i, *_: (i, 0)),
            scratch_shapes=scratch(),
        ),
        out_shape=jax.ShapeDtypeStruct((steps * BLK, HQ * DV), BF),
        compiler_params=params(),
        cost_estimate=cost(8),
        name="last_stage",
    )(order, ids, owners, wide, *kvs, *state, near, gates)


def swap(value, axis, bit):
    return lax.ppermute(value, axis, [(i, i ^ bit) for i in range(lax.axis_size(axis))])


def spread(value, axis, wraps, sib_shift):
    sib_count, count = lax.axis_size("sib"), lax.axis_size(axis)
    ring = wraps or count == 2
    reach = [count // 2, (count - 1) // 2] if ring else [count - 1, count - 1]
    held = [value, value]
    found = []
    for hop in range(1, max(reach) + 1):
        for side, sign in enumerate((1, -1)):
            if hop > reach[side]:
                continue
            pairs = []
            for source in range(count):
                target = source + sign
                if ring:
                    pairs.append((source, target % count))
                elif 0 <= target < count and 0 <= target - sign * hop < count:
                    pairs.append((source, target))
            axes = axis
            if axis == "ctx":
                axes = ("sib", "ctx")
                holders = [s for s in range(sib_count) if wraps or 0 <= s + sib_shift < sib_count]
                pairs = [(s * count + a, s * count + b) for s in holders for a, b in pairs]
            held[side] = lax.ppermute(held[side], axes, pairs)
            found.append((held[side], hop, -sign * hop))
    return found


def shards(wraps, queries, suffix_kv, prefix_kv, pooling, gate_logits, selected, lengths, w_out):
    rows = queries.shape[1]
    sib_count, ctx_count, head_count = (lax.axis_size(a) for a in ("sib", "ctx", "head"))
    blocks = rows // BLK
    sib, ctx, head = (lax.axis_index(a) for a in ("sib", "ctx", "head"))
    packed, comp = pack(prefix_kv[:, 0, :].T, pooling)

    own_t = suffix_kv[0, :, 0, :].T
    far_t = lax.ppermute(own_t, "ctx", [(i, i + 1) for i in range(ctx_count - 1)])
    for axis, count in (("ctx", ctx_count), ("sib", sib_count)):
        bit = 1
        while bit < count:
            comp = jnp.concatenate([comp, swap(comp, axis, bit)], axis=0)
            bit *= 2

    def owner_of(sib_shift, ctx_shift):
        s, c = sib + sib_shift, ctx + ctx_shift
        if wraps:
            s = s % sib_count
        if wraps or ctx_count == 2:
            c = c % ctx_count
        good = (s >= 0) & (s < sib_count) & (c >= 0) & (c < ctx_count)
        return jnp.where(good, s * ctx_count + c, -2)

    levels = {0: [(packed, 0)]}
    for array, hop, shift in spread(packed, "sib", wraps, 0):
        levels.setdefault(hop, []).append((array, shift))
    stages = []
    for hop, arrivals in levels.items():
        near_by, far_off = [], []
        for array, shift in arrivals:
            near_by.append((array, owner_of(shift, 0)))
            for other, _, ctx_shift in spread(array, "ctx", wraps, shift):
                far_off.append((other, owner_of(shift, ctx_shift)))
        stages.append((near_by, far_off))

    wide = wide_queries(queries.reshape(rows, HQ * DK))
    begin = (ctx * rows).astype(jnp.int32)
    gates = jax.nn.sigmoid(gate_logits.reshape(rows, 3, HQ))
    alive = begin + jnp.arange(rows, dtype=jnp.int32) < lengths[0]
    gates = jnp.where(alive[:, None, None], gates, 0.0)
    gates = gates.reshape(blocks, BLK, 3, HQ).transpose(0, 2, 3, 1).reshape(blocks, 3, HQ * BLK)
    near = near_parts(begin.reshape(1), wide, far_t, own_t, comp, gates)

    ids = selected.reshape(blocks, -1)
    work = []
    for near_by, far_off in stages[:-1]:
        work.append(near_by + far_off)
    work.append(stages[-1][0])
    state = None
    for items in work:
        owners = jnp.stack([o for _, o in items]).astype(jnp.int32)
        state = stage(ids, owners, wide, [a for a, _ in items], state)
    items = stages[-1][1]
    owners = jnp.stack([o for _, o in items]).astype(jnp.int32)
    kvs = [a for a, _ in items]

    half = head_count // 2
    chunk = rows // head_count
    per = chunk // BLK
    high, low = head // half, head % half

    def half_order(which):
        starts = [(which * half + (low ^ k)) * per for k in range(half - 1, -1, -1)]
        return jnp.concatenate([s + jnp.arange(per, dtype=jnp.int32) for s in starts])

    def half_sum(which):
        out = last_stage(half_order(which), ids, owners, wide, kvs, state, near, gates)
        share = jnp.dot(out, w_out, preferred_element_type=F32)
        other = swap(share[:chunk].astype(BF), "head", 1)
        return share[chunk:] + other.astype(F32)

    away = half_sum(1 - high)
    back = swap(away.astype(BF), "head", half)
    mine = half_sum(high)
    return (mine + back.astype(F32)).astype(BF).reshape(1, chunk, DM)


def solution(mesh):
    wraps = mesh.size >= 128
    return jax.shard_map(
        functools.partial(shards, wraps),
        mesh=mesh,
        in_specs=(
            P("sib", "ctx", "head", None),
            P("sib", "ctx", "head", None),
            P(("sib", "ctx"), "head", None),
            P(),
            P("sib", "ctx", "head", None),
            P("sib", "ctx", "head", None),
            P("sib"),
            P("head", None),
        ),
        out_specs=P("sib", ("ctx", "head"), None),
        check_vma=False,
    )
```

time: 416 us -> 199 us (0.48)
  the two profiles are of different devices: /device:TPU:0 before, /device:TPU:16 now
where the time goes in v1:
time: 199 us; the launch traced here: 197 us
  Pallas kernels  90.7 us (46%)
  waiting for transfers between devices  47.5 us (24%)
  starting transfers between devices  42 us (21%)
  matrix products  6.73 us (3%)
  other arithmetic  6.27 us (3%)
  local copies, waits for them, and re-layouts  3.44 us (2%)
    pallas_call x4, Pallas kernels, stage(): pl.pallas_call(functools.partial(stage_kernel, first, len(kvs)), grid_spe...  54.4 us
    ppermute x6, waiting for transfers between devices, swap(): lax.ppermute(value, axis, [(i, i ^ bit) for i in range(lax.axis_size(axis...  33.9 us
    ppermute x13, starting transfers between devices, spread(): held[side] = lax.ppermute(held[side], axes, pairs)  32.7 us
    pallas_call x1, Pallas kernels, near_parts(): pl.pallas_call(near_kernel, grid_spec=pltpu.PrefetchScalarGridSpec(num_sc...  13.8 us
    ppermute x13, waiting for transfers between devices, spread(): held[side] = lax.ppermute(held[side], axes, pairs)  13.6 us
    pallas_call x2, Pallas kernels, last_stage(): pl.pallas_call(functools.partial(last_kernel, len(kvs)), grid_spec=pltpu....  11.7 us
    dot_general x2, matrix products, half_sum(): share = jnp.dot(out, w_out, preferred_element_type=F32)  6.73 us
    pallas_call x1, Pallas kernels, wide_queries(): pl.pallas_call(wide_queries_kernel, grid=(rows // BLK,), in_specs=[pl.Blo...  5.94 us
  transfers between devices with their start and end apart: 20, of which 7 were waited for; matrix products, arithmetic and copies ran while one was open for 5% of the time, Pallas kernels for 41%

profile of v1, /device:TPU:16, one launch (start us, length us, event | category | flops | bytes accessed | tf_op | source)
XLA Modules:
  0.0 197.5 jit_solution(12131407371128104779)
XLA Ops:
  0.0 1.4 copy.17
  1.4 4.8 %pack.1 = (bf16[5120,128]{1,0:T(8,128)(2,1)}, bf16[32,384]{1,0:T(8,128)(2,1)}) custom-call(bf16[320,2048]{1,0:T(8,128)(2,1)} %bitcast.46, f32[64,2]{1,0:T(8,128)} %bitcast.42), custom_call_target="tpu_custom_call" | custom-call | flops 5000000000 | tf_op jit(solution)/shard_map/pack/pallas_call | solution.py:72
  6.1 1.5 collective-permute-start.12
  7.6 3.5 %collective-permute-start = (bf16[5120,128]{1,0:T(8,128)(2,1)}, bf16[5120,128]{1,0:T(8,128)(2,1)S(1)}, u32[]{:S(2)}, u32[]{:S(2)}) collective-permute-start(bf16[5120,128]{1,0:T(8,128)(2,1)} %get-tuple-element.15.refs_0_), channel_id=1, source_target_pairs={{0,8},{8,16},{16,24},{1,9},{9,17},{17,25},{2,10},{10,18},{18,26},{... | collective-permute-start | bytes 3932168 | tf_op jit(solution)/shard_map/ppermute | solution.py:363
  11.1 2.4 %collective-permute-start.4 = (bf16[5120,128]{1,0:T(8,128)(2,1)}, bf16[5120,128]{1,0:T(8,128)(2,1)S(1)}, u32[]{:S(2)}, u32[]{:S(2)}) collective-permute-start(bf16[5120,128]{1,0:T(8,128)(2,1)} %get-tuple-element.15.refs_0_), channel_id=1, source_target_pairs={{8,0},{16,8},{24,16},{9,1},{17,9},{25,17},{10,2},{18,10},{26,18},{... | collective-permute-start | bytes 3932168 | tf_op jit(solution)/shard_map/ppermute | solution.py:363
  13.5 0.6 collective-permute-start.14
  14.1 4.1 %collective-permute-start.13 = (bf16[320,512]{1,0:T(8,128)(2,1)S(1)}, bf16[320,512]{1,0:T(8,128)(2,1)}, u32[]{:S(2)}, u32[]{:S(2)}) collective-permute-start(bf16[320,512]{1,0:T(8,128)(2,1)S(1)} %bitcast.48), channel_id=1, source_target_pairs={{0,4},{1,5},{2,6},{3,7},{8,12},{9,13},{10,14},{11,15},{16,20},{17,... | collective-permute-start | bytes 983048 | tf_op jit(solution)/shard_map/ppermute | solution.py:376
  18.9 0.1 div.19
  19.0 0.6 pad_add_fusion.5.owner_ref
  19.5 0.6 pad_add_fusion.2.owner_ref
  20.2 0.6 pad_add_fusion.order_ref
  20.9 0.6 pad_add_fusion.1.owner_ref
  21.5 5.9 %wide_queries.1.q_ref = bf16[8,512,256]{2,1,0:T(8,128)(2,1)} custom-call(bf16[512,1536]{1,0:T(8,128)(2,1)} %bitcast.45), custom_call_target="tpu_custom_call" | custom-call | flops 6000000000 | tf_op jit(solution)/shard_map/wide_queries/pallas_call | solution.py:103
  27.4 0.6 pad_add_fusion.6.order_ref
  28.1 9.5 %collective-permute-done.14 = bf16[32,384]{1,0:T(8,128)(2,1)S(1)} collective-permute-done((bf16[32,384]{1,0:T(8,128)(2,1)}, bf16[32,384]{1,0:T(8,128)(2,1)S(1)}, u32[]{:S(2)}, u32[]{:S(2)}) %collective-permute-start.14) | collective-permute-done | bytes 24608 | tf_op jit(solution)/shard_map/ppermute | solution.py:338
  37.6 1.6 collective-permute-start.15
  39.2 0.7 pad_add_fusion.4.owner_ref
  39.9 0.1 reshape.34
  39.9 0.7 copy.19.gate_ref.refs_5_
  40.6 4.6 %collective-permute-done.15 = bf16[64,384]{1,0:T(8,128)(2,1)S(1)} collective-permute-done((bf16[64,384]{1,0:T(8,128)(2,1)S(1)}, bf16[64,384]{1,0:T(8,128)(2,1)S(1)}, u32[]{:S(2)}, u32[]{:S(2)}) %collective-permute-start.15) | collective-permute-done | bytes 49184 | tf_op jit(solution)/shard_map/ppermute | solution.py:338
  45.2 0.1 collective-permute-start.16
  45.3 0.6 pad_add_fusion.3.owner_ref
  45.9 4.9 %collective-permute-done.16 = bf16[128,384]{1,0:T(8,128)(2,1)S(1)} collective-permute-done((bf16[128,384]{1,0:T(8,128)(2,1)S(1)}, bf16[128,384]{1,0:T(8,128)(2,1)S(1)}, u32[]{:S(2)}, u32[]{:S(2)}) %collective-permute-start.16) | collective-permute-done | bytes 98336 | tf_op jit(solution)/shard_map/ppermute | solution.py:338
  50.8 0.7 pad_maximum_fusion.comp_ref
  51.5 0.0 collective-permute-done.refs_0_
  51.5 2.2 %collective-permute-start.10 = (bf16[5120,128]{1,0:T(8,128)(2,1)S(1)}, bf16[5120,128]{1,0:T(8,128)(2,1)}, u32[]{:S(2)}, u32[]{:S(2)}) collective-permute-start(bf16[5120,128]{1,0:T(8,128)(2,1)S(1)} %collective-permute-done.refs_0_), channel_id=1, source_target_pairs={{8,12},{12,8},{16,20},{20,16},{24,28},{28,24},{9,13},{13,9},{17,21... | collective-permute-start | bytes 3932168 | tf_op jit(solution)/shard_map/ppermute | solution.py:363
  53.7 2.2 %collective-permute-start.1 = (bf16[5120,128]{1,0:T(8,128)(2,1)S(1)}, bf16[5120,128]{1,0:T(8,128)(2,1)S(1)}, u32[]{:S(2)}, u32[]{:S(2)}) collective-permute-start(bf16[5120,128]{1,0:T(8,128)(2,1)S(1)} %collective-permute-done.refs_0_), channel_id=1, source_target_pairs={{8,16},{16,24},{9,17},{17,25},{10,18},{18,26},{11,19},{19,27},{12,... | collective-permute-start | bytes 3932168 | tf_op jit(solution)/shard_map/ppermute | solution.py:363
  55.9 0.0 collective-permute-done.4.refs_1_
  55.9 3.4 %collective-permute-start.11 = (bf16[5120,128]{1,0:T(8,128)(2,1)S(1)}, bf16[5120,128]{1,0:T(8,128)(2,1)}, u32[]{:S(2)}, u32[]{:S(2)}) collective-permute-start(bf16[5120,128]{1,0:T(8,128)(2,1)S(1)} %collective-permute-done.4.refs_1_), channel_id=1, source_target_pairs={{0,4},{4,0},{8,12},{12,8},{16,20},{20,16},{1,5},{5,1},{9,13},{13,9... | collective-permute-start | bytes 3932168 | tf_op jit(solution)/shard_map/ppermute | solution.py:363
  59.3 0.0 collective-permute-done.13.far_ref
  59.3 4.1 %collective-permute-start.5 = (bf16[5120,128]{1,0:T(8,128)(2,1)S(1)}, bf16[5120,128]{1,0:T(8,128)(2,1)S(1)}, u32[]{:S(2)}, u32[]{:S(2)}) collective-permute-start(bf16[5120,128]{1,0:T(8,128)(2,1)S(1)} %collective-permute-done.4.refs_1_), channel_id=1, source_target_pairs={{8,0},{16,8},{9,1},{17,9},{10,2},{18,10},{11,3},{19,11},{12,4},{20... | collective-permute-start | bytes 3932168 | tf_op jit(solution)/shard_map/ppermute | solution.py:363
  63.4 13.8 %near.1.refs_4_ = f32[8,128,512]{2,1,0:T(8,128)} custom-call(s32[1]{0:T(128)} %bitcast.19.begin_ref, bf16[8,512,256]{2,1,0:T(8,128)(2,1)} %wide_queries.1.q_ref, bf16[320,512]{1,0:T(8,128)(2,1)} %collective-permute-done.13.far_ref, bf16[320,512]{1,0:T(8,128)(2,1)} %bitcast.47, bf16[256,384]{1,0:T(8,128)(2,1)} %pad_maximum_fusion.comp_ref, ...), custom_call_target="tpu_custom_call" | custom-call | flops 14000000000 | tf_op jit(solution)/shard_map/near/pallas_call | solution.py:166
  77.2 5.3 %collective-permute-done.1.refs_0_ = bf16[5120,128]{1,0:T(8,128)(2,1)S(1)} collective-permute-done((bf16[5120,128]{1,0:T(8,128)(2,1)S(1)}, bf16[5120,128]{1,0:T(8,128)(2,1)S(1)}, u32[]{:S(2)}, u32[]{:S(2)}) %collective-permute-start.1) | collective-permute-done | bytes 1310752 | tf_op jit(solution)/shard_map/ppermute | solution.py:363
  82.6 3.3 %collective-permute-start.8 = (bf16[5120,128]{1,0:T(8,128)(2,1)S(1)}, bf16[5120,128]{1,0:T(8,128)(2,1)S(1)}, u32[]{:S(2)}, u32[]{:S(2)}) collective-permute-start(bf16[5120,128]{1,0:T(8,128)(2,1)S(1)} %collective-permute-done.1.refs_0_), channel_id=1, source_target_pairs={{16,20},{20,16},{24,28},{28,24},{17,21},{21,17},{25,29},{29,25},{1... | collective-permute-start | bytes 3932168 | tf_op jit(solution)/shard_map/ppermute | solution.py:363
  85.9 0.0 collective-permute-done.12.refs_1_
  85.9 3.3 %collective-permute-start.2 = (bf16[5120,128]{1,0:T(8,128)(2,1)S(1)}, bf16[5120,128]{1,0:T(8,128)(2,1)}, u32[]{:S(2)}, u32[]{:S(2)}) collective-permute-start(bf16[5120,128]{1,0:T(8,128)(2,1)S(1)} %collective-permute-done.1.refs_0_), channel_id=1, source_target_pairs={{16,24},{17,25},{18,26},{19,27},{20,28},{21,29},{22,30},{23,31}} | collective-permute-start | bytes 3932168 | tf_op jit(solution)/shard_map/ppermute | solution.py:363
  89.1 0.0 collective-permute-done.5.refs_1_
  89.1 1.7 collective-permute-start.9
  90.9 0.0 collective-permute-done.10.refs_2_
  90.9 1.7 collective-permute-start.6
  92.6 12.6 %stage.4 = (f32[8,2,512]{2,1,0:T(2,128)}, f32[8,128,512]{2,1,0:T(8,128)}) custom-call(s32[8,16]{1,0:T(8,128)} %bitcast.49, s32[2]{0:T(128)} %pad_add_fusion.5.owner_ref, bf16[8,512,256]{2,1,0:T(8,128)(2,1)} %wide_queries.1.q_ref, bf16[5120,128]{1,0:T(8,128)(2,1)} %get-tuple-element.15.refs_0_, bf16[5120,128]{1,0:T(8,128)(2,1)} %collective-permute-done.12.refs_1_), custom_call_target="tpu_custom_call" | custom-call | flops 12000000000 | tf_op jit(solution)/shard_map/stage/pallas_call | solution.py:275
  105.2 8.1 %collective-permute-done.11.refs_3_ = bf16[5120,128]{1,0:T(8,128)(2,1)} collective-permute-done((bf16[5120,128]{1,0:T(8,128)(2,1)S(1)}, bf16[5120,128]{1,0:T(8,128)(2,1)}, u32[]{:S(2)}, u32[]{:S(2)}) %collective-permute-start.11) | collective-permute-done | bytes 1310752 | tf_op jit(solution)/shard_map/ppermute | solution.py:363
  113.3 19.5 %stage.5 = (f32[8,2,512]{2,1,0:T(2,128)}, f32[8,128,512]{2,1,0:T(8,128)}) custom-call(s32[8,16]{1,0:T(8,128)} %bitcast.50, s32[4]{0:T(128)} %pad_add_fusion.4.owner_ref, bf16[8,512,256]{2,1,0:T(8,128)(2,1)} %wide_queries.1.q_ref, bf16[5120,128]{1,0:T(8,128)(2,1)} %copy-done.2, ...), custom_call_target="tpu_custom_call", output_to_operand_aliasing={{0}: (7, {}), {1}: (8, {})} | custom-call | flops 12000000000 | tf_op jit(solution)/shard_map/stage/pallas_call | solution.py:275
  132.8 1.7 collective-permute-start.3
  134.5 0.0 collective-permute-done.6.refs_1_
  134.5 1.8 collective-permute-start.7
  136.3 0.1 collective-permute-done.8.refs_2_
  136.5 0.0 collective-permute-done.9.refs_3_
  136.5 1.0 copy-done.6
  137.5 14.0 %stage.6 = (f32[8,2,512]{2,1,0:T(2,128)}, f32[8,128,512]{2,1,0:T(8,128)}) custom-call(s32[8,16]{1,0:T(8,128)} %bitcast.51, s32[4]{0:T(128)} %pad_add_fusion.3.owner_ref, bf16[8,512,256]{2,1,0:T(8,128)(2,1)} %wide_queries.1.q_ref, bf16[5120,128]{1,0:T(8,128)(2,1)} %copy-done.4, ...), custom_call_target="tpu_custom_call", output_to_operand_aliasing={{0}: (7, {}), {1}: (8, {})} | custom-call | flops 12000000000 | tf_op jit(solution)/shard_map/stage/pallas_call | solution.py:275
  151.5 8.4 %stage.7 = (f32[8,2,512]{2,1,0:T(2,128)}, f32[8,128,512]{2,1,0:T(8,128)}) custom-call(s32[8,16]{1,0:T(8,128)} %bitcast.52, s32[2]{0:T(128)} %pad_add_fusion.2.owner_ref, bf16[8,512,256]{2,1,0:T(8,128)(2,1)} %wide_queries.1.q_ref, bf16[5120,128]{1,0:T(8,128)(2,1)} %collective-permute-done.2.refs_0_, ...), custom_call_target="tpu_custom_call", output_to_operand_aliasing={{0}: (5, {}), {1}: (6, {})} | custom-call | flops 12000000000 | tf_op jit(solution)/shard_map/stage/pallas_call | solution.py:275
  159.9 5.9 %last_stage.3 = bf16[256,1024]{1,0:T(8,128)(2,1)} custom-call(s32[4]{0:T(128)} %pad_add_fusion.6.order_ref, s32[8,16]{1,0:T(8,128)} %bitcast.53, s32[2]{0:T(128)} %pad_add_fusion.1.owner_ref, bf16[8,512,256]{2,1,0:T(8,128)(2,1)} %wide_queries.1.q_ref, bf16[5120,128]{1,0:T(8,128)(2,1)} %collective-permute-done.3.refs_0_, ...), custom_call_target="tpu_custom_call" | custom-call | flops 8000000000 | tf_op jit(solution)/shard_map/last_stage/pallas_call | solution.py:314
  165.8 2.6 %fusion.6 = f32[256,2560]{1,0:T(8,128)S(1)} fusion(bf16[256,1024]{1,0:T(8,128)(2,1)} %last_stage.3, bf16[1024,2560]{1,0:T(8,128)(2,1)S(1)} %bitcast.44), kind=kOutput, calls=%fused_computation.27 | convolution fusion | flops 1342177280 | bytes 8388608 | tf_op jit(solution)/shard_map/dot_general | solution.py:436
  168.3 0.1 slice.34
  168.4 0.1 collective-permute-start.18
  168.5 5.9 %last_stage.2 = bf16[256,1024]{1,0:T(8,128)(2,1)} custom-call(s32[4]{0:T(128)} %pad_add_fusion.order_ref, s32[8,16]{1,0:T(8,128)} %bitcast.54, s32[2]{0:T(128)} %pad_add_fusion.1.owner_ref, bf16[8,512,256]{2,1,0:T(8,128)(2,1)} %wide_queries.1.q_ref, bf16[5120,128]{1,0:T(8,128)(2,1)} %collective-permute-done.3.refs_0_, ...), custom_call_target="tpu_custom_call" | custom-call | flops 8000000000 | tf_op jit(solution)/shard_map/last_stage/pallas_call | solution.py:314
  174.3 4.2 %fusion.5 = f32[256,2560]{1,0:T(8,128)S(1)} fusion(bf16[256,1024]{1,0:T(8,128)(2,1)} %last_stage.2, bf16[1024,2560]{1,0:T(8,128)(2,1)} %param.15), kind=kOutput, calls=%fused_computation.26 | convolution fusion | flops 1342177280 | bytes 8388608 | tf_op jit(solution)/shard_map/dot_general | solution.py:436
  178.5 0.1 slice.35
  178.6 0.6 collective-permute-start.17
  179.1 0.0 collective-permute-done.18
  179.2 0.1 fusion
  179.3 2.2 %collective-permute-start.19 = (bf16[128,2560]{1,0:T(8,128)(2,1)S(1)}, bf16[128,2560]{1,0:T(8,128)(2,1)S(1)}, u32[]{:S(2)}, u32[]{:S(2)}) collective-permute-start(bf16[128,2560]{1,0:T(8,128)(2,1)S(1)} %fusion), channel_id=1, source_target_pairs={{0,2},{1,3},{2,0},{3,1},{4,6},{5,7},{6,4},{7,5},{8,10},{9,11},{10,... | collective-permute-start | bytes 1966088 | tf_op jit(solution)/shard_map/ppermute | solution.py:338
  181.5 14.9 %collective-permute-done.19 = bf16[128,2560]{1,0:T(8,128)(2,1)S(1)} collective-permute-done((bf16[128,2560]{1,0:T(8,128)(2,1)S(1)}, bf16[128,2560]{1,0:T(8,128)(2,1)S(1)}, u32[]{:S(2)}, u32[]{:S(2)}) %collective-permute-start.19) | collective-permute-done | bytes 655392 | tf_op jit(solution)/shard_map/ppermute | solution.py:338
  196.4 1.1 fusion.3
  (31 shorter events, 0.1 us)
Async XLA Ops:
  1.4 12.7 %copy-start.7 = (bf16[1,512,1,320]{1,3,2,0:T(8,128)(2,1)S(1)}, bf16[1,512,1,320]{1,3,2,0:T(8,128)(2,1)}, u32[]{:S(2)}) copy-start(bf16[1,512,1,320]{1,3,2,0:T(8,128)(2,1)} %param.9) | copy-start | bytes 983044
  1.4 17.5 %copy-start.1 = (f32[1,512,1,24]{1,3,2,0:T(8,128)S(1)}, f32[1,512,1,24]{1,3,2,0:T(8,128)}, u32[]{:S(2)}) copy-start(f32[1,512,1,24]{1,3,2,0:T(8,128)} %param.12) | copy-start | bytes 147460
  6.1 79.7 %collective-permute-start.12 = (bf16[5120,128]{1,0:T(8,128)(2,1)}, bf16[5120,128]{1,0:T(8,128)(2,1)}, u32[]{:S(2)}, u32[]{:S(2)}) collective-permute-start(bf16[5120,128]{1,0:T(8,128)(2,1)} %get-tuple-element.15.refs_0_), channel_id=1, source_target_pairs={{0,4},{4,0},{8,12},{12,8},{16,20},{20,16},{24,28},{28,24},{1,5},{5... | collective-permute-start | bytes 3932168 | tf_op jit(solution)/shard_map/ppermute | solution.py:363
  7.6 43.9 %collective-permute-start = (bf16[5120,128]{1,0:T(8,128)(2,1)}, bf16[5120,128]{1,0:T(8,128)(2,1)S(1)}, u32[]{:S(2)}, u32[]{:S(2)}) collective-permute-start(bf16[5120,128]{1,0:T(8,128)(2,1)} %get-tuple-element.15.refs_0_), channel_id=1, source_target_pairs={{0,8},{8,16},{16,24},{1,9},{9,17},{17,25},{2,10},{10,18},{18,26},{... | collective-permute-start | bytes 3932168 | tf_op jit(solution)/shard_map/ppermute | solution.py:363
  11.1 44.8 %collective-permute-start.4 = (bf16[5120,128]{1,0:T(8,128)(2,1)}, bf16[5120,128]{1,0:T(8,128)(2,1)S(1)}, u32[]{:S(2)}, u32[]{:S(2)}) collective-permute-start(bf16[5120,128]{1,0:T(8,128)(2,1)} %get-tuple-element.15.refs_0_), channel_id=1, source_target_pairs={{8,0},{16,8},{24,16},{9,1},{17,9},{25,17},{10,2},{18,10},{26,18},{... | collective-permute-start | bytes 3932168 | tf_op jit(solution)/shard_map/ppermute | solution.py:363
  13.5 24.1 %collective-permute-start.14 = (bf16[32,384]{1,0:T(8,128)(2,1)}, bf16[32,384]{1,0:T(8,128)(2,1)S(1)}, u32[]{:S(2)}, u32[]{:S(2)}) collective-permute-start(bf16[32,384]{1,0:T(8,128)(2,1)} %get-tuple-element.24), channel_id=1, source_target_pairs={{0,4},{4,0},{1,5},{5,1},{2,6},{6,2},{3,7},{7,3},{8,12},{12,8},{9,1... | collective-permute-start | bytes 73736 | tf_op jit(solution)/shard_map/ppermute | solution.py:338
  14.1 45.2 %collective-permute-start.13 = (bf16[320,512]{1,0:T(8,128)(2,1)S(1)}, bf16[320,512]{1,0:T(8,128)(2,1)}, u32[]{:S(2)}, u32[]{:S(2)}) collective-permute-start(bf16[320,512]{1,0:T(8,128)(2,1)S(1)} %bitcast.48), channel_id=1, source_target_pairs={{0,4},{1,5},{2,6},{3,7},{8,12},{9,13},{10,14},{11,15},{16,20},{17,... | collective-permute-start | bytes 983048 | tf_op jit(solution)/shard_map/ppermute | solution.py:376
  21.5 16.1 %copy-start = (bf16[32,384]{1,0:T(8,128)(2,1)S(1)}, bf16[32,384]{1,0:T(8,128)(2,1)}, u32[]{:S(2)}) copy-start(bf16[32,384]{1,0:T(8,128)(2,1)} %get-tuple-element.24) | copy-start | bytes 73732
  37.6 7.6 %collective-permute-start.15 = (bf16[64,384]{1,0:T(8,128)(2,1)S(1)}, bf16[64,384]{1,0:T(8,128)(2,1)S(1)}, u32[]{:S(2)}, u32[]{:S(2)}) collective-permute-start(bf16[64,384]{1,0:T(8,128)(2,1)S(1)} %pad_maximum_fusion.2), channel_id=1, source_target_pairs={{0,8},{8,0},{16,24},{24,16},{1,9},{9,1},{17,25},{25,17},{2,10},{10... | collective-permute-start | bytes 147464 | tf_op jit(solution)/shard_map/ppermute | solution.py:338
  45.2 5.6 %collective-permute-start.16 = (bf16[128,384]{1,0:T(8,128)(2,1)S(1)}, bf16[128,384]{1,0:T(8,128)(2,1)S(1)}, u32[]{:S(2)}, u32[]{:S(2)}) collective-permute-start(bf16[128,384]{1,0:T(8,128)(2,1)S(1)} %pad_maximum_fusion.1), channel_id=1, source_target_pairs={{0,16},{8,24},{16,0},{24,8},{1,17},{9,25},{17,1},{25,9},{2,18},{10... | collective-permute-start | bytes 294920 | tf_op jit(solution)/shard_map/ppermute | solution.py:338
  51.5 25.7 %copy-start.2 = (bf16[5120,128]{1,0:T(8,128)(2,1)}, bf16[5120,128]{1,0:T(8,128)(2,1)S(1)}, u32[]{:S(2)}) copy-start(bf16[5120,128]{1,0:T(8,128)(2,1)S(1)} %collective-permute-done.refs_0_) | copy-start | bytes 3932164
  51.5 39.4 %collective-permute-start.10 = (bf16[5120,128]{1,0:T(8,128)(2,1)S(1)}, bf16[5120,128]{1,0:T(8,128)(2,1)}, u32[]{:S(2)}, u32[]{:S(2)}) collective-permute-start(bf16[5120,128]{1,0:T(8,128)(2,1)S(1)} %collective-permute-done.refs_0_), channel_id=1, source_target_pairs={{8,12},{12,8},{16,20},{20,16},{24,28},{28,24},{9,13},{13,9},{17,21... | collective-permute-start | bytes 3932168 | tf_op jit(solution)/shard_map/ppermute | solution.py:363
  53.7 28.8 %collective-permute-start.1 = (bf16[5120,128]{1,0:T(8,128)(2,1)S(1)}, bf16[5120,128]{1,0:T(8,128)(2,1)S(1)}, u32[]{:S(2)}, u32[]{:S(2)}) collective-permute-start(bf16[5120,128]{1,0:T(8,128)(2,1)S(1)} %collective-permute-done.refs_0_), channel_id=1, source_target_pairs={{8,16},{16,24},{9,17},{17,25},{10,18},{18,26},{11,19},{19,27},{12,... | collective-permute-start | bytes 3932168 | tf_op jit(solution)/shard_map/ppermute | solution.py:363
  55.9 21.3 %copy-start.3 = (bf16[5120,128]{1,0:T(8,128)(2,1)}, bf16[5120,128]{1,0:T(8,128)(2,1)S(1)}, u32[]{:S(2)}) copy-start(bf16[5120,128]{1,0:T(8,128)(2,1)S(1)} %collective-permute-done.4.refs_1_) | copy-start | bytes 3932164
  55.9 57.4 %collective-permute-start.11 = (bf16[5120,128]{1,0:T(8,128)(2,1)S(1)}, bf16[5120,128]{1,0:T(8,128)(2,1)}, u32[]{:S(2)}, u32[]{:S(2)}) collective-permute-start(bf16[5120,128]{1,0:T(8,128)(2,1)S(1)} %collective-permute-done.4.refs_1_), channel_id=1, source_target_pairs={{0,4},{4,0},{8,12},{12,8},{16,20},{20,16},{1,5},{5,1},{9,13},{13,9... | collective-permute-start | bytes 3932168 | tf_op jit(solution)/shard_map/ppermute | solution.py:363
  59.3 29.8 %collective-permute-start.5 = (bf16[5120,128]{1,0:T(8,128)(2,1)S(1)}, bf16[5120,128]{1,0:T(8,128)(2,1)S(1)}, u32[]{:S(2)}, u32[]{:S(2)}) collective-permute-start(bf16[5120,128]{1,0:T(8,128)(2,1)S(1)} %collective-permute-done.4.refs_1_), channel_id=1, source_target_pairs={{8,0},{16,8},{9,1},{17,9},{10,2},{18,10},{11,3},{19,11},{12,4},{20... | collective-permute-start | bytes 3932168 | tf_op jit(solution)/shard_map/ppermute | solution.py:363
  82.6 22.6 %copy-start.4 = (bf16[5120,128]{1,0:T(8,128)(2,1)}, bf16[5120,128]{1,0:T(8,128)(2,1)S(1)}, u32[]{:S(2)}) copy-start(bf16[5120,128]{1,0:T(8,128)(2,1)S(1)} %collective-permute-done.1.refs_0_) | copy-start | bytes 3932164
  82.6 53.9 %collective-permute-start.8 = (bf16[5120,128]{1,0:T(8,128)(2,1)S(1)}, bf16[5120,128]{1,0:T(8,128)(2,1)S(1)}, u32[]{:S(2)}, u32[]{:S(2)}) collective-permute-start(bf16[5120,128]{1,0:T(8,128)(2,1)S(1)} %collective-permute-done.1.refs_0_), channel_id=1, source_target_pairs={{16,20},{20,16},{24,28},{28,24},{17,21},{21,17},{25,29},{29,25},{1... | collective-permute-start | bytes 3932168 | tf_op jit(solution)/shard_map/ppermute | solution.py:363
  85.9 46.9 %collective-permute-start.2 = (bf16[5120,128]{1,0:T(8,128)(2,1)S(1)}, bf16[5120,128]{1,0:T(8,128)(2,1)}, u32[]{:S(2)}, u32[]{:S(2)}) collective-permute-start(bf16[5120,128]{1,0:T(8,128)(2,1)S(1)} %collective-permute-done.1.refs_0_), channel_id=1, source_target_pairs={{16,24},{17,25},{18,26},{19,27},{20,28},{21,29},{22,30},{23,31}} | collective-permute-start | bytes 3932168 | tf_op jit(solution)/shard_map/ppermute | solution.py:363
  89.1 16.1 %copy-start.5 = (bf16[5120,128]{1,0:T(8,128)(2,1)}, bf16[5120,128]{1,0:T(8,128)(2,1)S(1)}, u32[]{:S(2)}) copy-start(bf16[5120,128]{1,0:T(8,128)(2,1)S(1)} %collective-permute-done.5.refs_1_) | copy-start | bytes 3932164
  89.1 47.3 %collective-permute-start.9 = (bf16[5120,128]{1,0:T(8,128)(2,1)S(1)}, bf16[5120,128]{1,0:T(8,128)(2,1)}, u32[]{:S(2)}, u32[]{:S(2)}) collective-permute-start(bf16[5120,128]{1,0:T(8,128)(2,1)S(1)} %collective-permute-done.5.refs_1_), channel_id=1, source_target_pairs={{0,4},{4,0},{8,12},{12,8},{1,5},{5,1},{9,13},{13,9},{2,6},{6,2},{1... | collective-permute-start | bytes 3932168 | tf_op jit(solution)/shard_map/ppermute | solution.py:363
  90.9 43.6 %collective-permute-start.6 = (bf16[5120,128]{1,0:T(8,128)(2,1)S(1)}, bf16[5120,128]{1,0:T(8,128)(2,1)}, u32[]{:S(2)}, u32[]{:S(2)}) collective-permute-start(bf16[5120,128]{1,0:T(8,128)(2,1)S(1)} %collective-permute-done.5.refs_1_), channel_id=1, source_target_pairs={{8,0},{9,1},{10,2},{11,3},{12,4},{13,5},{14,6},{15,7}} | collective-permute-start | bytes 3932168 | tf_op jit(solution)/shard_map/ppermute | solution.py:363
  132.8 27.1 %collective-permute-start.3 = (bf16[5120,128]{1,0:T(8,128)(2,1)}, bf16[5120,128]{1,0:T(8,128)(2,1)}, u32[]{:S(2)}, u32[]{:S(2)}) collective-permute-start(bf16[5120,128]{1,0:T(8,128)(2,1)} %collective-permute-done.2.refs_0_), channel_id=1, source_target_pairs={{24,28},{28,24},{25,29},{29,25},{26,30},{30,26},{27,31},{31,27}} | collective-permute-start | bytes 3932168 | tf_op jit(solution)/shard_map/ppermute | solution.py:363
  134.5 25.4 %collective-permute-start.7 = (bf16[5120,128]{1,0:T(8,128)(2,1)}, bf16[5120,128]{1,0:T(8,128)(2,1)}, u32[]{:S(2)}, u32[]{:S(2)}) collective-permute-start(bf16[5120,128]{1,0:T(8,128)(2,1)} %collective-permute-done.6.refs_1_), channel_id=1, source_target_pairs={{0,4},{4,0},{1,5},{5,1},{2,6},{6,2},{3,7},{7,3}} | collective-permute-start | bytes 3932168 | tf_op jit(solution)/shard_map/ppermute | solution.py:363
  136.5 1.0 copy-start.6
  137.5 28.2 %slice-start = ((s8[5242880]{0:T(1024)(128)(4,1)}), s8[4194304]{0:T(1024)(128)(4,1)S(1)}, s32[]{:S(2)}) async-start(s8[5242880]{0:T(1024)(128)(4,1)} %bitcast.43), calls=%async_computation | async-start | bytes 8388608
  151.5 14.2 %slice-start.1 = ((s8[5242880]{0:T(1024)(128)(4,1)}), s8[1048576]{0:T(1024)(128)(4,1)S(1)}, s32[]{:S(2)}) async-start(s8[5242880]{0:T(1024)(128)(4,1)} %bitcast.43), calls=%async_computation.1 | async-start | bytes 2097152
  168.4 10.8 %collective-permute-start.18 = (bf16[128,2560]{1,0:T(8,128)(2,1)S(1)}, bf16[128,2560]{1,0:T(8,128)(2,1)S(1)}, u32[]{:S(2)}, u32[]{:S(2)}) collective-permute-start(bf16[128,2560]{1,0:T(8,128)(2,1)S(1)} %slice.34), channel_id=1, source_target_pairs={{0,1},{1,0},{2,3},{3,2},{4,5},{5,4},{6,7},{7,6},{8,9},{9,8},{10,11... | collective-permute-start | bytes 1966088 | tf_op jit(solution)/shard_map/ppermute | solution.py:338
  178.6 2.9 %collective-permute-start.17 = (bf16[128,2560]{1,0:T(8,128)(2,1)S(1)}, bf16[128,2560]{1,0:T(8,128)(2,1)S(1)}, u32[]{:S(2)}, u32[]{:S(2)}) collective-permute-start(bf16[128,2560]{1,0:T(8,128)(2,1)S(1)} %slice.35), channel_id=1, source_target_pairs={{0,1},{1,0},{2,3},{3,2},{4,5},{5,4},{6,7},{7,6},{8,9},{9,8},{10,11... | collective-permute-start | bytes 1966088 | tf_op jit(solution)/shard_map/ppermute | solution.py:338
  179.3 17.1 %collective-permute-start.19 = (bf16[128,2560]{1,0:T(8,128)(2,1)S(1)}, bf16[128,2560]{1,0:T(8,128)(2,1)S(1)}, u32[]{:S(2)}, u32[]{:S(2)}) collective-permute-start(bf16[128,2560]{1,0:T(8,128)(2,1)S(1)} %fusion), channel_id=1, source_target_pairs={{0,2},{1,3},{2,0},{3,1},{4,6},{5,7},{6,4},{7,5},{8,10},{9,11},{10,... | collective-permute-start | bytes 1966088 | tf_op jit(solution)/shard_map/ppermute | solution.py:338

commit v2 on v1

--- a/solution.py
+++ b/solution.py
@@ -17,10 +17,12 @@
 TAIL = DK - LANES
 EXT = 2 * LANES
 ROWS = BLK + BLK // 2 + BLK
-QUAD = 4
+UNIT = 4
+NOTES = 16
+PIECES = 2
 SCALE = DK ** (-0.5)
 LOW = -1e30
-VMEM = 56 * 1024 * 1024
+VMEM = 32 * 1024 * 1024
 BF = jnp.bfloat16
 F32 = jnp.float32
 
@@ -39,9 +41,9 @@
 
 def pack_kernel(kv_ref, pool_ref, packed_ref, comp_ref):
     tokens = kv_ref.shape[1]
-    pool = pool_ref[...]
-    pool_key = jnp.broadcast_to(pool[:, 0:1], (BLK, LANES))
-    pool_value = jnp.broadcast_to(pool[:, 1:2], (BLK, LANES))
+    pool_key, pool_value = (
+        jnp.broadcast_to(pool_ref[k : k + 1, :], (LANES, BLK)).T for k in range(2)
+    )
     half = BLK // 2
     pool_tail = jnp.where(lane_is_low((half, LANES)), pool_key[:half], pool_key[half:])
     rows = []
@@ -78,7 +80,7 @@
         compiler_params=params(),
         cost_estimate=cost(5),
         name="pack",
-    )(kv_t, pooling.T)
+    )(kv_t, pooling)
 
 
 def wide_queries_kernel(q_ref, out_ref):
@@ -185,30 +187,22 @@
     )(begin, wide, far_t, own_t, comp, gates)
 
 
-def selected_step(block, ids_ref, owner_ref, q_ref, kv_refs, state, list_ref, key_ref, value_ref):
-    top_k = ids_ref.shape[1]
-    held = kv_refs[0].shape[0] // ROWS
-    count = jnp.int32(0)
-    for slot in range(top_k):
-        index = ids_ref[block, slot]
-        owner = index // held
-        entry = jnp.int32(-1)
-        for place in range(len(kv_refs)):
-            entry = jnp.where(owner == owner_ref[place], place * held + index % held, entry)
-        list_ref[count] = entry
-        count = count + (entry >= 0).astype(jnp.int32)
+def add_selected(unit, list_ref, block, q_ref, kv_refs, top, total, acc_ref, key_ref, value_ref):
+    count = list_ref[block, list_ref.shape[1] - 1]
+    held = kv_refs[0].shape[0]
     half = BLK // 2
     low = lane_is_low((half, LANES))
 
-    def quad(step, state):
-        top, total, acc = state
-        for k in range(QUAD):
-            entry = list_ref[jnp.minimum(step * QUAD + k, count - 1)]
-            place, base = entry // held, pl.multiple_of((entry % held) * ROWS, 16)
-            for at, kv_ref in enumerate(kv_refs):
-
-                @pl.when(place == at)
-                def _():
+    def step(index, state):
+        top, total = state
+        for k in range(unit):
+            entry = list_ref[block, jnp.minimum(index * unit + k, count - 1)]
+            for place, kv_ref in enumerate(kv_refs):
+                inside = (entry >= place * held) & (entry < (place + 1) * held)
+
+                @pl.when(inside)
+                def _(kv_ref=kv_ref, place=place):
+                    base = pl.multiple_of(entry - place * held, 32)
                     to = k * BLK
                     key_ref[to : to + BLK, :LANES] = kv_ref[pl.ds(base, BLK), :]
                     end = kv_ref[pl.ds(base + BLK, half), :]
@@ -217,151 +211,242 @@
                     key_ref[to + half : to + BLK, LANES:] = jnp.where(low, zero, end)
                     value_ref[to : to + BLK, :] = kv_ref[pl.ds(base + BLK + half, BLK), :]
 
-        scores = scores_of(key_ref[...], q_ref[0])
+        keys = unit * BLK
+        scores = scores_of(key_ref[:keys], q_ref[0])
         row = lax.broadcasted_iota(jnp.int32, scores.shape, 0)
-        scores = jnp.where(row < (count - step * QUAD) * BLK, scores, LOW)
+        scores = jnp.where(row < (count - index * unit) * BLK, scores, LOW)
         new_top = jnp.maximum(top, jnp.max(scores, axis=0, keepdims=True))
         weights = jnp.exp((scores - new_top) * SCALE)
         keep = jnp.exp((top - new_top) * SCALE)
         total = total * keep + jnp.sum(weights, axis=0, keepdims=True)
-        acc = acc * keep + lax.dot_general(
-            value_ref[...], weights.astype(BF), (((0,), (0,)), ((), ())), preferred_element_type=F32
+        acc_ref[...] = acc_ref[...] * keep + lax.dot_general(
+            value_ref[:keys],
+            weights.astype(BF),
+            (((0,), (0,)), ((), ())),
+            preferred_element_type=F32,
         )
-        return new_top, total, acc
-
-    return lax.fori_loop(0, (count + QUAD - 1) // QUAD, quad, state)
-
-
-def stage_kernel(first, n_kv, ids_ref, owner_ref, q_ref, *refs):
+        return new_top, total
+
+    return lax.fori_loop(0, (count + unit - 1) // unit, step, (top, total))
+
+
+def scratch(unit):
+    return [pltpu.VMEM((unit * BLK, EXT), BF), pltpu.VMEM((unit * BLK, DV), BF)]
+
+
+def whole_spec(array):
+    return pl.BlockSpec(array.shape, lambda i, *_: (0,) * array.ndim)
+
+
+def stage_kernel(first, n_kv, unit, list_ref, q_ref, *refs):
     kv_refs, refs = refs[:n_kv], refs[n_kv:]
+    lanes = q_ref.shape[1]
     if first:
-        state_out, acc_out, list_ref, key_ref, value_ref = refs
-        lanes = q_ref.shape[1]
-        state = (
-            jnp.full((1, lanes), LOW, F32),
-            jnp.zeros((1, lanes), F32),
-            jnp.zeros((DV, lanes), F32),
-        )
+        state_out, acc_out, key_ref, value_ref = refs
+        top = jnp.full((1, lanes), LOW, F32)
+        total = jnp.zeros((1, lanes), F32)
+        acc_out[...] = jnp.zeros_like(acc_out)
     else:
-        state_in, acc_in, state_out, acc_out, list_ref, key_ref, value_ref = refs
-        state = (state_in[0, 0:1], state_in[0, 1:2], acc_in[0])
-    top, total, acc = selected_step(
-        pl.program_id(0), ids_ref, owner_ref, q_ref, kv_refs, state, list_ref, key_ref, value_ref
+        state_in, acc_in, state_out, acc_out, key_ref, value_ref = refs
+        top, total = state_in[0, 0:1], state_in[0, 1:2]
+        acc_out[...] = acc_in[...]
+    top, total = add_selected(
+        unit, list_ref, pl.program_id(0), q_ref, kv_refs, top, total, acc_out.at[0], key_ref, value_ref
     )
     state_out[0, 0:1] = top
     state_out[0, 1:2] = total
-    acc_out[0] = acc
-
-
-def scratch():
-    return [
-        pltpu.SMEM((64,), jnp.int32),
-        pltpu.VMEM((QUAD * BLK, EXT), BF),
-        pltpu.VMEM((QUAD * BLK, DV), BF),
-    ]
-
-
-def stage(ids, owners, wide, kvs, state):
+
+
+def stage(unit, lists, wide, kvs, state):
     steps, lanes, _ = wide.shape
     row = pl.BlockSpec((1, 2, lanes), lambda i, *_: (i, 0, 0))
     wide_row = pl.BlockSpec((1, DV, lanes), lambda i, *_: (i, 0, 0))
     in_specs = [pl.BlockSpec((1, lanes, EXT), lambda i, *_: (i, 0, 0))]
-    in_specs += [pl.BlockSpec(kv.shape, lambda i, *_: (0, 0)) for kv in kvs]
+    in_specs += [whole_spec(kv) for kv in kvs]
     first = state is None
     aliases = {}
     if not first:
         in_specs += [row, wide_row]
-        aliases = {3 + len(kvs): 0, 4 + len(kvs): 1}
+        aliases = {2 + len(kvs): 0, 3 + len(kvs): 1}
     return pl.pallas_call(
-        functools.partial(stage_kernel, first, len(kvs)),
+        functools.partial(stage_kernel, first, len(kvs), unit),
+        grid_spec=pltpu.PrefetchScalarGridSpec(
+            num_scalar_prefetch=1,
+            grid=(steps,),
+            in_specs=in_specs,
+            out_specs=[row, wide_row],
+            scratch_shapes=scratch(unit),
+        ),
+        out_shape=(
+            jax.ShapeDtypeStruct((steps, 2, lanes), F32),
+            jax.ShapeDtypeStruct((steps, DV, lanes), F32),
+        ),
+        input_output_aliases=aliases,
+        compiler_params=params(),
+        cost_estimate=cost(9),
+        name="stage",
+    )(lists, wide, *kvs, *(() if first else state))
+
+
+def log_total(top, total):
+    return jnp.where(total > 0, top * SCALE + jnp.log(jnp.maximum(total, 1e-30)), LOW)
+
+
+def part_kernel(n_kv, unit, order_ref, list_ref, q_ref, *refs):
+    kv_refs, refs = refs[:n_kv], refs[n_kv:]
+    state_in, acc_in, out_ref, acc_ref, key_ref, value_ref = refs
+    acc_ref[...] = acc_in[0]
+    top, total = add_selected(
+        unit,
+        list_ref,
+        order_ref[pl.program_id(0)],
+        q_ref,
+        kv_refs,
+        state_in[0, 0:1],
+        state_in[0, 1:2],
+        acc_ref,
+        key_ref,
+        value_ref,
+    )
+    out_ref[0, :DV] = (acc_ref[...] / jnp.maximum(total, 1e-30)).astype(BF)
+    rest = log_total(top, total)
+    terms = []
+    for _ in range(3):
+        terms.append(rest.astype(BF).astype(F32))
+        rest = rest - terms[-1]
+    terms.append(jnp.zeros((NOTES - len(terms), rest.shape[1]), F32))
+    out_ref[0, DV:] = jnp.concatenate(terms, axis=0).astype(BF)
+
+
+def part_stage(unit, order, lists, wide, kvs, state):
+    _, lanes, _ = wide.shape
+    (steps,) = order.shape
+    at = lambda i, order, *_: (order[i], 0, 0)
+    return pl.pallas_call(
+        functools.partial(part_kernel, len(kvs), unit),
         grid_spec=pltpu.PrefetchScalarGridSpec(
             num_scalar_prefetch=2,
             grid=(steps,),
-            in_specs=in_specs,
-            out_specs=[row, wide_row],
-            scratch_shapes=scratch(),
-        ),
-        out_shape=(
-            jax.ShapeDtypeStruct((steps, 2, lanes), F32),
-            jax.ShapeDtypeStruct((steps, DV, lanes), F32),
-        ),
-        input_output_aliases=aliases,
+            in_specs=[pl.BlockSpec((1, lanes, EXT), at)]
+            + [whole_spec(kv) for kv in kvs]
+            + [pl.BlockSpec((1, 2, lanes), at), pl.BlockSpec((1, DV, lanes), at)],
+            out_specs=pl.BlockSpec((1, DV + NOTES, lanes), lambda i, *_: (i, 0, 0)),
+            scratch_shapes=[pltpu.VMEM((DV, lanes), F32)] + scratch(unit),
+        ),
+        out_shape=jax.ShapeDtypeStruct((steps, DV + NOTES, lanes), BF),
         compiler_params=params(),
-        cost_estimate=cost(12),
-        name="stage",
-    )(ids, owners, wide, *kvs, *(() if first else state))
-
-
-def last_kernel(n_kv, order_ref, ids_ref, owner_ref, q_ref, *refs):
+        cost_estimate=cost(4),
+        name="part_stage",
+    )(order, lists, wide, *kvs, *state)
+
+
+def last_kernel(n_kv, unit, order_ref, list_ref, q_ref, *refs):
     kv_refs, refs = refs[:n_kv], refs[n_kv:]
-    state_in, acc_in, near_ref, gate_ref, out_ref, list_ref, key_ref, value_ref = refs
-    state = (state_in[0, 0:1], state_in[0, 1:2], acc_in[0])
-    block = order_ref[pl.program_id(0)]
-    _, total, acc = selected_step(
-        block, ids_ref, owner_ref, q_ref, kv_refs, state, list_ref, key_ref, value_ref
-    )
-    out = near_ref[0] + acc * (gate_ref[0, 1:2] / total)
+    state_in, acc_in, near_ref, gate_ref = refs[:4]
+    part_refs, (out_ref, acc_ref, key_ref, value_ref) = refs[4:-4], refs[-4:]
+    acc_ref[...] = acc_in[0]
+    top, total = add_selected(
+        unit,
+        list_ref,
+        order_ref[pl.program_id(0)],
+        q_ref,
+        kv_refs,
+        state_in[0, 0:1],
+        state_in[0, 1:2],
+        acc_ref,
+        key_ref,
+        value_ref,
+    )
+    logs = [log_total(top, total)]
+    for part_ref in part_refs:
+        notes = part_ref[0, DV:].astype(F32)
+        logs.append(notes[0:1] + notes[1:2] + notes[2:3])
+    peak = functools.reduce(jnp.maximum, logs)
+    shares = [jnp.exp(log - peak) for log in logs]
+    gate = gate_ref[0, 1:2] / functools.reduce(jnp.add, shares)
+    out = near_ref[0] + acc_ref[...] * (gate * shares[0] / jnp.maximum(total, 1e-30))
+    for share, part_ref in zip(shares[1:], part_refs):
+        out = out + part_ref[0, :DV].astype(F32) * (gate * share)
     for head in range(0, HQ, 2):
         pair = out[:, head * BLK : (head + 2) * BLK].T.astype(BF)
         out_ref[:, head * DV : (head + 1) * DV] = pair[:BLK]
         out_ref[:, (head + 1) * DV : (head + 2) * DV] = pair[BLK:]
 
 
-def last_stage(order, ids, owners, wide, kvs, state, near, gates):
+def last_stage(unit, order, lists, wide, kvs, state, near, gates, others):
     _, lanes, _ = wide.shape
     (steps,) = order.shape
     at = lambda i, order, *_: (order[i], 0, 0)
     return pl.pallas_call(
-        functools.partial(last_kernel, len(kvs)),
+        functools.partial(last_kernel, len(kvs), unit),
         grid_spec=pltpu.PrefetchScalarGridSpec(
-            num_scalar_prefetch=3,
+            num_scalar_prefetch=2,
             grid=(steps,),
             in_specs=[pl.BlockSpec((1, lanes, EXT), at)]
-            + [pl.BlockSpec(kv.shape, lambda i, *_: (0, 0)) for kv in kvs]
+            + [whole_spec(kv) for kv in kvs]
             + [
                 pl.BlockSpec((1, 2, lanes), at),
                 pl.BlockSpec((1, DV, lanes), at),
                 pl.BlockSpec((1, DV, lanes), at),
                 pl.BlockSpec((1, 3, lanes), at),
-            ],
+            ]
+            + [pl.BlockSpec((1, DV + NOTES, lanes), lambda i, *_: (i, 0, 0)) for _ in others],
             out_specs=pl.BlockSpec((BLK, HQ * DV), lambda i, *_: (i, 0)),
-            scratch_shapes=scratch(),
+            scratch_shapes=[pltpu.VMEM((DV, lanes), F32)] + scratch(unit),
         ),
         out_shape=jax.ShapeDtypeStruct((steps * BLK, HQ * DV), BF),
         compiler_params=params(),
-        cost_estimate=cost(8),
+        cost_estimate=cost(5),
         name="last_stage",
-    )(order, ids, owners, wide, *kvs, *state, near, gates)
+    )(order, lists, wide, *kvs, *state, near, gates, *others)
+
+
+def held_lists(ids, owners, held):
+    top_k = ids.shape[-1]
+    owner = ids // held
+    entry = (ids % held) * ROWS
+    match = jnp.zeros(ids.shape, jnp.bool_)
+    for place, one in enumerate(owners):
+        here = owner == one
+        match = match | here
+        entry = entry + jnp.where(here, place * held * ROWS, 0)
+    slot = jnp.arange(top_k, dtype=jnp.int32)
+    before = (slot[:, None] < slot[None, :]) & match[..., :, None]
+    rank = jnp.sum(before.astype(jnp.int32), axis=-2)
+    rank = jnp.where(match, rank, -1)
+    front = jnp.sum(jnp.where(rank[..., :, None] == slot, entry[..., :, None], 0), axis=-2)
+    count = jnp.sum(match.astype(jnp.int32), axis=-1, keepdims=True)
+    return jnp.concatenate([front, count], axis=-1).astype(jnp.int32)
 
 
 def swap(value, axis, bit):
     return lax.ppermute(value, axis, [(i, i ^ bit) for i in range(lax.axis_size(axis))])
 
 
-def spread(value, axis, wraps, sib_shift):
-    sib_count, count = lax.axis_size("sib"), lax.axis_size(axis)
-    ring = wraps or count == 2
-    reach = [count // 2, (count - 1) // 2] if ring else [count - 1, count - 1]
+def shift(value, axis, steps):
+    count = lax.axis_size(axis)
+    return lax.ppermute(value, axis, [(i, (i + steps) % count) for i in range(count)])
+
+
+def spread(value, axis, wraps):
+    count = lax.axis_size(axis)
+    reach = [count // 2, (count - 1) // 2] if wraps else [count - 1, count - 1]
     held = [value, value]
     found = []
     for hop in range(1, max(reach) + 1):
+        found.append([])
         for side, sign in enumerate((1, -1)):
             if hop > reach[side]:
                 continue
             pairs = []
             for source in range(count):
                 target = source + sign
-                if ring:
+                if wraps:
                     pairs.append((source, target % count))
                 elif 0 <= target < count and 0 <= target - sign * hop < count:
                     pairs.append((source, target))
-            axes = axis
-            if axis == "ctx":
-                axes = ("sib", "ctx")
-                holders = [s for s in range(sib_count) if wraps or 0 <= s + sib_shift < sib_count]
-                pairs = [(s * count + a, s * count + b) for s in holders for a, b in pairs]
-            held[side] = lax.ppermute(held[side], axes, pairs)
-            found.append((held[side], hop, -sign * hop))
+            held[side] = lax.ppermute(held[side], axis, pairs)
+            found[-1].append((held[side], -sign * hop))
     return found
 
 
@@ -370,57 +455,51 @@
     sib_count, ctx_count, head_count = (lax.axis_size(a) for a in ("sib", "ctx", "head"))
     blocks = rows // BLK
     sib, ctx, head = (lax.axis_index(a) for a in ("sib", "ctx", "head"))
+    held_blocks = prefix_kv.shape[0] // BLK
+
+    flat = queries.reshape(rows, HQ * DK)
+    ids = selected.reshape(blocks, -1)
     packed, comp = pack(prefix_kv[:, 0, :].T, pooling)
-
-    own_t = suffix_kv[0, :, 0, :].T
+    run_ids = [ids] + [shift(ids, "ctx", -d) for d in range(1, ctx_count)]
+    bit = 1
+    while bit < ctx_count:
+        comp = jnp.concatenate([comp, swap(comp, "ctx", bit)], axis=0)
+        bit *= 2
+    flat, own_t, _ = lax.optimization_barrier((flat, suffix_kv[0, :, 0, :].T, comp))
+    flats = [flat] + [shift(flat, "ctx", -d) for d in range(1, ctx_count)]
     far_t = lax.ppermute(own_t, "ctx", [(i, i + 1) for i in range(ctx_count - 1)])
-    for axis, count in (("ctx", ctx_count), ("sib", sib_count)):
-        bit = 1
-        while bit < count:
-            comp = jnp.concatenate([comp, swap(comp, axis, bit)], axis=0)
-            bit *= 2
-
-    def owner_of(sib_shift, ctx_shift):
-        s, c = sib + sib_shift, ctx + ctx_shift
+
+    hops = [[(packed, 0)]] + spread(packed, "sib", wraps)
+    for number, bit in enumerate(1 << k for k in range((sib_count - 1).bit_length())):
+        got = swap(comp, "sib", bit)
+        behind = [a for a, _ in hops[min(number + 1, len(hops) - 1)]]
+        comp, got = lax.optimization_barrier((comp, got, behind))[:2]
+        comp = jnp.concatenate([comp, got], axis=0)
+
+    def owner_of(steps):
+        other = sib + steps
         if wraps:
-            s = s % sib_count
-        if wraps or ctx_count == 2:
-            c = c % ctx_count
-        good = (s >= 0) & (s < sib_count) & (c >= 0) & (c < ctx_count)
-        return jnp.where(good, s * ctx_count + c, -2)
-
-    levels = {0: [(packed, 0)]}
-    for array, hop, shift in spread(packed, "sib", wraps, 0):
-        levels.setdefault(hop, []).append((array, shift))
-    stages = []
-    for hop, arrivals in levels.items():
-        near_by, far_off = [], []
-        for array, shift in arrivals:
-            near_by.append((array, owner_of(shift, 0)))
-            for other, _, ctx_shift in spread(array, "ctx", wraps, shift):
-                far_off.append((other, owner_of(shift, ctx_shift)))
-        stages.append((near_by, far_off))
-
-    wide = wide_queries(queries.reshape(rows, HQ * DK))
+            other = other % sib_count
+        good = (other >= 0) & (other < sib_count)
+        return jnp.where(good, other * ctx_count + ctx, -2)
+
+    levels = [hops[0] + hops[1]] + hops[2:]
+    lists = [held_lists(jnp.stack(run_ids), [owner_of(t) for _, t in level], held_blocks) for level in levels]
+
     begin = (ctx * rows).astype(jnp.int32)
     gates = jax.nn.sigmoid(gate_logits.reshape(rows, 3, HQ))
     alive = begin + jnp.arange(rows, dtype=jnp.int32) < lengths[0]
     gates = jnp.where(alive[:, None, None], gates, 0.0)
     gates = gates.reshape(blocks, BLK, 3, HQ).transpose(0, 2, 3, 1).reshape(blocks, 3, HQ * BLK)
-    near = near_parts(begin.reshape(1), wide, far_t, own_t, comp, gates)
-
-    ids = selected.reshape(blocks, -1)
-    work = []
-    for near_by, far_off in stages[:-1]:
-        work.append(near_by + far_off)
-    work.append(stages[-1][0])
-    state = None
-    for items in work:
-        owners = jnp.stack([o for _, o in items]).astype(jnp.int32)
-        state = stage(ids, owners, wide, [a for a, _ in items], state)
-    items = stages[-1][1]
-    owners = jnp.stack([o for _, o in items]).astype(jnp.int32)
-    kvs = [a for a, _ in items]
+
+    wides = [wide_queries(f) for f in flats]
+    near = near_parts(begin.reshape(1), wides[0], far_t, own_t, comp, gates)
+    states = [None] * ctx_count
+    for level, table in zip(levels[:-1], lists[:-1]):
+        for run in range(ctx_count):
+            states[run] = stage(UNIT, table[run], wides[run], [a for a, _ in level], states[run])
+    table = lax.optimization_barrier((lists[-1], near, states))[0]
+    kvs = [a for a, _ in levels[-1]]
 
     half = head_count // 2
     chunk = rows // head_count
@@ -431,15 +510,29 @@
         starts = [(which * half + (low ^ k)) * per for k in range(half - 1, -1, -1)]
         return jnp.concatenate([s + jnp.arange(per, dtype=jnp.int32) for s in starts])
 
+    orders = [half_order(1 - high), half_order(high)]
+    parts = [
+        [part_stage(UNIT, order, table[run], wides[run], kvs, states[run]) for run in range(1, ctx_count)]
+        for order in orders
+    ]
+    others = [[shift(p, "ctx", d + 1) for d, p in enumerate(ps)] for ps in parts]
+    orders[0] = lax.optimization_barrier((orders[0], parts[1]))[0]
+
     def half_sum(which):
-        out = last_stage(half_order(which), ids, owners, wide, kvs, state, near, gates)
+        out = last_stage(
+            UNIT, orders[which], table[0], wides[0], kvs, states[0], near, gates, others[which]
+        )
         share = jnp.dot(out, w_out, preferred_element_type=F32)
-        other = swap(share[:chunk].astype(BF), "head", 1)
+        size = chunk // PIECES
+        pieces = [share[k * size : (k + 1) * size].astype(BF) for k in range(PIECES)]
+        other = jnp.concatenate([swap(piece, "head", 1) for piece in pieces], axis=0)
         return share[chunk:] + other.astype(F32)
 
-    away = half_sum(1 - high)
-    back = swap(away.astype(BF), "head", half)
-    mine = half_sum(high)
+    away = half_sum(0)
+    away = away.astype(BF)
+    back = swap(away, "head", half)
+    orders[1] = lax.optimization_barrier((orders[1], away))[0]
+    mine = half_sum(1)
     return (mine + back.astype(F32)).astype(BF).reshape(1, chunk, DM)
 
 

time: 199 us -> 155 us (0.78)
  the two profiles are of different devices: /device:TPU:16 before, /device:TPU:0 now
where the time goes in v2:
time: 155 us
  waiting for transfers between devices  60.6 us (39%)
  Pallas kernels  58.9 us (38%)
  starting transfers between devices  25.7 us (17%)
  matrix products  3.09 us (2%)
  local copies, waits for them, and re-layouts  2.6 us (2%)
  other arithmetic  2.52 us (2%)
    pallas_call x4, Pallas kernels, stage(): pl.pallas_call(functools.partial(stage_kernel, first, len(kvs), unit), gr...  28.9 us
    ppermute x4, waiting for transfers between devices, shift(): lax.ppermute(value, axis, [(i, (i + steps) % count) for i in range(count)])  22.3 us
    ppermute x8, waiting for transfers between devices, swap(): lax.ppermute(value, axis, [(i, i ^ bit) for i in range(lax.axis_size(axis...  21.4 us
    ppermute x6, waiting for transfers between devices, spread(): held[side] = lax.ppermute(held[side], axis, pairs)  16.8 us
    pallas_call x1, Pallas kernels, near_parts(): pl.pallas_call(near_kernel, grid_spec=pltpu.PrefetchScalarGridSpec(num_sc...  11.7 us
    ppermute x6, starting transfers between devices, spread(): held[side] = lax.ppermute(held[side], axis, pairs)  11.5 us
    pallas_call x2, Pallas kernels, last_stage(): pl.pallas_call(functools.partial(last_kernel, len(kvs), unit), grid_spec=...  7.26 us
    ppermute x8, starting transfers between devices, swap(): lax.ppermute(value, axis, [(i, i ^ bit) for i in range(lax.axis_size(axis...  6.4 us
  transfers between devices with their start and end apart: 19, of which 10 were waited for; matrix products, arithmetic and copies ran while one was open for 2% of the time, Pallas kernels for 31%

profile of v2, /device:TPU:0, one launch (start us, length us, event | category | flops | bytes accessed | tf_op | source)
XLA Modules:
  0.0 154.5 jit_solution(9148681074451353205)
XLA Ops:
  0.0 1.3 copy-done.1
  1.3 0.7 copy-done.3
  2.0 3.3 %pack.1 = (bf16[5120,128]{1,0:T(8,128)(2,1)}, bf16[32,384]{1,0:T(8,128)(2,1)S(1)}) custom-call(bf16[320,2048]{1,0:T(8,128)(2,1)S(1)} %bitcast.46, f32[2,64]{1,0:T(2,128)S(1)} %copy-done.3), custom_call_target="tpu_custom_call" | custom-call | flops 5000000000 | tf_op jit(solution)/shard_map/pack/pallas_call | solution.py:74
  5.3 6.0 %collective-permute-start.4 = (bf16[5120,128]{1,0:T(8,128)(2,1)}, bf16[5120,128]{1,0:T(8,128)(2,1)}, u32[]{:S(2)}, u32[]{:S(2)}) collective-permute-start(bf16[5120,128]{1,0:T(8,128)(2,1)} %get-tuple-element.27.refs_0_), channel_id=1, source_target_pairs={{0,8},{8,16},{16,24},{1,9},{9,17},{17,25},{2,10},{10,18},{18,26},{... | collective-permute-start | bytes 3932168 | tf_op jit(solution)/shard_map/ppermute | solution.py:448
  11.3 1.3 collective-permute-start.5
  12.6 1.6 %collective-permute-start = (s32[8,16]{1,0:T(8,128)S(1)}, s32[8,16]{1,0:T(8,128)S(1)}, u32[]{:S(2)}, u32[]{:S(2)}) collective-permute-start(s32[8,16]{1,0:T(8,128)S(1)} %bitcast.51), channel_id=1, source_target_pairs={{0,4},{4,0},{1,5},{5,1},{2,6},{6,2},{3,7},{7,3},{8,12},{12,8},{9,1... | collective-permute-start | bytes 1544 | tf_op jit(solution)/shard_map/ppermute | solution.py:428
  14.2 0.5 collective-permute-start.1
  15.5 0.1 div.39
  15.6 0.1 reshape.525
  15.8 0.1 pad_add_fusion.5.order_ref
  15.8 0.5 collective-permute-done
  16.3 0.1 convert_reduce_fusion.3
  16.5 0.2 select_add_fusion
  16.7 0.2 convert_reduce_fusion
  16.9 0.1 copy.28
  17.0 0.1 copy.27
  17.1 0.1 copy.24
  17.1 0.2 select_reduce_fusion
  17.4 0.1 fusion.11
  17.4 0.1 fusion.12
  17.5 0.1 select_reduce_fusion.2
  17.7 0.1 pad_add_fusion.1
  17.7 0.3 collective-permute-done.1
  18.0 2.6 %collective-permute-start.3 = (bf16[64,384]{1,0:T(8,128)(2,1)S(1)}, bf16[64,384]{1,0:T(8,128)(2,1)S(1)}, u32[]{:S(2)}, u32[]{:S(2)}) collective-permute-start(bf16[64,384]{1,0:T(8,128)(2,1)S(1)} %constant_dynamic-update-slice_fusion), channel_id=1, source_target_pairs={{0,8},{8,0},{16,24},{24,16},{1,9},{9,1},{17,25},{25,17},{2,10},{10... | collective-permute-start | bytes 147464 | tf_op jit(solution)/shard_map/ppermute | solution.py:423
  20.7 1.3 collective-permute-start.9
  21.9 1.0 wide_queries.2.q_ref
  22.9 2.7 %collective-permute-start.2 = (bf16[320,512]{1,0:T(8,128)(2,1)S(1)}, bf16[320,512]{1,0:T(8,128)(2,1)S(1)}, u32[]{:S(2)}, u32[]{:S(2)}) collective-permute-start(bf16[320,512]{1,0:T(8,128)(2,1)S(1)} %bitcast.47), channel_id=1, source_target_pairs={{0,4},{1,5},{2,6},{3,7},{8,12},{9,13},{10,14},{11,15},{16,20},{17,... | collective-permute-start | bytes 983048 | tf_op jit(solution)/shard_map/ppermute | solution.py:470
  25.6 19.1 %collective-permute-done.3 = bf16[64,384]{1,0:T(8,128)(2,1)S(1)} collective-permute-done((bf16[64,384]{1,0:T(8,128)(2,1)S(1)}, bf16[64,384]{1,0:T(8,128)(2,1)S(1)}, u32[]{:S(2)}, u32[]{:S(2)}) %collective-permute-start.3) | collective-permute-done | bytes 49184 | tf_op jit(solution)/shard_map/ppermute | solution.py:423
  44.7 0.0 collective-permute-done.5.refs_2_
  44.7 1.6 %collective-permute-start.6 = (bf16[128,384]{1,0:T(8,128)(2,1)S(1)}, bf16[128,384]{1,0:T(8,128)(2,1)S(1)}, u32[]{:S(2)}, u32[]{:S(2)}) collective-permute-start(bf16[128,384]{1,0:T(8,128)(2,1)S(1)} %constant_dynamic-update-slice_fusion.2), channel_id=1, source_target_pairs={{0,16},{8,24},{16,0},{24,8},{1,17},{9,25},{17,1},{25,9},{2,18},{10... | collective-permute-start | bytes 294920 | tf_op jit(solution)/shard_map/ppermute | solution.py:423
  46.4 0.7 collective-permute-start.7
  47.1 1.3 collective-permute-start.8
  48.4 10.0 %stage.4 = (f32[8,2,512]{2,1,0:T(2,128)S(1)}, f32[8,128,512]{2,1,0:T(8,128)S(1)}) custom-call(s32[8,17]{1,0:T(8,128)S(1)} %get-tuple-element.58.list_ref, bf16[8,512,256]{2,1,0:T(8,128)(2,1)S(1)} %wide_queries.2.q_ref, bf16[5120,128]{1,0:T(8,128)(2,1)} %get-tuple-element.27.refs_0_, bf16[5120,128]{1,0:T(8,128)(2,1)} %collective-permute-done.4.refs_1_, ...), custom_call_target="tpu_custom_call" | custom-call | flops 8999999488 | tf_op jit(solution)/shard_map/stage/pallas_call | solution.py:271
  58.4 1.0 wide_queries.3.q_ref
  59.4 9.3 %stage.6 = (f32[8,2,512]{2,1,0:T(2,128)S(1)}, f32[8,128,512]{2,1,0:T(8,128)S(1)}) custom-call(s32[8,17]{1,0:T(8,128)S(1)} %get-tuple-element.57.list_ref, bf16[8,512,256]{2,1,0:T(8,128)(2,1)S(1)} %wide_queries.3.q_ref, bf16[5120,128]{1,0:T(8,128)(2,1)} %get-tuple-element.27.refs_0_, bf16[5120,128]{1,0:T(8,128)(2,1)} %collective-permute-done.4.refs_1_, ...), custom_call_target="tpu_custom_call" | custom-call | flops 8999999488 | tf_op jit(solution)/shard_map/stage/pallas_call | solution.py:271
  68.7 0.7 collective-permute-start.10
  69.4 9.8 %collective-permute-done.8.refs_1_ = bf16[5120,128]{1,0:T(8,128)(2,1)S(1)} collective-permute-done((bf16[5120,128]{1,0:T(8,128)(2,1)S(1)}, bf16[5120,128]{1,0:T(8,128)(2,1)S(1)}, u32[]{:S(2)}, u32[]{:S(2)}) %collective-permute-start.8) | collective-permute-done | bytes 1310752 | tf_op jit(solution)/shard_map/ppermute | solution.py:448
  79.2 1.5 collective-permute-start.11
  80.7 4.2 %stage.7 = (f32[8,2,512]{2,1,0:T(2,128)S(1)}, f32[8,128,512]{2,1,0:T(8,128)S(1)}) custom-call(s32[8,17]{1,0:T(8,128)S(1)} %get-tuple-element.59.list_ref, bf16[8,512,256]{2,1,0:T(8,128)(2,1)S(1)} %wide_queries.3.q_ref, bf16[5120,128]{1,0:T(8,128)(2,1)S(1)} %collective-permute-done.7.refs_0_, ...), custom_call_target="tpu_custom_call", output_to_operand_aliasing={{0}: (4, {}), {1}: (5, {})} | custom-call | flops 8999999488 | tf_op jit(solution)/shard_map/stage/pallas_call | solution.py:271
  84.9 5.5 %stage.5 = (f32[8,2,512]{2,1,0:T(2,128)S(1)}, f32[8,128,512]{2,1,0:T(8,128)S(1)}) custom-call(s32[8,17]{1,0:T(8,128)S(1)} %get-tuple-element.60.list_ref, bf16[8,512,256]{2,1,0:T(8,128)(2,1)S(1)} %wide_queries.2.q_ref, bf16[5120,128]{1,0:T(8,128)(2,1)S(1)} %collective-permute-done.7.refs_0_, ...), custom_call_target="tpu_custom_call", output_to_operand_aliasing={{0}: (4, {}), {1}: (5, {})} | custom-call | flops 8999999488 | tf_op jit(solution)/shard_map/stage/pallas_call | solution.py:271
  90.4 11.7 %near.1.refs_4_ = f32[8,128,512]{2,1,0:T(8,128)S(1)} custom-call(s32[1]{0:T(128)} %bitcast.4.begin_ref, bf16[8,512,256]{2,1,0:T(8,128)(2,1)S(1)} %wide_queries.2.q_ref, bf16[320,512]{1,0:T(8,128)(2,1)S(1)} %collective-permute-done.2.far_ref, bf16[320,512]{1,0:T(8,128)(2,1)S(1)} %bitcast.48, bf16[256,384]{1,0:T(8,128)(2,1)S(1)} %pad_maximum_fusion.comp_ref, ...), custom_call_target="tpu_custom_call" | custom-call | flops 14000000000 | tf_op jit(solution)/shard_map/near/pallas_call | solution.py:168
  102.2 7.1 %collective-permute-done.11.refs_1_ = bf16[5120,128]{1,0:T(8,128)(2,1)S(1)} collective-permute-done((bf16[5120,128]{1,0:T(8,128)(2,1)S(1)}, bf16[5120,128]{1,0:T(8,128)(2,1)S(1)}, u32[]{:S(2)}, u32[]{:S(2)}) %collective-permute-start.11) | collective-permute-done | bytes 1310752 | tf_op jit(solution)/shard_map/ppermute | solution.py:448
  109.2 3.5 %part_stage.3 = bf16[4,144,512]{2,1,0:T(8,128)(2,1)S(1)} custom-call(s32[4]{0:T(128)S(1)} %pad_add_fusion.5.order_ref, s32[8,17]{1,0:T(8,128)S(1)} %get-tuple-element.65.list_ref, bf16[8,512,256]{2,1,0:T(8,128)(2,1)S(1)} %wide_queries.3.q_ref, bf16[5120,128]{1,0:T(8,128)(2,1)S(1)} %collective-permute-done.10.refs_0_, ...), custom_call_target="tpu_custom_call" | custom-call | flops 4000000000 | tf_op jit(solution)/shard_map/part_stage/pallas_call | solution.py:325
  112.7 1.2 collective-permute-start.12
  114.0 0.1 pad_add_fusion.4.order_ref
  114.0 2.2 %part_stage.2 = bf16[4,144,512]{2,1,0:T(8,128)(2,1)S(1)} custom-call(s32[4]{0:T(128)S(1)} %pad_add_fusion.4.order_ref, s32[8,17]{1,0:T(8,128)S(1)} %get-tuple-element.65.list_ref, bf16[8,512,256]{2,1,0:T(8,128)(2,1)S(1)} %wide_queries.3.q_ref, bf16[5120,128]{1,0:T(8,128)(2,1)S(1)} %collective-permute-done.10.refs_0_, ...), custom_call_target="tpu_custom_call" | custom-call | flops 4000000000 | tf_op jit(solution)/shard_map/part_stage/pallas_call | solution.py:325
  116.3 8.7 %collective-permute-done.12.refs_6_ = bf16[4,144,512]{2,1,0:T(8,128)(2,1)S(1)} collective-permute-done((bf16[4,144,512]{2,1,0:T(8,128)(2,1)S(1)}, bf16[4,144,512]{2,1,0:T(8,128)(2,1)S(1)}, u32[]{:S(2)}, u32[]{:S(2)}) %collective-permute-start.12) | collective-permute-done | bytes 589856 | tf_op jit(solution)/shard_map/ppermute | solution.py:428
  124.9 4.0 %last_stage.2 = bf16[256,1024]{1,0:T(8,128)(2,1)S(1)} custom-call(s32[4]{0:T(128)S(1)} %pad_add_fusion.5.order_ref, s32[8,17]{1,0:T(8,128)S(1)} %get-tuple-element.64.list_ref, bf16[8,512,256]{2,1,0:T(8,128)(2,1)S(1)} %wide_queries.2.q_ref, bf16[5120,128]{1,0:T(8,128)(2,1)S(1)} %collective-permute-done.10.refs_0_, ...), custom_call_target="tpu_custom_call" | custom-call | flops 5000000000 | tf_op jit(solution)/shard_map/last_stage/pallas_call | solution.py:380
  128.9 1.5 fusion.15
  130.5 0.1 collective-permute-start.13
  130.6 0.5 collective-permute-start.14
  131.1 1.1 collective-permute-start.15
  132.2 0.0 collective-permute-done.13
  132.2 0.5 collective-permute-done.14
  132.7 0.1 fusion.2
  132.8 0.5 collective-permute-start.18
  133.3 13.1 %collective-permute-done.15.refs_6_ = bf16[4,144,512]{2,1,0:T(8,128)(2,1)S(1)} collective-permute-done((bf16[4,144,512]{2,1,0:T(8,128)(2,1)S(1)}, bf16[4,144,512]{2,1,0:T(8,128)(2,1)S(1)}, u32[]{:S(2)}, u32[]{:S(2)}) %collective-permute-start.15) | collective-permute-done | bytes 589856 | tf_op jit(solution)/shard_map/ppermute | solution.py:428
  146.4 3.3 %last_stage.3 = bf16[256,1024]{1,0:T(8,128)(2,1)S(1)} custom-call(s32[4]{0:T(128)S(1)} %pad_add_fusion.4.order_ref, s32[8,17]{1,0:T(8,128)S(1)} %get-tuple-element.64.list_ref, bf16[8,512,256]{2,1,0:T(8,128)(2,1)S(1)} %wide_queries.2.q_ref, bf16[5120,128]{1,0:T(8,128)(2,1)S(1)} %collective-permute-done.10.refs_0_, ...), custom_call_target="tpu_custom_call" | custom-call | flops 5000000000 | tf_op jit(solution)/shard_map/last_stage/pallas_call | solution.py:380
  149.7 1.6 %fusion.16 = (bf16[256,2560]{1,0:T(8,128)(2,1)S(1)}, f32[256,2560]{1,0:T(8,128)S(1)}) fusion(bf16[256,1024]{1,0:T(8,128)(2,1)S(1)} %last_stage.3, bf16[1024,2560]{1,0:T(8,128)(2,1)S(1)} %bitcast.50), kind=kOutput, calls=%fused_computation.75 | convolution fusion | flops 1342832640 | bytes 9699328 | tf_op jit(solution)/shard_map/dot_general | solution.py:525
  151.3 0.1 collective-permute-start.16
  151.4 0.5 collective-permute-start.17
  151.9 1.1 collective-permute-done.16
  153.0 0.5 collective-permute-done.17
  153.5 1.0 fusion.3
  (40 shorter events, 0.3 us)
Async XLA Ops:
  0.0 1.3 copy-start.1
  1.3 0.7 copy-start.3
  2.0 10.6 %copy-start.5 = (s32[1,8,1,16]{3,2,1,0:T(1,128)S(1)}, s32[1,8,1,16]{3,2,1,0:T(1,128)}, u32[]{:S(2)}) copy-start(s32[1,8,1,16]{3,2,1,0:T(1,128)} %param.13) | copy-start | bytes 1540
  2.0 13.4 %copy-start.4 = (f32[1,512,1,24]{1,3,2,0:T(8,128)S(1)}, f32[1,512,1,24]{1,3,2,0:T(8,128)}, u32[]{:S(2)}) copy-start(f32[1,512,1,24]{1,3,2,0:T(8,128)} %param.12) | copy-start | bytes 147460
  2.0 18.7 %copy-start = (bf16[1,512,1,1536]{3,1,2,0:T(8,128)(2,1)S(1)}, bf16[1,512,1,1536]{3,1,2,0:T(8,128)(2,1)}, u32[]{:S(2)}) copy-start(bf16[1,512,1,1536]{3,1,2,0:T(8,128)(2,1)} %param.8) | copy-start | bytes 4718596
  5.3 39.4 %collective-permute-start.4 = (bf16[5120,128]{1,0:T(8,128)(2,1)}, bf16[5120,128]{1,0:T(8,128)(2,1)}, u32[]{:S(2)}, u32[]{:S(2)}) collective-permute-start(bf16[5120,128]{1,0:T(8,128)(2,1)} %get-tuple-element.27.refs_0_), channel_id=1, source_target_pairs={{0,8},{8,16},{16,24},{1,9},{9,17},{17,25},{2,10},{10,18},{18,26},{... | collective-permute-start | bytes 3932168 | tf_op jit(solution)/shard_map/ppermute | solution.py:448
  11.3 33.4 %collective-permute-start.5 = (bf16[5120,128]{1,0:T(8,128)(2,1)}, bf16[5120,128]{1,0:T(8,128)(2,1)S(1)}, u32[]{:S(2)}, u32[]{:S(2)}) collective-permute-start(bf16[5120,128]{1,0:T(8,128)(2,1)} %get-tuple-element.27.refs_0_), channel_id=1, source_target_pairs={{8,0},{16,8},{24,16},{9,1},{17,9},{25,17},{10,2},{18,10},{26,18},{... | collective-permute-start | bytes 3932168 | tf_op jit(solution)/shard_map/ppermute | solution.py:448
  12.6 3.7 %collective-permute-start = (s32[8,16]{1,0:T(8,128)S(1)}, s32[8,16]{1,0:T(8,128)S(1)}, u32[]{:S(2)}, u32[]{:S(2)}) collective-permute-start(s32[8,16]{1,0:T(8,128)S(1)} %bitcast.51), channel_id=1, source_target_pairs={{0,4},{4,0},{1,5},{5,1},{2,6},{6,2},{3,7},{7,3},{8,12},{12,8},{9,1... | collective-permute-start | bytes 1544 | tf_op jit(solution)/shard_map/ppermute | solution.py:428
  14.2 3.8 %collective-permute-start.1 = (bf16[32,384]{1,0:T(8,128)(2,1)S(1)}, bf16[32,384]{1,0:T(8,128)(2,1)S(1)}, u32[]{:S(2)}, u32[]{:S(2)}) collective-permute-start(bf16[32,384]{1,0:T(8,128)(2,1)S(1)} %get-tuple-element.24), channel_id=1, source_target_pairs={{0,4},{4,0},{1,5},{5,1},{2,6},{6,2},{3,7},{7,3},{8,12},{12,8},{9,1... | collective-permute-start | bytes 73736 | tf_op jit(solution)/shard_map/ppermute | solution.py:423
  18.0 26.7 %collective-permute-start.3 = (bf16[64,384]{1,0:T(8,128)(2,1)S(1)}, bf16[64,384]{1,0:T(8,128)(2,1)S(1)}, u32[]{:S(2)}, u32[]{:S(2)}) collective-permute-start(bf16[64,384]{1,0:T(8,128)(2,1)S(1)} %constant_dynamic-update-slice_fusion), channel_id=1, source_target_pairs={{0,8},{8,0},{16,24},{24,16},{1,9},{9,1},{17,25},{25,17},{2,10},{10... | collective-permute-start | bytes 147464 | tf_op jit(solution)/shard_map/ppermute | solution.py:423
  20.7 2.2 %copy-start.2 = (bf16[1,512,1,320]{1,3,2,0:T(8,128)(2,1)S(1)}, bf16[1,512,1,320]{1,3,2,0:T(8,128)(2,1)}, u32[]{:S(2)}) copy-start(bf16[1,512,1,320]{1,3,2,0:T(8,128)(2,1)} %param.9) | copy-start | bytes 983044
  20.7 37.7 %collective-permute-start.9 = (bf16[512,1536]{1,0:T(8,128)(2,1)S(1)}, bf16[512,1536]{1,0:T(8,128)(2,1)S(1)}, u32[]{:S(2)}, u32[]{:S(2)}) collective-permute-start(bf16[512,1536]{1,0:T(8,128)(2,1)S(1)} %bitcast.44), channel_id=1, source_target_pairs={{0,4},{4,0},{1,5},{5,1},{2,6},{6,2},{3,7},{7,3},{8,12},{12,8},{9,1... | collective-permute-start | bytes 4718600 | tf_op jit(solution)/shard_map/ppermute | solution.py:428
  22.9 67.5 %collective-permute-start.2 = (bf16[320,512]{1,0:T(8,128)(2,1)S(1)}, bf16[320,512]{1,0:T(8,128)(2,1)S(1)}, u32[]{:S(2)}, u32[]{:S(2)}) collective-permute-start(bf16[320,512]{1,0:T(8,128)(2,1)S(1)} %bitcast.47), channel_id=1, source_target_pairs={{0,4},{1,5},{2,6},{3,7},{8,12},{9,13},{10,14},{11,15},{16,20},{17,... | collective-permute-start | bytes 983048 | tf_op jit(solution)/shard_map/ppermute | solution.py:470
  44.7 45.6 %collective-permute-start.6 = (bf16[128,384]{1,0:T(8,128)(2,1)S(1)}, bf16[128,384]{1,0:T(8,128)(2,1)S(1)}, u32[]{:S(2)}, u32[]{:S(2)}) collective-permute-start(bf16[128,384]{1,0:T(8,128)(2,1)S(1)} %constant_dynamic-update-slice_fusion.2), channel_id=1, source_target_pairs={{0,16},{8,24},{16,0},{24,8},{1,17},{9,25},{17,1},{25,9},{2,18},{10... | collective-permute-start | bytes 294920 | tf_op jit(solution)/shard_map/ppermute | solution.py:423
  46.4 22.3 %collective-permute-start.7 = (bf16[5120,128]{1,0:T(8,128)(2,1)}, bf16[5120,128]{1,0:T(8,128)(2,1)S(1)}, u32[]{:S(2)}, u32[]{:S(2)}) collective-permute-start(bf16[5120,128]{1,0:T(8,128)(2,1)} %collective-permute-done.4.refs_1_), channel_id=1, source_target_pairs={{8,16},{16,24},{9,17},{17,25},{10,18},{18,26},{11,19},{19,27},{12,... | collective-permute-start | bytes 3932168 | tf_op jit(solution)/shard_map/ppermute | solution.py:448
  47.1 32.1 %collective-permute-start.8 = (bf16[5120,128]{1,0:T(8,128)(2,1)S(1)}, bf16[5120,128]{1,0:T(8,128)(2,1)S(1)}, u32[]{:S(2)}, u32[]{:S(2)}) collective-permute-start(bf16[5120,128]{1,0:T(8,128)(2,1)S(1)} %collective-permute-done.5.refs_2_), channel_id=1, source_target_pairs={{8,0},{16,8},{9,1},{17,9},{10,2},{18,10},{11,3},{19,11},{12,4},{20... | collective-permute-start | bytes 3932168 | tf_op jit(solution)/shard_map/ppermute | solution.py:448
  68.7 33.5 %collective-permute-start.10 = (bf16[5120,128]{1,0:T(8,128)(2,1)S(1)}, bf16[5120,128]{1,0:T(8,128)(2,1)S(1)}, u32[]{:S(2)}, u32[]{:S(2)}) collective-permute-start(bf16[5120,128]{1,0:T(8,128)(2,1)S(1)} %collective-permute-done.7.refs_0_), channel_id=1, source_target_pairs={{16,24},{17,25},{18,26},{19,27},{20,28},{21,29},{22,30},{23,31}} | collective-permute-start | bytes 3932168 | tf_op jit(solution)/shard_map/ppermute | solution.py:448
  79.2 30.0 %collective-permute-start.11 = (bf16[5120,128]{1,0:T(8,128)(2,1)S(1)}, bf16[5120,128]{1,0:T(8,128)(2,1)S(1)}, u32[]{:S(2)}, u32[]{:S(2)}) collective-permute-start(bf16[5120,128]{1,0:T(8,128)(2,1)S(1)} %collective-permute-done.8.refs_1_), channel_id=1, source_target_pairs={{8,0},{9,1},{10,2},{11,3},{12,4},{13,5},{14,6},{15,7}} | collective-permute-start | bytes 3932168 | tf_op jit(solution)/shard_map/ppermute | solution.py:448
  112.7 12.2 %collective-permute-start.12 = (bf16[4,144,512]{2,1,0:T(8,128)(2,1)S(1)}, bf16[4,144,512]{2,1,0:T(8,128)(2,1)S(1)}, u32[]{:S(2)}, u32[]{:S(2)}) collective-permute-start(bf16[4,144,512]{2,1,0:T(8,128)(2,1)S(1)} %part_stage.3), channel_id=1, source_target_pairs={{0,4},{4,0},{1,5},{5,1},{2,6},{6,2},{3,7},{7,3},{8,12},{12,8},{9,1... | collective-permute-start | bytes 1769480 | tf_op jit(solution)/shard_map/ppermute | solution.py:428
  114.0 14.9 %slice-start = ((s8[5242880]{0:T(1024)(128)(4,1)}), s8[4194304]{0:T(1024)(128)(4,1)S(1)}, s32[]{:S(2)}) async-start(s8[5242880]{0:T(1024)(128)(4,1)} %bitcast.49), calls=%async_computation | async-start | bytes 8388608
  124.9 4.0 %slice-start.1 = ((s8[5242880]{0:T(1024)(128)(4,1)}), s8[1048576]{0:T(1024)(128)(4,1)S(1)}, s32[]{:S(2)}) async-start(s8[5242880]{0:T(1024)(128)(4,1)} %bitcast.49), calls=%async_computation.1 | async-start | bytes 2097152
  130.5 1.7 %collective-permute-start.13 = (bf16[64,2560]{1,0:T(8,128)(2,1)S(1)}, bf16[64,2560]{1,0:T(8,128)(2,1)S(1)}, u32[]{:S(2)}, u32[]{:S(2)}) collective-permute-start(bf16[64,2560]{1,0:T(8,128)(2,1)S(1)} %get-tuple-element.55), channel_id=1, source_target_pairs={{0,1},{1,0},{2,3},{3,2},{4,5},{5,4},{6,7},{7,6},{8,9},{9,8},{10,11... | collective-permute-start | bytes 983048 | tf_op jit(solution)/shard_map/ppermute | solution.py:423
  130.6 2.1 %collective-permute-start.14 = (bf16[64,2560]{1,0:T(8,128)(2,1)S(1)}, bf16[64,2560]{1,0:T(8,128)(2,1)S(1)}, u32[]{:S(2)}, u32[]{:S(2)}) collective-permute-start(bf16[64,2560]{1,0:T(8,128)(2,1)S(1)} %get-tuple-element.56), channel_id=1, source_target_pairs={{0,1},{1,0},{2,3},{3,2},{4,5},{5,4},{6,7},{7,6},{8,9},{9,8},{10,11... | collective-permute-start | bytes 983048 | tf_op jit(solution)/shard_map/ppermute | solution.py:423
  131.1 15.3 %collective-permute-start.15 = (bf16[4,144,512]{2,1,0:T(8,128)(2,1)S(1)}, bf16[4,144,512]{2,1,0:T(8,128)(2,1)S(1)}, u32[]{:S(2)}, u32[]{:S(2)}) collective-permute-start(bf16[4,144,512]{2,1,0:T(8,128)(2,1)S(1)} %part_stage.2), channel_id=1, source_target_pairs={{0,4},{4,0},{1,5},{5,1},{2,6},{6,2},{3,7},{7,3},{8,12},{12,8},{9,1... | collective-permute-start | bytes 1769480 | tf_op jit(solution)/shard_map/ppermute | solution.py:428
  132.8 20.7 %collective-permute-start.18 = (bf16[128,2560]{1,0:T(8,128)(2,1)S(1)}, bf16[128,2560]{1,0:T(8,128)(2,1)S(1)}, u32[]{:S(2)}, u32[]{:S(2)}) collective-permute-start(bf16[128,2560]{1,0:T(8,128)(2,1)S(1)} %fusion.2), channel_id=1, source_target_pairs={{0,2},{1,3},{2,0},{3,1},{4,6},{5,7},{6,4},{7,5},{8,10},{9,11},{10,... | collective-permute-start | bytes 1966088 | tf_op jit(solution)/shard_map/ppermute | solution.py:423
  151.3 1.7 %collective-permute-start.16 = (bf16[64,2560]{1,0:T(8,128)(2,1)S(1)}, bf16[64,2560]{1,0:T(8,128)(2,1)S(1)}, u32[]{:S(2)}, u32[]{:S(2)}) collective-permute-start(bf16[64,2560]{1,0:T(8,128)(2,1)S(1)} %get-tuple-element.53), channel_id=1, source_target_pairs={{0,1},{1,0},{2,3},{3,2},{4,5},{5,4},{6,7},{7,6},{8,9},{9,8},{10,11... | collective-permute-start | bytes 983048 | tf_op jit(solution)/shard_map/ppermute | solution.py:423
  151.4 2.1 %collective-permute-start.17 = (bf16[64,2560]{1,0:T(8,128)(2,1)S(1)}, bf16[64,2560]{1,0:T(8,128)(2,1)S(1)}, u32[]{:S(2)}, u32[]{:S(2)}) collective-permute-start(bf16[64,2560]{1,0:T(8,128)(2,1)S(1)} %get-tuple-element.54), channel_id=1, source_target_pairs={{0,1},{1,0},{2,3},{3,2},{4,5},{5,4},{6,7},{7,6},{8,9},{9,8},{10,11... | collective-permute-start | bytes 983048 | tf_op jit(solution)/shard_map/ppermute | solution.py:423

commit v3 on v2

--- a/solution.py
+++ b/solution.py
@@ -340,31 +340,17 @@
     )(order, lists, wide, *kvs, *state)
 
 
-def last_kernel(n_kv, unit, order_ref, list_ref, q_ref, *refs):
-    kv_refs, refs = refs[:n_kv], refs[n_kv:]
-    state_in, acc_in, near_ref, gate_ref = refs[:4]
-    part_refs, (out_ref, acc_ref, key_ref, value_ref) = refs[4:-4], refs[-4:]
-    acc_ref[...] = acc_in[0]
-    top, total = add_selected(
-        unit,
-        list_ref,
-        order_ref[pl.program_id(0)],
-        q_ref,
-        kv_refs,
-        state_in[0, 0:1],
-        state_in[0, 1:2],
-        acc_ref,
-        key_ref,
-        value_ref,
-    )
-    logs = [log_total(top, total)]
+def last_kernel(order_ref, state_ref, acc_ref, near_ref, gate_ref, *refs):
+    part_refs, out_ref = refs[:-1], refs[-1]
+    total = state_ref[0, 1:2]
+    logs = [log_total(state_ref[0, 0:1], total)]
     for part_ref in part_refs:
         notes = part_ref[0, DV:].astype(F32)
         logs.append(notes[0:1] + notes[1:2] + notes[2:3])
     peak = functools.reduce(jnp.maximum, logs)
     shares = [jnp.exp(log - peak) for log in logs]
     gate = gate_ref[0, 1:2] / functools.reduce(jnp.add, shares)
-    out = near_ref[0] + acc_ref[...] * (gate * shares[0] / jnp.maximum(total, 1e-30))
+    out = near_ref[0] + acc_ref[0] * (gate * shares[0] / jnp.maximum(total, 1e-30))
     for share, part_ref in zip(shares[1:], part_refs):
         out = out + part_ref[0, :DV].astype(F32) * (gate * share)
     for head in range(0, HQ, 2):
@@ -373,32 +359,29 @@
         out_ref[:, (head + 1) * DV : (head + 2) * DV] = pair[BLK:]
 
 
-def last_stage(unit, order, lists, wide, kvs, state, near, gates, others):
-    _, lanes, _ = wide.shape
+def last_stage(order, state, near, gates, others):
+    lanes = near.shape[2]
     (steps,) = order.shape
-    at = lambda i, order, *_: (order[i], 0, 0)
+    at = lambda i, order: (order[i], 0, 0)
     return pl.pallas_call(
-        functools.partial(last_kernel, len(kvs), unit),
+        last_kernel,
         grid_spec=pltpu.PrefetchScalarGridSpec(
-            num_scalar_prefetch=2,
+            num_scalar_prefetch=1,
             grid=(steps,),
-            in_specs=[pl.BlockSpec((1, lanes, EXT), at)]
-            + [whole_spec(kv) for kv in kvs]
-            + [
+            in_specs=[
                 pl.BlockSpec((1, 2, lanes), at),
                 pl.BlockSpec((1, DV, lanes), at),
                 pl.BlockSpec((1, DV, lanes), at),
                 pl.BlockSpec((1, 3, lanes), at),
             ]
-            + [pl.BlockSpec((1, DV + NOTES, lanes), lambda i, *_: (i, 0, 0)) for _ in others],
-            out_specs=pl.BlockSpec((BLK, HQ * DV), lambda i, *_: (i, 0)),
-            scratch_shapes=[pltpu.VMEM((DV, lanes), F32)] + scratch(unit),
+            + [pl.BlockSpec((1, DV + NOTES, lanes), lambda i, order: (i, 0, 0)) for _ in others],
+            out_specs=pl.BlockSpec((BLK, HQ * DV), lambda i, order: (i, 0)),
         ),
         out_shape=jax.ShapeDtypeStruct((steps * BLK, HQ * DV), BF),
         compiler_params=params(),
         cost_estimate=cost(5),
         name="last_stage",
-    )(order, lists, wide, *kvs, *state, near, gates, *others)
+    )(order, *state, near, gates, *others)
 
 
 def held_lists(ids, owners, held):
@@ -516,12 +499,11 @@
         for order in orders
     ]
     others = [[shift(p, "ctx", d + 1) for d, p in enumerate(ps)] for ps in parts]
-    orders[0] = lax.optimization_barrier((orders[0], parts[1]))[0]
+    mine_table = lax.optimization_barrier((table[0], parts[1]))[0]
+    state = stage(UNIT, mine_table, wides[0], kvs, states[0])
 
     def half_sum(which):
-        out = last_stage(
-            UNIT, orders[which], table[0], wides[0], kvs, states[0], near, gates, others[which]
-        )
+        out = last_stage(orders[which], state, near, gates, others[which])
         share = jnp.dot(out, w_out, preferred_element_type=F32)
         size = chunk // PIECES
         pieces = [share[k * size : (k + 1) * size].astype(BF) for k in range(PIECES)]

time: 155 us -> 150 us (0.968)
  waiting for transfers between devices: 60.6 us -> 54.8 us
    ppermute x4, waiting for transfers between devices: 22.3 us -> 16.2 us  [shift(): lax.ppermute(value, axis, [(i, (i + steps) % count) for i in range(count)])]
    pallas_call x2, Pallas kernels: 7.26 us -> 2.46 us  [last_stage(): pl.pallas_call(last_kernel, grid_spec=pltpu.PrefetchScalarGridSpec(num_sc...]
    pallas_call x4 -> x5, Pallas kernels: 28.9 us -> 33.7 us  [stage(): pl.pallas_call(functools.partial(stage_kernel, first, len(kvs), unit), gr...]
  transfers between devices with their start and end apart: 19 -> 19, of which waited for: 10 -> 10; matrix products, arithmetic and copies ran while one was open for 2% -> 2% of each run, Pallas kernels for 31% -> 34%
where the time goes in v3:
time: 150 us; the launch traced here: 149 us
  Pallas kernels  58.9 us (39%)
  waiting for transfers between devices  54.8 us (37%)
  starting transfers between devices  26.3 us (18%)
  matrix products  3.07 us (2%)
  local copies, waits for them, and re-layouts  2.61 us (2%)
  other arithmetic  2.59 us (2%)
    pallas_call x5, Pallas kernels, stage(): pl.pallas_call(functools.partial(stage_kernel, first, len(kvs), unit), gr...  33.7 us
    ppermute x8, waiting for transfers between devices, swap(): lax.ppermute(value, axis, [(i, i ^ bit) for i in range(lax.axis_size(axis...  21 us
    ppermute x6, waiting for transfers between devices, spread(): held[side] = lax.ppermute(held[side], axis, pairs)  17.6 us
    ppermute x4, waiting for transfers between devices, shift(): lax.ppermute(value, axis, [(i, (i + steps) % count) for i in range(count)])  16.2 us
    pallas_call x1, Pallas kernels, near_parts(): pl.pallas_call(near_kernel, grid_spec=pltpu.PrefetchScalarGridSpec(num_sc...  11.7 us
    ppermute x6, starting transfers between devices, spread(): held[side] = lax.ppermute(held[side], axis, pairs)  11.5 us
    ppermute x8, starting transfers between devices, swap(): lax.ppermute(value, axis, [(i, i ^ bit) for i in range(lax.axis_size(axis...  6.92 us
    pallas_call x2, Pallas kernels, part_stage(): pl.pallas_call(functools.partial(part_kernel, len(kvs), unit), grid_spec=...  5.72 us
  transfers between devices with their start and end apart: 19, of which 10 were waited for; matrix products, arithmetic and copies ran while one was open for 2% of the time, Pallas kernels for 34%

profile of v3, /device:TPU:0, one launch (start us, length us, event | category | flops | bytes accessed | tf_op | source)
XLA Modules:
  0.0 149.4 jit_solution(8419208667620198210)
XLA Ops:
  0.0 1.3 copy-done.1
  1.3 0.7 copy-done.3
  2.0 3.3 %pack.1 = (bf16[5120,128]{1,0:T(8,128)(2,1)}, bf16[32,384]{1,0:T(8,128)(2,1)S(1)}) custom-call(bf16[320,2048]{1,0:T(8,128)(2,1)S(1)} %bitcast.46, f32[2,64]{1,0:T(2,128)S(1)} %copy-done.3), custom_call_target="tpu_custom_call" | custom-call | flops 5000000000 | tf_op jit(solution)/shard_map/pack/pallas_call | solution.py:74
  5.3 6.0 %collective-permute-start.4 = (bf16[5120,128]{1,0:T(8,128)(2,1)}, bf16[5120,128]{1,0:T(8,128)(2,1)}, u32[]{:S(2)}, u32[]{:S(2)}) collective-permute-start(bf16[5120,128]{1,0:T(8,128)(2,1)} %get-tuple-element.29.refs_0_), channel_id=1, source_target_pairs={{0,8},{8,16},{16,24},{1,9},{9,17},{17,25},{2,10},{10,18},{18,26},{... | collective-permute-start | bytes 3932168 | tf_op jit(solution)/shard_map/ppermute | solution.py:431
  11.3 1.3 collective-permute-start.5
  12.6 1.6 %collective-permute-start = (s32[8,16]{1,0:T(8,128)S(1)}, s32[8,16]{1,0:T(8,128)S(1)}, u32[]{:S(2)}, u32[]{:S(2)}) collective-permute-start(s32[8,16]{1,0:T(8,128)S(1)} %bitcast.51), channel_id=1, source_target_pairs={{0,4},{4,0},{1,5},{5,1},{2,6},{6,2},{3,7},{7,3},{8,12},{12,8},{9,1... | collective-permute-start | bytes 1544 | tf_op jit(solution)/shard_map/ppermute | solution.py:411
  14.2 0.5 collective-permute-start.1
  15.4 0.1 div.39
  15.6 0.1 reshape.525
  15.7 0.1 pad_add_fusion.5.order_ref
  15.8 0.1 pad_add_fusion.4.order_ref
  15.9 0.4 collective-permute-done
  16.3 0.1 convert_reduce_fusion.3
  16.5 0.2 select_add_fusion
  16.6 0.2 convert_reduce_fusion
  16.9 0.1 copy.30
  17.0 0.1 copy.29
  17.0 0.1 copy.26
  17.1 0.2 select_reduce_fusion
  17.4 0.1 fusion.11
  17.4 0.1 fusion.12
  17.5 0.1 select_reduce_fusion.2
  17.7 0.1 pad_add_fusion.1
  17.7 0.3 collective-permute-done.1
  18.0 2.6 %collective-permute-start.3 = (bf16[64,384]{1,0:T(8,128)(2,1)S(1)}, bf16[64,384]{1,0:T(8,128)(2,1)S(1)}, u32[]{:S(2)}, u32[]{:S(2)}) collective-permute-start(bf16[64,384]{1,0:T(8,128)(2,1)S(1)} %constant_dynamic-update-slice_fusion), channel_id=1, source_target_pairs={{0,8},{8,0},{16,24},{24,16},{1,9},{9,1},{17,25},{25,17},{2,10},{10... | collective-permute-start | bytes 147464 | tf_op jit(solution)/shard_map/ppermute | solution.py:406
  20.7 1.3 collective-permute-start.9
  21.9 1.0 wide_queries.2.q_ref
  22.9 2.7 %collective-permute-start.2 = (bf16[320,512]{1,0:T(8,128)(2,1)S(1)}, bf16[320,512]{1,0:T(8,128)(2,1)S(1)}, u32[]{:S(2)}, u32[]{:S(2)}) collective-permute-start(bf16[320,512]{1,0:T(8,128)(2,1)S(1)} %bitcast.47), channel_id=1, source_target_pairs={{0,4},{1,5},{2,6},{3,7},{8,12},{9,13},{10,14},{11,15},{16,20},{17,... | collective-permute-start | bytes 983048 | tf_op jit(solution)/shard_map/ppermute | solution.py:453
  25.6 19.1 %collective-permute-done.3 = bf16[64,384]{1,0:T(8,128)(2,1)S(1)} collective-permute-done((bf16[64,384]{1,0:T(8,128)(2,1)S(1)}, bf16[64,384]{1,0:T(8,128)(2,1)S(1)}, u32[]{:S(2)}, u32[]{:S(2)}) %collective-permute-start.3) | collective-permute-done | bytes 49184 | tf_op jit(solution)/shard_map/ppermute | solution.py:406
  44.7 1.6 %collective-permute-start.6 = (bf16[128,384]{1,0:T(8,128)(2,1)S(1)}, bf16[128,384]{1,0:T(8,128)(2,1)S(1)}, u32[]{:S(2)}, u32[]{:S(2)}) collective-permute-start(bf16[128,384]{1,0:T(8,128)(2,1)S(1)} %constant_dynamic-update-slice_fusion.2), channel_id=1, source_target_pairs={{0,16},{8,24},{16,0},{24,8},{1,17},{9,25},{17,1},{25,9},{2,18},{10... | collective-permute-start | bytes 294920 | tf_op jit(solution)/shard_map/ppermute | solution.py:406
  46.4 0.7 collective-permute-start.7
  47.1 1.3 collective-permute-start.8
  48.4 8.6 %stage.5 = (f32[8,2,512]{2,1,0:T(2,128)S(1)}, f32[8,128,512]{2,1,0:T(8,128)S(1)}) custom-call(s32[8,17]{1,0:T(8,128)S(1)} %get-tuple-element.62.list_ref, bf16[8,512,256]{2,1,0:T(8,128)(2,1)S(1)} %wide_queries.2.q_ref, bf16[5120,128]{1,0:T(8,128)(2,1)} %get-tuple-element.29.refs_0_, bf16[5120,128]{1,0:T(8,128)(2,1)} %collective-permute-done.4.refs_1_, ...), custom_call_target="tpu_custom_call" | custom-call | flops 8999999488 | tf_op jit(solution)/shard_map/stage/pallas_call | solution.py:271
  57.0 1.0 wide_queries.3.q_ref
  58.0 9.3 %stage.7 = (f32[8,2,512]{2,1,0:T(2,128)S(1)}, f32[8,128,512]{2,1,0:T(8,128)S(1)}) custom-call(s32[8,17]{1,0:T(8,128)S(1)} %get-tuple-element.61.list_ref, bf16[8,512,256]{2,1,0:T(8,128)(2,1)S(1)} %wide_queries.3.q_ref, bf16[5120,128]{1,0:T(8,128)(2,1)} %get-tuple-element.29.refs_0_, bf16[5120,128]{1,0:T(8,128)(2,1)} %collective-permute-done.4.refs_1_, ...), custom_call_target="tpu_custom_call" | custom-call | flops 8999999488 | tf_op jit(solution)/shard_map/stage/pallas_call | solution.py:271
  67.4 0.7 collective-permute-start.10
  68.1 11.1 %collective-permute-done.8.refs_1_ = bf16[5120,128]{1,0:T(8,128)(2,1)S(1)} collective-permute-done((bf16[5120,128]{1,0:T(8,128)(2,1)S(1)}, bf16[5120,128]{1,0:T(8,128)(2,1)S(1)}, u32[]{:S(2)}, u32[]{:S(2)}) %collective-permute-start.8) | collective-permute-done | bytes 1310752 | tf_op jit(solution)/shard_map/ppermute | solution.py:431
  79.2 1.5 collective-permute-start.11
  80.7 5.5 %stage.8 = (f32[8,2,512]{2,1,0:T(2,128)S(1)}, f32[8,128,512]{2,1,0:T(8,128)S(1)}) custom-call(s32[8,17]{1,0:T(8,128)S(1)} %get-tuple-element.63.list_ref, bf16[8,512,256]{2,1,0:T(8,128)(2,1)S(1)} %wide_queries.3.q_ref, bf16[5120,128]{1,0:T(8,128)(2,1)S(1)} %collective-permute-done.7.refs_0_, ...), custom_call_target="tpu_custom_call", output_to_operand_aliasing={{0}: (4, {}), {1}: (5, {})} | custom-call | flops 8999999488 | tf_op jit(solution)/shard_map/stage/pallas_call | solution.py:271
  86.2 4.8 %stage.6 = (f32[8,2,512]{2,1,0:T(2,128)S(1)}, f32[8,128,512]{2,1,0:T(8,128)S(1)}) custom-call(s32[8,17]{1,0:T(8,128)S(1)} %get-tuple-element.64.list_ref, bf16[8,512,256]{2,1,0:T(8,128)(2,1)S(1)} %wide_queries.2.q_ref, bf16[5120,128]{1,0:T(8,128)(2,1)S(1)} %collective-permute-done.7.refs_0_, ...), custom_call_target="tpu_custom_call", output_to_operand_aliasing={{0}: (4, {}), {1}: (5, {})} | custom-call | flops 8999999488 | tf_op jit(solution)/shard_map/stage/pallas_call | solution.py:271
  91.0 11.7 %near.1.near_ref = f32[8,128,512]{2,1,0:T(8,128)S(1)} custom-call(s32[1]{0:T(128)} %bitcast.4.begin_ref, bf16[8,512,256]{2,1,0:T(8,128)(2,1)S(1)} %wide_queries.2.q_ref, bf16[320,512]{1,0:T(8,128)(2,1)S(1)} %collective-permute-done.2.far_ref, bf16[320,512]{1,0:T(8,128)(2,1)S(1)} %bitcast.48, bf16[256,384]{1,0:T(8,128)(2,1)S(1)} %pad_maximum_fusion.comp_ref, ...), custom_call_target="tpu_custom_call" | custom-call | flops 14000000000 | tf_op jit(solution)/shard_map/near/pallas_call | solution.py:168
  102.8 6.4 %collective-permute-done.11.refs_1_ = bf16[5120,128]{1,0:T(8,128)(2,1)S(1)} collective-permute-done((bf16[5120,128]{1,0:T(8,128)(2,1)S(1)}, bf16[5120,128]{1,0:T(8,128)(2,1)S(1)}, u32[]{:S(2)}, u32[]{:S(2)}) %collective-permute-start.11) | collective-permute-done | bytes 1310752 | tf_op jit(solution)/shard_map/ppermute | solution.py:431
  109.2 3.5 %part_stage.3 = bf16[4,144,512]{2,1,0:T(8,128)(2,1)S(1)} custom-call(s32[4]{0:T(128)S(1)} %pad_add_fusion.5.order_ref, s32[8,17]{1,0:T(8,128)S(1)} %get-tuple-element.68.list_ref, bf16[8,512,256]{2,1,0:T(8,128)(2,1)S(1)} %wide_queries.3.q_ref, bf16[5120,128]{1,0:T(8,128)(2,1)S(1)} %collective-permute-done.10.refs_0_, ...), custom_call_target="tpu_custom_call" | custom-call | flops 4000000000 | tf_op jit(solution)/shard_map/part_stage/pallas_call | solution.py:325
  112.7 0.9 collective-permute-start.12
  113.6 2.2 %part_stage.2 = bf16[4,144,512]{2,1,0:T(8,128)(2,1)S(1)} custom-call(s32[4]{0:T(128)S(1)} %pad_add_fusion.4.order_ref, s32[8,17]{1,0:T(8,128)S(1)} %get-tuple-element.68.list_ref, bf16[8,512,256]{2,1,0:T(8,128)(2,1)S(1)} %wide_queries.3.q_ref, bf16[5120,128]{1,0:T(8,128)(2,1)S(1)} %collective-permute-done.10.refs_0_, ...), custom_call_target="tpu_custom_call" | custom-call | flops 4000000000 | tf_op jit(solution)/shard_map/part_stage/pallas_call | solution.py:325
  115.9 0.0 slice-start.1
  115.9 5.5 %stage.9 = (f32[8,2,512]{2,1,0:T(2,128)S(1)}, f32[8,128,512]{2,1,0:T(8,128)S(1)}) custom-call(s32[8,17]{1,0:T(8,128)S(1)} %get-tuple-element.43.list_ref, bf16[8,512,256]{2,1,0:T(8,128)(2,1)S(1)} %wide_queries.2.q_ref, bf16[5120,128]{1,0:T(8,128)(2,1)S(1)} %collective-permute-done.10.refs_0_, ...), custom_call_target="tpu_custom_call", output_to_operand_aliasing={{0}: (4, {}), {1}: (5, {})} | custom-call | flops 8999999488 | tf_op jit(solution)/shard_map/stage/pallas_call | solution.py:271
  121.4 3.2 %collective-permute-done.12.refs_0_ = bf16[4,144,512]{2,1,0:T(8,128)(2,1)S(1)} collective-permute-done((bf16[4,144,512]{2,1,0:T(8,128)(2,1)S(1)}, bf16[4,144,512]{2,1,0:T(8,128)(2,1)S(1)}, u32[]{:S(2)}, u32[]{:S(2)}) %collective-permute-start.12) | collective-permute-done | bytes 589856 | tf_op jit(solution)/shard_map/ppermute | solution.py:411
  124.5 1.2 last_stage.2
  125.8 1.5 %fusion.15 = (bf16[256,2560]{1,0:T(8,128)(2,1)S(1)}, f32[256,2560]{1,0:T(8,128)S(1)}) fusion(bf16[256,1024]{1,0:T(8,128)(2,1)S(1)} %last_stage.2, bf16[1024,2560]{1,0:T(8,128)(2,1)S(1)} %bitcast.50), kind=kOutput, calls=%fused_computation.74 | convolution fusion | flops 1342832640 | bytes 9699328 | tf_op jit(solution)/shard_map/dot_general | solution.py:507
  127.4 0.1 collective-permute-start.13
  127.5 0.5 collective-permute-start.14
  128.0 1.5 collective-permute-start.15
  129.5 0.1 collective-permute-done.14
  129.6 0.2 fusion.2
  129.7 1.0 collective-permute-start.18
  130.7 12.6 %collective-permute-done.15.refs_0_ = bf16[4,144,512]{2,1,0:T(8,128)(2,1)S(1)} collective-permute-done((bf16[4,144,512]{2,1,0:T(8,128)(2,1)S(1)}, bf16[4,144,512]{2,1,0:T(8,128)(2,1)S(1)}, u32[]{:S(2)}, u32[]{:S(2)}) %collective-permute-start.15) | collective-permute-done | bytes 589856 | tf_op jit(solution)/shard_map/ppermute | solution.py:411
  143.3 1.2 last_stage.3
  144.5 1.5 %fusion.16 = (bf16[256,2560]{1,0:T(8,128)(2,1)S(1)}, f32[256,2560]{1,0:T(8,128)S(1)}) fusion(bf16[256,1024]{1,0:T(8,128)(2,1)S(1)} %last_stage.3, bf16[1024,2560]{1,0:T(8,128)(2,1)S(1)} %bitcast.50), kind=kOutput, calls=%fused_computation.75 | convolution fusion | flops 1342832640 | bytes 9699328 | tf_op jit(solution)/shard_map/dot_general | solution.py:507
  146.1 0.1 collective-permute-start.16
  146.2 0.5 collective-permute-start.17
  146.7 1.1 collective-permute-done.16
  147.8 0.5 collective-permute-done.17
  148.3 1.1 fusion.3
  (41 shorter events, 0.3 us)
Async XLA Ops:
  0.0 1.3 copy-start.1
  1.3 0.7 copy-start.3
  2.0 10.6 %copy-start.5 = (s32[1,8,1,16]{3,2,1,0:T(1,128)S(1)}, s32[1,8,1,16]{3,2,1,0:T(1,128)}, u32[]{:S(2)}) copy-start(s32[1,8,1,16]{3,2,1,0:T(1,128)} %param.13) | copy-start | bytes 1540
  2.0 13.4 %copy-start.4 = (f32[1,512,1,24]{1,3,2,0:T(8,128)S(1)}, f32[1,512,1,24]{1,3,2,0:T(8,128)}, u32[]{:S(2)}) copy-start(f32[1,512,1,24]{1,3,2,0:T(8,128)} %param.12) | copy-start | bytes 147460
  2.0 18.7 %copy-start = (bf16[1,512,1,1536]{3,1,2,0:T(8,128)(2,1)S(1)}, bf16[1,512,1,1536]{3,1,2,0:T(8,128)(2,1)}, u32[]{:S(2)}) copy-start(bf16[1,512,1,1536]{3,1,2,0:T(8,128)(2,1)} %param.8) | copy-start | bytes 4718596
  5.3 39.4 %collective-permute-start.4 = (bf16[5120,128]{1,0:T(8,128)(2,1)}, bf16[5120,128]{1,0:T(8,128)(2,1)}, u32[]{:S(2)}, u32[]{:S(2)}) collective-permute-start(bf16[5120,128]{1,0:T(8,128)(2,1)} %get-tuple-element.29.refs_0_), channel_id=1, source_target_pairs={{0,8},{8,16},{16,24},{1,9},{9,17},{17,25},{2,10},{10,18},{18,26},{... | collective-permute-start | bytes 3932168 | tf_op jit(solution)/shard_map/ppermute | solution.py:431
  11.3 33.4 %collective-permute-start.5 = (bf16[5120,128]{1,0:T(8,128)(2,1)}, bf16[5120,128]{1,0:T(8,128)(2,1)S(1)}, u32[]{:S(2)}, u32[]{:S(2)}) collective-permute-start(bf16[5120,128]{1,0:T(8,128)(2,1)} %get-tuple-element.29.refs_0_), channel_id=1, source_target_pairs={{8,0},{16,8},{24,16},{9,1},{17,9},{25,17},{10,2},{18,10},{26,18},{... | collective-permute-start | bytes 3932168 | tf_op jit(solution)/shard_map/ppermute | solution.py:431
  12.6 3.7 %collective-permute-start = (s32[8,16]{1,0:T(8,128)S(1)}, s32[8,16]{1,0:T(8,128)S(1)}, u32[]{:S(2)}, u32[]{:S(2)}) collective-permute-start(s32[8,16]{1,0:T(8,128)S(1)} %bitcast.51), channel_id=1, source_target_pairs={{0,4},{4,0},{1,5},{5,1},{2,6},{6,2},{3,7},{7,3},{8,12},{12,8},{9,1... | collective-permute-start | bytes 1544 | tf_op jit(solution)/shard_map/ppermute | solution.py:411
  14.2 3.8 %collective-permute-start.1 = (bf16[32,384]{1,0:T(8,128)(2,1)S(1)}, bf16[32,384]{1,0:T(8,128)(2,1)S(1)}, u32[]{:S(2)}, u32[]{:S(2)}) collective-permute-start(bf16[32,384]{1,0:T(8,128)(2,1)S(1)} %get-tuple-element.26), channel_id=1, source_target_pairs={{0,4},{4,0},{1,5},{5,1},{2,6},{6,2},{3,7},{7,3},{8,12},{12,8},{9,1... | collective-permute-start | bytes 73736 | tf_op jit(solution)/shard_map/ppermute | solution.py:406
  18.0 26.7 %collective-permute-start.3 = (bf16[64,384]{1,0:T(8,128)(2,1)S(1)}, bf16[64,384]{1,0:T(8,128)(2,1)S(1)}, u32[]{:S(2)}, u32[]{:S(2)}) collective-permute-start(bf16[64,384]{1,0:T(8,128)(2,1)S(1)} %constant_dynamic-update-slice_fusion), channel_id=1, source_target_pairs={{0,8},{8,0},{16,24},{24,16},{1,9},{9,1},{17,25},{25,17},{2,10},{10... | collective-permute-start | bytes 147464 | tf_op jit(solution)/shard_map/ppermute | solution.py:406
  20.7 2.2 %copy-start.2 = (bf16[1,512,1,320]{1,3,2,0:T(8,128)(2,1)S(1)}, bf16[1,512,1,320]{1,3,2,0:T(8,128)(2,1)}, u32[]{:S(2)}) copy-start(bf16[1,512,1,320]{1,3,2,0:T(8,128)(2,1)} %param.9) | copy-start | bytes 983044
  20.7 36.4 %collective-permute-start.9 = (bf16[512,1536]{1,0:T(8,128)(2,1)S(1)}, bf16[512,1536]{1,0:T(8,128)(2,1)S(1)}, u32[]{:S(2)}, u32[]{:S(2)}) collective-permute-start(bf16[512,1536]{1,0:T(8,128)(2,1)S(1)} %bitcast.44), channel_id=1, source_target_pairs={{0,4},{4,0},{1,5},{5,1},{2,6},{6,2},{3,7},{7,3},{8,12},{12,8},{9,1... | collective-permute-start | bytes 4718600 | tf_op jit(solution)/shard_map/ppermute | solution.py:411
  22.9 68.1 %collective-permute-start.2 = (bf16[320,512]{1,0:T(8,128)(2,1)S(1)}, bf16[320,512]{1,0:T(8,128)(2,1)S(1)}, u32[]{:S(2)}, u32[]{:S(2)}) collective-permute-start(bf16[320,512]{1,0:T(8,128)(2,1)S(1)} %bitcast.47), channel_id=1, source_target_pairs={{0,4},{1,5},{2,6},{3,7},{8,12},{9,13},{10,14},{11,15},{16,20},{17,... | collective-permute-start | bytes 983048 | tf_op jit(solution)/shard_map/ppermute | solution.py:453
  44.7 46.2 %collective-permute-start.6 = (bf16[128,384]{1,0:T(8,128)(2,1)S(1)}, bf16[128,384]{1,0:T(8,128)(2,1)S(1)}, u32[]{:S(2)}, u32[]{:S(2)}) collective-permute-start(bf16[128,384]{1,0:T(8,128)(2,1)S(1)} %constant_dynamic-update-slice_fusion.2), channel_id=1, source_target_pairs={{0,16},{8,24},{16,0},{24,8},{1,17},{9,25},{17,1},{25,9},{2,18},{10... | collective-permute-start | bytes 294920 | tf_op jit(solution)/shard_map/ppermute | solution.py:406
  46.4 21.0 %collective-permute-start.7 = (bf16[5120,128]{1,0:T(8,128)(2,1)}, bf16[5120,128]{1,0:T(8,128)(2,1)S(1)}, u32[]{:S(2)}, u32[]{:S(2)}) collective-permute-start(bf16[5120,128]{1,0:T(8,128)(2,1)} %collective-permute-done.4.refs_1_), channel_id=1, source_target_pairs={{8,16},{16,24},{9,17},{17,25},{10,18},{18,26},{11,19},{19,27},{12,... | collective-permute-start | bytes 3932168 | tf_op jit(solution)/shard_map/ppermute | solution.py:431
  47.1 32.1 %collective-permute-start.8 = (bf16[5120,128]{1,0:T(8,128)(2,1)S(1)}, bf16[5120,128]{1,0:T(8,128)(2,1)S(1)}, u32[]{:S(2)}, u32[]{:S(2)}) collective-permute-start(bf16[5120,128]{1,0:T(8,128)(2,1)S(1)} %collective-permute-done.5.refs_2_), channel_id=1, source_target_pairs={{8,0},{16,8},{9,1},{17,9},{10,2},{18,10},{11,3},{19,11},{12,4},{20... | collective-permute-start | bytes 3932168 | tf_op jit(solution)/shard_map/ppermute | solution.py:431
  67.4 35.4 %collective-permute-start.10 = (bf16[5120,128]{1,0:T(8,128)(2,1)S(1)}, bf16[5120,128]{1,0:T(8,128)(2,1)S(1)}, u32[]{:S(2)}, u32[]{:S(2)}) collective-permute-start(bf16[5120,128]{1,0:T(8,128)(2,1)S(1)} %collective-permute-done.7.refs_0_), channel_id=1, source_target_pairs={{16,24},{17,25},{18,26},{19,27},{20,28},{21,29},{22,30},{23,31}} | collective-permute-start | bytes 3932168 | tf_op jit(solution)/shard_map/ppermute | solution.py:431
  79.2 30.0 %collective-permute-start.11 = (bf16[5120,128]{1,0:T(8,128)(2,1)S(1)}, bf16[5120,128]{1,0:T(8,128)(2,1)S(1)}, u32[]{:S(2)}, u32[]{:S(2)}) collective-permute-start(bf16[5120,128]{1,0:T(8,128)(2,1)S(1)} %collective-permute-done.8.refs_1_), channel_id=1, source_target_pairs={{8,0},{9,1},{10,2},{11,3},{12,4},{13,5},{14,6},{15,7}} | collective-permute-start | bytes 3932168 | tf_op jit(solution)/shard_map/ppermute | solution.py:431
  112.7 11.8 %collective-permute-start.12 = (bf16[4,144,512]{2,1,0:T(8,128)(2,1)S(1)}, bf16[4,144,512]{2,1,0:T(8,128)(2,1)S(1)}, u32[]{:S(2)}, u32[]{:S(2)}) collective-permute-start(bf16[4,144,512]{2,1,0:T(8,128)(2,1)S(1)} %part_stage.3), channel_id=1, source_target_pairs={{0,4},{4,0},{1,5},{5,1},{2,6},{6,2},{3,7},{7,3},{8,12},{12,8},{9,1... | collective-permute-start | bytes 1769480 | tf_op jit(solution)/shard_map/ppermute | solution.py:411
  113.6 12.2 %slice-start = ((s8[5242880]{0:T(1024)(128)(4,1)}), s8[4194304]{0:T(1024)(128)(4,1)S(1)}, s32[]{:S(2)}) async-start(s8[5242880]{0:T(1024)(128)(4,1)} %bitcast.49), calls=%async_computation | async-start | bytes 8388608
  115.9 9.9 %slice-start.1 = ((s8[5242880]{0:T(1024)(128)(4,1)}), s8[1048576]{0:T(1024)(128)(4,1)S(1)}, s32[]{:S(2)}) async-start(s8[5242880]{0:T(1024)(128)(4,1)} %bitcast.49), calls=%async_computation.1 | async-start | bytes 2097152
  127.4 2.1 %collective-permute-start.13 = (bf16[64,2560]{1,0:T(8,128)(2,1)S(1)}, bf16[64,2560]{1,0:T(8,128)(2,1)S(1)}, u32[]{:S(2)}, u32[]{:S(2)}) collective-permute-start(bf16[64,2560]{1,0:T(8,128)(2,1)S(1)} %get-tuple-element.59), channel_id=1, source_target_pairs={{0,1},{1,0},{2,3},{3,2},{4,5},{5,4},{6,7},{7,6},{8,9},{9,8},{10,11... | collective-permute-start | bytes 983048 | tf_op jit(solution)/shard_map/ppermute | solution.py:406
  127.5 2.1 %collective-permute-start.14 = (bf16[64,2560]{1,0:T(8,128)(2,1)S(1)}, bf16[64,2560]{1,0:T(8,128)(2,1)S(1)}, u32[]{:S(2)}, u32[]{:S(2)}) collective-permute-start(bf16[64,2560]{1,0:T(8,128)(2,1)S(1)} %get-tuple-element.60), channel_id=1, source_target_pairs={{0,1},{1,0},{2,3},{3,2},{4,5},{5,4},{6,7},{7,6},{8,9},{9,8},{10,11... | collective-permute-start | bytes 983048 | tf_op jit(solution)/shard_map/ppermute | solution.py:406
  128.0 15.3 %collective-permute-start.15 = (bf16[4,144,512]{2,1,0:T(8,128)(2,1)S(1)}, bf16[4,144,512]{2,1,0:T(8,128)(2,1)S(1)}, u32[]{:S(2)}, u32[]{:S(2)}) collective-permute-start(bf16[4,144,512]{2,1,0:T(8,128)(2,1)S(1)} %part_stage.2), channel_id=1, source_target_pairs={{0,4},{4,0},{1,5},{5,1},{2,6},{6,2},{3,7},{7,3},{8,12},{12,8},{9,1... | collective-permute-start | bytes 1769480 | tf_op jit(solution)/shard_map/ppermute | solution.py:411
  129.7 18.6 %collective-permute-start.18 = (bf16[128,2560]{1,0:T(8,128)(2,1)S(1)}, bf16[128,2560]{1,0:T(8,128)(2,1)S(1)}, u32[]{:S(2)}, u32[]{:S(2)}) collective-permute-start(bf16[128,2560]{1,0:T(8,128)(2,1)S(1)} %fusion.2), channel_id=1, source_target_pairs={{0,2},{1,3},{2,0},{3,1},{4,6},{5,7},{6,4},{7,5},{8,10},{9,11},{10,... | collective-permute-start | bytes 1966088 | tf_op jit(solution)/shard_map/ppermute | solution.py:406
  146.1 1.7 %collective-permute-start.16 = (bf16[64,2560]{1,0:T(8,128)(2,1)S(1)}, bf16[64,2560]{1,0:T(8,128)(2,1)S(1)}, u32[]{:S(2)}, u32[]{:S(2)}) collective-permute-start(bf16[64,2560]{1,0:T(8,128)(2,1)S(1)} %get-tuple-element.57), channel_id=1, source_target_pairs={{0,1},{1,0},{2,3},{3,2},{4,5},{5,4},{6,7},{7,6},{8,9},{9,8},{10,11... | collective-permute-start | bytes 983048 | tf_op jit(solution)/shard_map/ppermute | solution.py:406
  146.2 2.1 %collective-permute-start.17 = (bf16[64,2560]{1,0:T(8,128)(2,1)S(1)}, bf16[64,2560]{1,0:T(8,128)(2,1)S(1)}, u32[]{:S(2)}, u32[]{:S(2)}) collective-permute-start(bf16[64,2560]{1,0:T(8,128)(2,1)S(1)} %get-tuple-element.58), channel_id=1, source_target_pairs={{0,1},{1,0},{2,3},{3,2},{4,5},{5,4},{6,7},{7,6},{8,9},{9,8},{10,11... | collective-permute-start | bytes 983048 | tf_op jit(solution)/shard_map/ppermute | solution.py:406

commit v4 on v3

--- a/solution.py
+++ b/solution.py
@@ -70,9 +70,20 @@
 
 
 def pack(kv_t, pooling):
-    blocks = kv_t.shape[1] // BLK
+    depth, tokens = kv_t.shape
+    blocks = tokens // BLK
+    part = NOTES
     return pl.pallas_call(
         pack_kernel,
+        grid=(blocks // part,),
+        in_specs=[
+            pl.BlockSpec((depth, part * BLK), lambda i: (0, i)),
+            pl.BlockSpec(pooling.shape, lambda i: (0, 0)),
+        ],
+        out_specs=(
+            pl.BlockSpec((part * ROWS, LANES), lambda i: (i, 0)),
+            pl.BlockSpec((part, EXT + DV), lambda i: (i, 0)),
+        ),
         out_shape=(
             jax.ShapeDtypeStruct((blocks * ROWS, LANES), BF),
             jax.ShapeDtypeStruct((blocks, EXT + DV), BF),
@@ -294,7 +305,7 @@
 
 def part_kernel(n_kv, unit, order_ref, list_ref, q_ref, *refs):
     kv_refs, refs = refs[:n_kv], refs[n_kv:]
-    state_in, acc_in, out_ref, acc_ref, key_ref, value_ref = refs
+    state_in, acc_in, out_ref, acc_ref, notes_ref, key_ref, value_ref = refs
     acc_ref[...] = acc_in[0]
     top, total = add_selected(
         unit,
@@ -308,19 +319,24 @@
         key_ref,
         value_ref,
     )
-    out_ref[0, :DV] = (acc_ref[...] / jnp.maximum(total, 1e-30)).astype(BF)
+    step, steps = pl.program_id(0), pl.num_programs(0)
+    at = pl.multiple_of(step * DV, DV)
+    out_ref[pl.ds(at, DV), :] = (acc_ref[...] / jnp.maximum(total, 1e-30)).astype(BF)
     rest = log_total(top, total)
-    terms = []
-    for _ in range(3):
-        terms.append(rest.astype(BF).astype(F32))
-        rest = rest - terms[-1]
-    terms.append(jnp.zeros((NOTES - len(terms), rest.shape[1]), F32))
-    out_ref[0, DV:] = jnp.concatenate(terms, axis=0).astype(BF)
+    row = lax.broadcasted_iota(jnp.int32, notes_ref.shape, 0)
+    notes = jnp.where(step == 0, 0.0, notes_ref[...])
+    for term in range(3):
+        value = rest.astype(BF).astype(F32)
+        notes = jnp.where(row == term * steps + step, value, notes)
+        rest = rest - value
+    notes_ref[...] = notes
+    out_ref[out_ref.shape[0] - notes.shape[0] :, :] = notes.astype(BF)
 
 
 def part_stage(unit, order, lists, wide, kvs, state):
     _, lanes, _ = wide.shape
     (steps,) = order.shape
+    notes = -(-3 * steps // NOTES) * NOTES
     at = lambda i, order, *_: (order[i], 0, 0)
     return pl.pallas_call(
         functools.partial(part_kernel, len(kvs), unit),
@@ -330,10 +346,11 @@
             in_specs=[pl.BlockSpec((1, lanes, EXT), at)]
             + [whole_spec(kv) for kv in kvs]
             + [pl.BlockSpec((1, 2, lanes), at), pl.BlockSpec((1, DV, lanes), at)],
-            out_specs=pl.BlockSpec((1, DV + NOTES, lanes), lambda i, *_: (i, 0, 0)),
-            scratch_shapes=[pltpu.VMEM((DV, lanes), F32)] + scratch(unit),
-        ),
-        out_shape=jax.ShapeDtypeStruct((steps, DV + NOTES, lanes), BF),
+            out_specs=pl.BlockSpec((steps * DV + notes, lanes), lambda i, *_: (0, 0)),
+            scratch_shapes=[pltpu.VMEM((DV, lanes), F32), pltpu.VMEM((notes, lanes), F32)]
+            + scratch(unit),
+        ),
+        out_shape=jax.ShapeDtypeStruct((steps * DV + notes, lanes), BF),
         compiler_params=params(),
         cost_estimate=cost(4),
         name="part_stage",
@@ -344,15 +361,19 @@
     part_refs, out_ref = refs[:-1], refs[-1]
     total = state_ref[0, 1:2]
     logs = [log_total(state_ref[0, 0:1], total)]
+    step, steps = pl.program_id(0), pl.num_programs(0)
+    at = pl.multiple_of(step * DV, DV)
     for part_ref in part_refs:
-        notes = part_ref[0, DV:].astype(F32)
-        logs.append(notes[0:1] + notes[1:2] + notes[2:3])
+        notes = part_ref[part_ref.shape[0] // DV * DV :, :].astype(F32)
+        row = lax.broadcasted_iota(jnp.int32, notes.shape, 0)
+        here = functools.reduce(jnp.logical_or, [row == term * steps + step for term in range(3)])
+        logs.append(jnp.sum(jnp.where(here, notes, 0.0), axis=0, keepdims=True))
     peak = functools.reduce(jnp.maximum, logs)
     shares = [jnp.exp(log - peak) for log in logs]
     gate = gate_ref[0, 1:2] / functools.reduce(jnp.add, shares)
     out = near_ref[0] + acc_ref[0] * (gate * shares[0] / jnp.maximum(total, 1e-30))
     for share, part_ref in zip(shares[1:], part_refs):
-        out = out + part_ref[0, :DV].astype(F32) * (gate * share)
+        out = out + part_ref[pl.ds(at, DV), :].astype(F32) * (gate * share)
     for head in range(0, HQ, 2):
         pair = out[:, head * BLK : (head + 2) * BLK].T.astype(BF)
         out_ref[:, head * DV : (head + 1) * DV] = pair[:BLK]
@@ -374,7 +395,7 @@
                 pl.BlockSpec((1, DV, lanes), at),
                 pl.BlockSpec((1, 3, lanes), at),
             ]
-            + [pl.BlockSpec((1, DV + NOTES, lanes), lambda i, order: (i, 0, 0)) for _ in others],
+            + [pl.BlockSpec(other.shape, lambda i, order: (0, 0)) for other in others],
             out_specs=pl.BlockSpec((BLK, HQ * DV), lambda i, order: (i, 0)),
         ),
         out_shape=jax.ShapeDtypeStruct((steps * BLK, HQ * DV), BF),

time: 150 us -> 147 us (0.980)
  waiting for transfers between devices: 54.8 us -> 51.1 us
  starting transfers between devices: 26.3 us -> 27.8 us
    ppermute x4, waiting for transfers between devices: 16.2 us -> 12.4 us  [shift(): lax.ppermute(value, axis, [(i, (i + steps) % count) for i in range(count)])]
  transfers between devices with their start and end apart: 19 -> 19, of which waited for: 10 -> 11; matrix products, arithmetic and copies ran while one was open for 2% -> 2% of each run, Pallas kernels for 34% -> 35%
where the time goes in v4:
time: 147 us
  Pallas kernels  58.4 us (40%)
  waiting for transfers between devices  51.1 us (35%)
  starting transfers between devices  27.8 us (19%)
  matrix products  3.07 us (2%)
  local copies, waits for them, and re-layouts  2.61 us (2%)
  other arithmetic  2.58 us (2%)
    pallas_call x5, Pallas kernels, stage(): pl.pallas_call(functools.partial(stage_kernel, first, len(kvs), unit), gr...  33.8 us
    ppermute x8, waiting for transfers between devices, swap(): lax.ppermute(value, axis, [(i, i ^ bit) for i in range(lax.axis_size(axis...  21.7 us
    ppermute x6, waiting for transfers between devices, spread(): held[side] = lax.ppermute(held[side], axis, pairs)  17 us
    ppermute x4, waiting for transfers between devices, shift(): lax.ppermute(value, axis, [(i, (i + steps) % count) for i in range(count)])  12.4 us
    pallas_call x1, Pallas kernels, near_parts(): pl.pallas_call(near_kernel, grid_spec=pltpu.PrefetchScalarGridSpec(num_sc...  11.7 us
    ppermute x6, starting transfers between devices, spread(): held[side] = lax.ppermute(held[side], axis, pairs)  11.3 us
    ppermute x8, starting transfers between devices, swap(): lax.ppermute(value, axis, [(i, i ^ bit) for i in range(lax.axis_size(axis...  7.97 us
    ppermute x4, starting transfers between devices, shift(): lax.ppermute(value, axis, [(i, (i + steps) % count) for i in range(count)])  5.86 us
  transfers between devices with their start and end apart: 19, of which 11 were waited for; matrix products, arithmetic and copies ran while one was open for 2% of the time, Pallas kernels for 35%

profile of v4, /device:TPU:0, one launch (start us, length us, event | category | flops | bytes accessed | tf_op | source)
XLA Modules:
  0.0 146.7 jit_solution(10043763886618539807)
XLA Ops:
  0.0 1.3 copy-done.1
  1.3 0.7 copy-done.3
  2.0 2.7 %pack.1 = (bf16[5120,128]{1,0:T(8,128)(2,1)}, bf16[32,384]{1,0:T(8,128)(2,1)S(1)}) custom-call(bf16[320,2048]{1,0:T(8,128)(2,1)S(1)} %bitcast.46, f32[2,64]{1,0:T(2,128)S(1)} %copy-done.3), custom_call_target="tpu_custom_call" | custom-call | flops 5000000000 | tf_op jit(solution)/shard_map/pack/pallas_call | solution.py:76
  4.7 6.0 %collective-permute-start.4 = (bf16[5120,128]{1,0:T(8,128)(2,1)}, bf16[5120,128]{1,0:T(8,128)(2,1)}, u32[]{:S(2)}, u32[]{:S(2)}) collective-permute-start(bf16[5120,128]{1,0:T(8,128)(2,1)} %get-tuple-element.29.refs_0_), channel_id=1, source_target_pairs={{0,8},{8,16},{16,24},{1,9},{9,17},{17,25},{2,10},{10,18},{18,26},{... | collective-permute-start | bytes 3932168 | tf_op jit(solution)/shard_map/ppermute | solution.py:452
  10.7 1.3 collective-permute-start.5
  12.0 1.6 %collective-permute-start = (s32[8,16]{1,0:T(8,128)S(1)}, s32[8,16]{1,0:T(8,128)S(1)}, u32[]{:S(2)}, u32[]{:S(2)}) collective-permute-start(s32[8,16]{1,0:T(8,128)S(1)} %bitcast.51), channel_id=1, source_target_pairs={{0,4},{4,0},{1,5},{5,1},{2,6},{6,2},{3,7},{7,3},{8,12},{12,8},{9,1... | collective-permute-start | bytes 1544 | tf_op jit(solution)/shard_map/ppermute | solution.py:432
  13.6 0.5 collective-permute-start.1
  14.8 0.1 div.39
  15.0 0.1 reshape.525
  15.1 0.1 pad_add_fusion.5.order_ref
  15.2 0.1 pad_add_fusion.4.order_ref
  15.3 0.4 collective-permute-done
  15.7 0.1 convert_reduce_fusion.3
  15.9 0.2 select_add_fusion
  16.0 0.2 convert_reduce_fusion
  16.3 0.1 copy.30
  16.3 0.1 copy.29
  16.4 0.1 copy.26
  16.5 0.2 select_reduce_fusion
  16.7 0.1 fusion.11
  16.8 0.1 fusion.12
  16.9 0.1 select_reduce_fusion.2
  17.0 0.1 pad_add_fusion.1
  17.1 0.3 collective-permute-done.1
  17.4 2.6 %collective-permute-start.3 = (bf16[64,384]{1,0:T(8,128)(2,1)S(1)}, bf16[64,384]{1,0:T(8,128)(2,1)S(1)}, u32[]{:S(2)}, u32[]{:S(2)}) collective-permute-start(bf16[64,384]{1,0:T(8,128)(2,1)S(1)} %constant_dynamic-update-slice_fusion), channel_id=1, source_target_pairs={{0,8},{8,0},{16,24},{24,16},{1,9},{9,1},{17,25},{25,17},{2,10},{10... | collective-permute-start | bytes 147464 | tf_op jit(solution)/shard_map/ppermute | solution.py:427
  20.0 1.3 collective-permute-start.9
  21.3 1.0 wide_queries.2.q_ref
  22.3 2.7 %collective-permute-start.2 = (bf16[320,512]{1,0:T(8,128)(2,1)S(1)}, bf16[320,512]{1,0:T(8,128)(2,1)S(1)}, u32[]{:S(2)}, u32[]{:S(2)}) collective-permute-start(bf16[320,512]{1,0:T(8,128)(2,1)S(1)} %bitcast.47), channel_id=1, source_target_pairs={{0,4},{1,5},{2,6},{3,7},{8,12},{9,13},{10,14},{11,15},{16,20},{17,... | collective-permute-start | bytes 983048 | tf_op jit(solution)/shard_map/ppermute | solution.py:474
  25.0 19.1 %collective-permute-done.3 = bf16[64,384]{1,0:T(8,128)(2,1)S(1)} collective-permute-done((bf16[64,384]{1,0:T(8,128)(2,1)S(1)}, bf16[64,384]{1,0:T(8,128)(2,1)S(1)}, u32[]{:S(2)}, u32[]{:S(2)}) %collective-permute-start.3) | collective-permute-done | bytes 49184 | tf_op jit(solution)/shard_map/ppermute | solution.py:427
  44.1 1.6 %collective-permute-start.6 = (bf16[128,384]{1,0:T(8,128)(2,1)S(1)}, bf16[128,384]{1,0:T(8,128)(2,1)S(1)}, u32[]{:S(2)}, u32[]{:S(2)}) collective-permute-start(bf16[128,384]{1,0:T(8,128)(2,1)S(1)} %constant_dynamic-update-slice_fusion.2), channel_id=1, source_target_pairs={{0,16},{8,24},{16,0},{24,8},{1,17},{9,25},{17,1},{25,9},{2,18},{10... | collective-permute-start | bytes 294920 | tf_op jit(solution)/shard_map/ppermute | solution.py:427
  45.7 0.7 collective-permute-start.7
  46.5 1.3 collective-permute-start.8
  47.8 10.0 %stage.5 = (f32[8,2,512]{2,1,0:T(2,128)S(1)}, f32[8,128,512]{2,1,0:T(8,128)S(1)}) custom-call(s32[8,17]{1,0:T(8,128)S(1)} %get-tuple-element.62.list_ref, bf16[8,512,256]{2,1,0:T(8,128)(2,1)S(1)} %wide_queries.2.q_ref, bf16[5120,128]{1,0:T(8,128)(2,1)} %get-tuple-element.29.refs_0_, bf16[5120,128]{1,0:T(8,128)(2,1)} %collective-permute-done.4.refs_1_, ...), custom_call_target="tpu_custom_call" | custom-call | flops 8999999488 | tf_op jit(solution)/shard_map/stage/pallas_call | solution.py:282
  57.8 1.0 wide_queries.3.q_ref
  58.8 10.6 %stage.7 = (f32[8,2,512]{2,1,0:T(2,128)S(1)}, f32[8,128,512]{2,1,0:T(8,128)S(1)}) custom-call(s32[8,17]{1,0:T(8,128)S(1)} %get-tuple-element.61.list_ref, bf16[8,512,256]{2,1,0:T(8,128)(2,1)S(1)} %wide_queries.3.q_ref, bf16[5120,128]{1,0:T(8,128)(2,1)} %get-tuple-element.29.refs_0_, bf16[5120,128]{1,0:T(8,128)(2,1)} %collective-permute-done.4.refs_1_, ...), custom_call_target="tpu_custom_call" | custom-call | flops 8999999488 | tf_op jit(solution)/shard_map/stage/pallas_call | solution.py:282
  69.4 0.7 collective-permute-start.10
  70.1 8.4 %collective-permute-done.8.refs_1_ = bf16[5120,128]{1,0:T(8,128)(2,1)S(1)} collective-permute-done((bf16[5120,128]{1,0:T(8,128)(2,1)S(1)}, bf16[5120,128]{1,0:T(8,128)(2,1)S(1)}, u32[]{:S(2)}, u32[]{:S(2)}) %collective-permute-start.8) | collective-permute-done | bytes 1310752 | tf_op jit(solution)/shard_map/ppermute | solution.py:452
  78.6 1.3 collective-permute-start.11
  79.9 4.8 %stage.8 = (f32[8,2,512]{2,1,0:T(2,128)S(1)}, f32[8,128,512]{2,1,0:T(8,128)S(1)}) custom-call(s32[8,17]{1,0:T(8,128)S(1)} %get-tuple-element.63.list_ref, bf16[8,512,256]{2,1,0:T(8,128)(2,1)S(1)} %wide_queries.3.q_ref, bf16[5120,128]{1,0:T(8,128)(2,1)S(1)} %collective-permute-done.7.refs_0_, ...), custom_call_target="tpu_custom_call", output_to_operand_aliasing={{0}: (4, {}), {1}: (5, {})} | custom-call | flops 8999999488 | tf_op jit(solution)/shard_map/stage/pallas_call | solution.py:282
  84.7 3.5 %stage.6 = (f32[8,2,512]{2,1,0:T(2,128)S(1)}, f32[8,128,512]{2,1,0:T(8,128)S(1)}) custom-call(s32[8,17]{1,0:T(8,128)S(1)} %get-tuple-element.64.list_ref, bf16[8,512,256]{2,1,0:T(8,128)(2,1)S(1)} %wide_queries.2.q_ref, bf16[5120,128]{1,0:T(8,128)(2,1)S(1)} %collective-permute-done.7.refs_0_, ...), custom_call_target="tpu_custom_call", output_to_operand_aliasing={{0}: (4, {}), {1}: (5, {})} | custom-call | flops 8999999488 | tf_op jit(solution)/shard_map/stage/pallas_call | solution.py:282
  88.3 11.7 %near.1.near_ref = f32[8,128,512]{2,1,0:T(8,128)S(1)} custom-call(s32[1]{0:T(128)} %bitcast.4.begin_ref, bf16[8,512,256]{2,1,0:T(8,128)(2,1)S(1)} %wide_queries.2.q_ref, bf16[320,512]{1,0:T(8,128)(2,1)S(1)} %collective-permute-done.2.far_ref, bf16[320,512]{1,0:T(8,128)(2,1)S(1)} %bitcast.48, bf16[256,384]{1,0:T(8,128)(2,1)S(1)} %pad_maximum_fusion.comp_ref, ...), custom_call_target="tpu_custom_call" | custom-call | flops 14000000000 | tf_op jit(solution)/shard_map/near/pallas_call | solution.py:179
  100.0 8.6 %collective-permute-done.11.refs_1_ = bf16[5120,128]{1,0:T(8,128)(2,1)S(1)} collective-permute-done((bf16[5120,128]{1,0:T(8,128)(2,1)S(1)}, bf16[5120,128]{1,0:T(8,128)(2,1)S(1)}, u32[]{:S(2)}, u32[]{:S(2)}) %collective-permute-start.11) | collective-permute-done | bytes 1310752 | tf_op jit(solution)/shard_map/ppermute | solution.py:452
  108.6 2.9 %part_stage.3 = bf16[528,512]{1,0:T(8,128)(2,1)S(1)} custom-call(s32[4]{0:T(128)S(1)} %pad_add_fusion.5.order_ref, s32[8,17]{1,0:T(8,128)S(1)} %get-tuple-element.68.list_ref, bf16[8,512,256]{2,1,0:T(8,128)(2,1)S(1)} %wide_queries.3.q_ref, bf16[5120,128]{1,0:T(8,128)(2,1)S(1)} %collective-permute-done.10.refs_0_, ...), custom_call_target="tpu_custom_call" | custom-call | flops 4000000000 | tf_op jit(solution)/shard_map/part_stage/pallas_call | solution.py:341
  111.5 2.2 %collective-permute-start.12 = (bf16[528,512]{1,0:T(8,128)(2,1)S(1)}, bf16[528,512]{1,0:T(8,128)(2,1)S(1)}, u32[]{:S(2)}, u32[]{:S(2)}) collective-permute-start(bf16[528,512]{1,0:T(8,128)(2,1)S(1)} %part_stage.3), channel_id=1, source_target_pairs={{0,4},{4,0},{1,5},{5,1},{2,6},{6,2},{3,7},{7,3},{8,12},{12,8},{9,1... | collective-permute-start | bytes 1622024 | tf_op jit(solution)/shard_map/ppermute | solution.py:432
  113.7 2.9 %part_stage.2 = bf16[528,512]{1,0:T(8,128)(2,1)S(1)} custom-call(s32[4]{0:T(128)S(1)} %pad_add_fusion.4.order_ref, s32[8,17]{1,0:T(8,128)S(1)} %get-tuple-element.68.list_ref, bf16[8,512,256]{2,1,0:T(8,128)(2,1)S(1)} %wide_queries.3.q_ref, bf16[5120,128]{1,0:T(8,128)(2,1)S(1)} %collective-permute-done.10.refs_0_, ...), custom_call_target="tpu_custom_call" | custom-call | flops 4000000000 | tf_op jit(solution)/shard_map/part_stage/pallas_call | solution.py:341
  116.6 4.8 %stage.9 = (f32[8,2,512]{2,1,0:T(2,128)S(1)}, f32[8,128,512]{2,1,0:T(8,128)S(1)}) custom-call(s32[8,17]{1,0:T(8,128)S(1)} %get-tuple-element.43.list_ref, bf16[8,512,256]{2,1,0:T(8,128)(2,1)S(1)} %wide_queries.2.q_ref, bf16[5120,128]{1,0:T(8,128)(2,1)S(1)} %collective-permute-done.10.refs_0_, ...), custom_call_target="tpu_custom_call", output_to_operand_aliasing={{0}: (4, {}), {1}: (5, {})} | custom-call | flops 8999999488 | tf_op jit(solution)/shard_map/stage/pallas_call | solution.py:282
  121.4 1.5 %collective-permute-done.12.refs_0_ = bf16[528,512]{1,0:T(8,128)(2,1)S(1)} collective-permute-done((bf16[528,512]{1,0:T(8,128)(2,1)S(1)}, bf16[528,512]{1,0:T(8,128)(2,1)S(1)}, u32[]{:S(2)}, u32[]{:S(2)}) %collective-permute-start.12) | collective-permute-done | bytes 540704 | tf_op jit(solution)/shard_map/ppermute | solution.py:432
  122.9 1.2 last_stage.2
  124.2 1.5 %fusion.15 = (bf16[256,2560]{1,0:T(8,128)(2,1)S(1)}, f32[256,2560]{1,0:T(8,128)S(1)}) fusion(bf16[256,1024]{1,0:T(8,128)(2,1)S(1)} %last_stage.2, bf16[1024,2560]{1,0:T(8,128)(2,1)S(1)} %bitcast.50), kind=kOutput, calls=%fused_computation.74 | convolution fusion | flops 1342832640 | bytes 9699328 | tf_op jit(solution)/shard_map/dot_general | solution.py:528
  125.8 0.1 collective-permute-start.13
  125.8 0.5 collective-permute-start.14
  126.3 0.8 collective-permute-start.15
  127.2 0.3 collective-permute-done.13
  127.4 0.5 collective-permute-done.14
  127.9 0.1 fusion.2
  128.1 2.0 %collective-permute-start.18 = (bf16[128,2560]{1,0:T(8,128)(2,1)S(1)}, bf16[128,2560]{1,0:T(8,128)(2,1)S(1)}, u32[]{:S(2)}, u32[]{:S(2)}) collective-permute-start(bf16[128,2560]{1,0:T(8,128)(2,1)S(1)} %fusion.2), channel_id=1, source_target_pairs={{0,2},{1,3},{2,0},{3,1},{4,6},{5,7},{6,4},{7,5},{8,10},{9,11},{10,... | collective-permute-start | bytes 1966088 | tf_op jit(solution)/shard_map/ppermute | solution.py:427
  130.1 10.5 %collective-permute-done.15.refs_0_ = bf16[528,512]{1,0:T(8,128)(2,1)S(1)} collective-permute-done((bf16[528,512]{1,0:T(8,128)(2,1)S(1)}, bf16[528,512]{1,0:T(8,128)(2,1)S(1)}, u32[]{:S(2)}, u32[]{:S(2)}) %collective-permute-start.15) | collective-permute-done | bytes 540704 | tf_op jit(solution)/shard_map/ppermute | solution.py:432
  140.6 1.2 last_stage.3
  141.8 1.5 %fusion.16 = (bf16[256,2560]{1,0:T(8,128)(2,1)S(1)}, f32[256,2560]{1,0:T(8,128)S(1)}) fusion(bf16[256,1024]{1,0:T(8,128)(2,1)S(1)} %last_stage.3, bf16[1024,2560]{1,0:T(8,128)(2,1)S(1)} %bitcast.50), kind=kOutput, calls=%fused_computation.75 | convolution fusion | flops 1342832640 | bytes 9699328 | tf_op jit(solution)/shard_map/dot_general | solution.py:528
  143.4 0.1 collective-permute-start.16
  143.5 0.5 collective-permute-start.17
  144.0 1.1 collective-permute-done.16
  145.1 0.5 collective-permute-done.17
  145.6 1.1 fusion.3
  (41 shorter events, 0.3 us)
Async XLA Ops:
  0.0 1.3 copy-start.1
  1.3 0.7 copy-start.3
  2.0 10.0 %copy-start.5 = (s32[1,8,1,16]{3,2,1,0:T(1,128)S(1)}, s32[1,8,1,16]{3,2,1,0:T(1,128)}, u32[]{:S(2)}) copy-start(s32[1,8,1,16]{3,2,1,0:T(1,128)} %param.13) | copy-start | bytes 1540
  2.0 12.8 %copy-start.4 = (f32[1,512,1,24]{1,3,2,0:T(8,128)S(1)}, f32[1,512,1,24]{1,3,2,0:T(8,128)}, u32[]{:S(2)}) copy-start(f32[1,512,1,24]{1,3,2,0:T(8,128)} %param.12) | copy-start | bytes 147460
  2.0 18.0 %copy-start = (bf16[1,512,1,1536]{3,1,2,0:T(8,128)(2,1)S(1)}, bf16[1,512,1,1536]{3,1,2,0:T(8,128)(2,1)}, u32[]{:S(2)}) copy-start(bf16[1,512,1,1536]{3,1,2,0:T(8,128)(2,1)} %param.8) | copy-start | bytes 4718596
  4.7 39.4 %collective-permute-start.4 = (bf16[5120,128]{1,0:T(8,128)(2,1)}, bf16[5120,128]{1,0:T(8,128)(2,1)}, u32[]{:S(2)}, u32[]{:S(2)}) collective-permute-start(bf16[5120,128]{1,0:T(8,128)(2,1)} %get-tuple-element.29.refs_0_), channel_id=1, source_target_pairs={{0,8},{8,16},{16,24},{1,9},{9,17},{17,25},{2,10},{10,18},{18,26},{... | collective-permute-start | bytes 3932168 | tf_op jit(solution)/shard_map/ppermute | solution.py:452
  10.7 33.4 %collective-permute-start.5 = (bf16[5120,128]{1,0:T(8,128)(2,1)}, bf16[5120,128]{1,0:T(8,128)(2,1)S(1)}, u32[]{:S(2)}, u32[]{:S(2)}) collective-permute-start(bf16[5120,128]{1,0:T(8,128)(2,1)} %get-tuple-element.29.refs_0_), channel_id=1, source_target_pairs={{8,0},{16,8},{24,16},{9,1},{17,9},{25,17},{10,2},{18,10},{26,18},{... | collective-permute-start | bytes 3932168 | tf_op jit(solution)/shard_map/ppermute | solution.py:452
  12.0 3.7 %collective-permute-start = (s32[8,16]{1,0:T(8,128)S(1)}, s32[8,16]{1,0:T(8,128)S(1)}, u32[]{:S(2)}, u32[]{:S(2)}) collective-permute-start(s32[8,16]{1,0:T(8,128)S(1)} %bitcast.51), channel_id=1, source_target_pairs={{0,4},{4,0},{1,5},{5,1},{2,6},{6,2},{3,7},{7,3},{8,12},{12,8},{9,1... | collective-permute-start | bytes 1544 | tf_op jit(solution)/shard_map/ppermute | solution.py:432
  13.6 3.8 %collective-permute-start.1 = (bf16[32,384]{1,0:T(8,128)(2,1)S(1)}, bf16[32,384]{1,0:T(8,128)(2,1)S(1)}, u32[]{:S(2)}, u32[]{:S(2)}) collective-permute-start(bf16[32,384]{1,0:T(8,128)(2,1)S(1)} %get-tuple-element.26), channel_id=1, source_target_pairs={{0,4},{4,0},{1,5},{5,1},{2,6},{6,2},{3,7},{7,3},{8,12},{12,8},{9,1... | collective-permute-start | bytes 73736 | tf_op jit(solution)/shard_map/ppermute | solution.py:427
  17.4 26.7 %collective-permute-start.3 = (bf16[64,384]{1,0:T(8,128)(2,1)S(1)}, bf16[64,384]{1,0:T(8,128)(2,1)S(1)}, u32[]{:S(2)}, u32[]{:S(2)}) collective-permute-start(bf16[64,384]{1,0:T(8,128)(2,1)S(1)} %constant_dynamic-update-slice_fusion), channel_id=1, source_target_pairs={{0,8},{8,0},{16,24},{24,16},{1,9},{9,1},{17,25},{25,17},{2,10},{10... | collective-permute-start | bytes 147464 | tf_op jit(solution)/shard_map/ppermute | solution.py:427
  20.0 2.2 %copy-start.2 = (bf16[1,512,1,320]{1,3,2,0:T(8,128)(2,1)S(1)}, bf16[1,512,1,320]{1,3,2,0:T(8,128)(2,1)}, u32[]{:S(2)}) copy-start(bf16[1,512,1,320]{1,3,2,0:T(8,128)(2,1)} %param.9) | copy-start | bytes 983044
  20.0 37.7 %collective-permute-start.9 = (bf16[512,1536]{1,0:T(8,128)(2,1)S(1)}, bf16[512,1536]{1,0:T(8,128)(2,1)S(1)}, u32[]{:S(2)}, u32[]{:S(2)}) collective-permute-start(bf16[512,1536]{1,0:T(8,128)(2,1)S(1)} %bitcast.44), channel_id=1, source_target_pairs={{0,4},{4,0},{1,5},{5,1},{2,6},{6,2},{3,7},{7,3},{8,12},{12,8},{9,1... | collective-permute-start | bytes 4718600 | tf_op jit(solution)/shard_map/ppermute | solution.py:432
  22.3 66.0 %collective-permute-start.2 = (bf16[320,512]{1,0:T(8,128)(2,1)S(1)}, bf16[320,512]{1,0:T(8,128)(2,1)S(1)}, u32[]{:S(2)}, u32[]{:S(2)}) collective-permute-start(bf16[320,512]{1,0:T(8,128)(2,1)S(1)} %bitcast.47), channel_id=1, source_target_pairs={{0,4},{1,5},{2,6},{3,7},{8,12},{9,13},{10,14},{11,15},{16,20},{17,... | collective-permute-start | bytes 983048 | tf_op jit(solution)/shard_map/ppermute | solution.py:474
  44.1 44.1 %collective-permute-start.6 = (bf16[128,384]{1,0:T(8,128)(2,1)S(1)}, bf16[128,384]{1,0:T(8,128)(2,1)S(1)}, u32[]{:S(2)}, u32[]{:S(2)}) collective-permute-start(bf16[128,384]{1,0:T(8,128)(2,1)S(1)} %constant_dynamic-update-slice_fusion.2), channel_id=1, source_target_pairs={{0,16},{8,24},{16,0},{24,8},{1,17},{9,25},{17,1},{25,9},{2,18},{10... | collective-permute-start | bytes 294920 | tf_op jit(solution)/shard_map/ppermute | solution.py:427
  45.7 23.6 %collective-permute-start.7 = (bf16[5120,128]{1,0:T(8,128)(2,1)}, bf16[5120,128]{1,0:T(8,128)(2,1)S(1)}, u32[]{:S(2)}, u32[]{:S(2)}) collective-permute-start(bf16[5120,128]{1,0:T(8,128)(2,1)} %collective-permute-done.4.refs_1_), channel_id=1, source_target_pairs={{8,16},{16,24},{9,17},{17,25},{10,18},{18,26},{11,19},{19,27},{12,... | collective-permute-start | bytes 3932168 | tf_op jit(solution)/shard_map/ppermute | solution.py:452
  46.5 32.1 %collective-permute-start.8 = (bf16[5120,128]{1,0:T(8,128)(2,1)S(1)}, bf16[5120,128]{1,0:T(8,128)(2,1)S(1)}, u32[]{:S(2)}, u32[]{:S(2)}) collective-permute-start(bf16[5120,128]{1,0:T(8,128)(2,1)S(1)} %collective-permute-done.5.refs_2_), channel_id=1, source_target_pairs={{8,0},{16,8},{9,1},{17,9},{10,2},{18,10},{11,3},{19,11},{12,4},{20... | collective-permute-start | bytes 3932168 | tf_op jit(solution)/shard_map/ppermute | solution.py:452
  69.4 30.6 %collective-permute-start.10 = (bf16[5120,128]{1,0:T(8,128)(2,1)S(1)}, bf16[5120,128]{1,0:T(8,128)(2,1)S(1)}, u32[]{:S(2)}, u32[]{:S(2)}) collective-permute-start(bf16[5120,128]{1,0:T(8,128)(2,1)S(1)} %collective-permute-done.7.refs_0_), channel_id=1, source_target_pairs={{16,24},{17,25},{18,26},{19,27},{20,28},{21,29},{22,30},{23,31}} | collective-permute-start | bytes 3932168 | tf_op jit(solution)/shard_map/ppermute | solution.py:452
  78.6 30.0 %collective-permute-start.11 = (bf16[5120,128]{1,0:T(8,128)(2,1)S(1)}, bf16[5120,128]{1,0:T(8,128)(2,1)S(1)}, u32[]{:S(2)}, u32[]{:S(2)}) collective-permute-start(bf16[5120,128]{1,0:T(8,128)(2,1)S(1)} %collective-permute-done.8.refs_1_), channel_id=1, source_target_pairs={{8,0},{9,1},{10,2},{11,3},{12,4},{13,5},{14,6},{15,7}} | collective-permute-start | bytes 3932168 | tf_op jit(solution)/shard_map/ppermute | solution.py:452
  111.5 11.4 %collective-permute-start.12 = (bf16[528,512]{1,0:T(8,128)(2,1)S(1)}, bf16[528,512]{1,0:T(8,128)(2,1)S(1)}, u32[]{:S(2)}, u32[]{:S(2)}) collective-permute-start(bf16[528,512]{1,0:T(8,128)(2,1)S(1)} %part_stage.3), channel_id=1, source_target_pairs={{0,4},{4,0},{1,5},{5,1},{2,6},{6,2},{3,7},{7,3},{8,12},{12,8},{9,1... | collective-permute-start | bytes 1622024 | tf_op jit(solution)/shard_map/ppermute | solution.py:432
  113.7 10.5 %slice-start = ((s8[5242880]{0:T(1024)(128)(4,1)}), s8[4194304]{0:T(1024)(128)(4,1)S(1)}, s32[]{:S(2)}) async-start(s8[5242880]{0:T(1024)(128)(4,1)} %bitcast.49), calls=%async_computation | async-start | bytes 8388608
  116.6 7.6 %slice-start.1 = ((s8[5242880]{0:T(1024)(128)(4,1)}), s8[1048576]{0:T(1024)(128)(4,1)S(1)}, s32[]{:S(2)}) async-start(s8[5242880]{0:T(1024)(128)(4,1)} %bitcast.49), calls=%async_computation.1 | async-start | bytes 2097152
  125.8 1.7 %collective-permute-start.13 = (bf16[64,2560]{1,0:T(8,128)(2,1)S(1)}, bf16[64,2560]{1,0:T(8,128)(2,1)S(1)}, u32[]{:S(2)}, u32[]{:S(2)}) collective-permute-start(bf16[64,2560]{1,0:T(8,128)(2,1)S(1)} %get-tuple-element.59), channel_id=1, source_target_pairs={{0,1},{1,0},{2,3},{3,2},{4,5},{5,4},{6,7},{7,6},{8,9},{9,8},{10,11... | collective-permute-start | bytes 983048 | tf_op jit(solution)/shard_map/ppermute | solution.py:427
  125.8 2.1 %collective-permute-start.14 = (bf16[64,2560]{1,0:T(8,128)(2,1)S(1)}, bf16[64,2560]{1,0:T(8,128)(2,1)S(1)}, u32[]{:S(2)}, u32[]{:S(2)}) collective-permute-start(bf16[64,2560]{1,0:T(8,128)(2,1)S(1)} %get-tuple-element.60), channel_id=1, source_target_pairs={{0,1},{1,0},{2,3},{3,2},{4,5},{5,4},{6,7},{7,6},{8,9},{9,8},{10,11... | collective-permute-start | bytes 983048 | tf_op jit(solution)/shard_map/ppermute | solution.py:427
  126.3 14.3 %collective-permute-start.15 = (bf16[528,512]{1,0:T(8,128)(2,1)S(1)}, bf16[528,512]{1,0:T(8,128)(2,1)S(1)}, u32[]{:S(2)}, u32[]{:S(2)}) collective-permute-start(bf16[528,512]{1,0:T(8,128)(2,1)S(1)} %part_stage.2), channel_id=1, source_target_pairs={{0,4},{4,0},{1,5},{5,1},{2,6},{6,2},{3,7},{7,3},{8,12},{12,8},{9,1... | collective-permute-start | bytes 1622024 | tf_op jit(solution)/shard_map/ppermute | solution.py:432
  128.1 17.5 %collective-permute-start.18 = (bf16[128,2560]{1,0:T(8,128)(2,1)S(1)}, bf16[128,2560]{1,0:T(8,128)(2,1)S(1)}, u32[]{:S(2)}, u32[]{:S(2)}) collective-permute-start(bf16[128,2560]{1,0:T(8,128)(2,1)S(1)} %fusion.2), channel_id=1, source_target_pairs={{0,2},{1,3},{2,0},{3,1},{4,6},{5,7},{6,4},{7,5},{8,10},{9,11},{10,... | collective-permute-start | bytes 1966088 | tf_op jit(solution)/shard_map/ppermute | solution.py:427
  143.4 1.7 %collective-permute-start.16 = (bf16[64,2560]{1,0:T(8,128)(2,1)S(1)}, bf16[64,2560]{1,0:T(8,128)(2,1)S(1)}, u32[]{:S(2)}, u32[]{:S(2)}) collective-permute-start(bf16[64,2560]{1,0:T(8,128)(2,1)S(1)} %get-tuple-element.57), channel_id=1, source_target_pairs={{0,1},{1,0},{2,3},{3,2},{4,5},{5,4},{6,7},{7,6},{8,9},{9,8},{10,11... | collective-permute-start | bytes 983048 | tf_op jit(solution)/shard_map/ppermute | solution.py:427
  143.5 2.1 %collective-permute-start.17 = (bf16[64,2560]{1,0:T(8,128)(2,1)S(1)}, bf16[64,2560]{1,0:T(8,128)(2,1)S(1)}, u32[]{:S(2)}, u32[]{:S(2)}) collective-permute-start(bf16[64,2560]{1,0:T(8,128)(2,1)S(1)} %get-tuple-element.58), channel_id=1, source_target_pairs={{0,1},{1,0},{2,3},{3,2},{4,5},{5,4},{6,7},{7,6},{8,9},{9,8},{10,11... | collective-permute-start | bytes 983048 | tf_op jit(solution)/shard_map/ppermute | solution.py:427

commit v5 on v4

--- a/solution.py
+++ b/solution.py
@@ -88,7 +88,7 @@
             jax.ShapeDtypeStruct((blocks * ROWS, LANES), BF),
             jax.ShapeDtypeStruct((blocks, EXT + DV), BF),
         ),
-        compiler_params=params(),
+        compiler_params=pltpu.CompilerParams(vmem_limit_bytes=2 * VMEM - 4 * 1024 * 1024),
         cost_estimate=cost(5),
         name="pack",
     )(kv_t, pooling)
@@ -439,7 +439,7 @@
     found = []
     for hop in range(1, max(reach) + 1):
         found.append([])
-        for side, sign in enumerate((1, -1)):
+        for side, sign in enumerate((-1, 1)):
             if hop > reach[side]:
                 continue
             pairs = []
@@ -500,8 +500,9 @@
     near = near_parts(begin.reshape(1), wides[0], far_t, own_t, comp, gates)
     states = [None] * ctx_count
     for level, table in zip(levels[:-1], lists[:-1]):
+        unit = UNIT * min(len(level) - 1, 2)
         for run in range(ctx_count):
-            states[run] = stage(UNIT, table[run], wides[run], [a for a, _ in level], states[run])
+            states[run] = stage(unit, table[run], wides[run], [a for a, _ in level], states[run])
     table = lax.optimization_barrier((lists[-1], near, states))[0]
     kvs = [a for a, _ in levels[-1]]
 

time: 147 us -> 145 us (0.986)
  Pallas kernels: 58.4 us -> 62.6 us
  waiting for transfers between devices: 51.1 us -> 47.9 us
    ppermute x6, waiting for transfers between devices: 17 us -> 14.3 us  [spread(): held[side] = lax.ppermute(held[side], axis, pairs)]
    pallas_call x5, Pallas kernels: 33.8 us -> 36.3 us  [stage(): pl.pallas_call(functools.partial(stage_kernel, first, len(kvs), unit), gr...]
    ppermute x8, waiting for transfers between devices: 21.7 us -> 19.6 us  [swap(): lax.ppermute(value, axis, [(i, i ^ bit) for i in range(lax.axis_size(axis...]
    ppermute x4, waiting for transfers between devices: 12.4 us -> 14.1 us  [shift(): lax.ppermute(value, axis, [(i, (i + steps) % count) for i in range(count)])]
  transfers between devices with their start and end apart: 19 -> 19, of which waited for: 11 -> 10; matrix products, arithmetic and copies ran while one was open for 2% -> 3% of each run, Pallas kernels for 35% -> 37%
where the time goes in v5:
time: 145 us
  Pallas kernels  62.6 us (43%)
  waiting for transfers between devices  47.9 us (33%)
  starting transfers between devices  26.4 us (18%)
  matrix products  3.04 us (2%)
  other arithmetic  2.53 us (2%)
    pallas_call x5, Pallas kernels, stage(): pl.pallas_call(functools.partial(stage_kernel, first, len(kvs), unit), gr...  36.3 us
    ppermute x8, waiting for transfers between devices, swap(): lax.ppermute(value, axis, [(i, i ^ bit) for i in range(lax.axis_size(axis...  19.6 us
    ppermute x6, waiting for transfers between devices, spread(): held[side] = lax.ppermute(held[side], axis, pairs)  14.3 us
    ppermute x4, waiting for transfers between devices, shift(): lax.ppermute(value, axis, [(i, (i + steps) % count) for i in range(count)])  14.1 us
    pallas_call x1, Pallas kernels, near_parts(): pl.pallas_call(near_kernel, grid_spec=pltpu.PrefetchScalarGridSpec(num_sc...  11.7 us
    ppermute x6, starting transfers between devices, spread(): held[side] = lax.ppermute(held[side], axis, pairs)  11.2 us
    ppermute x8, starting transfers between devices, swap(): lax.ppermute(value, axis, [(i, i ^ bit) for i in range(lax.axis_size(axis...  6.89 us
    pallas_call x2, Pallas kernels, part_stage(): pl.pallas_call(functools.partial(part_kernel, len(kvs), unit), grid_spec=...  6.38 us
  transfers between devices with their start and end apart: 19, of which 10 were waited for; matrix products, arithmetic and copies ran while one was open for 3% of the time, Pallas kernels for 37%

profile of v5, /device:TPU:0, one launch (start us, length us, event | category | flops | bytes accessed | tf_op | source)
XLA Modules:
  0.0 145.0 jit_solution(17323943520851167094)
XLA Ops:
  0.0 3.8 %pack.1 = (bf16[5120,128]{1,0:T(8,128)(2,1)}, bf16[32,384]{1,0:T(8,128)(2,1)}) custom-call(bf16[320,2048]{1,0:T(8,128)(2,1)} %bitcast.58, f32[2,64]{1,0:T(2,128)} %pool_ref.1), custom_call_target="tpu_custom_call" | custom-call | flops 5000000000 | tf_op jit(solution)/shard_map/pack/pallas_call | solution.py:76
  3.8 1.3 collective-permute-start.4
  5.1 5.6 %collective-permute-start.5 = (bf16[5120,128]{1,0:T(8,128)(2,1)}, bf16[5120,128]{1,0:T(8,128)(2,1)S(1)}, u32[]{:S(2)}, u32[]{:S(2)}) collective-permute-start(bf16[5120,128]{1,0:T(8,128)(2,1)} %get-tuple-element.29.refs_0_), channel_id=1, source_target_pairs={{0,8},{8,16},{16,24},{1,9},{9,17},{17,25},{2,10},{10,18},{18,26},{... | collective-permute-start | bytes 3932168 | tf_op jit(solution)/shard_map/ppermute | solution.py:452
  10.8 2.0 %collective-permute-start = (s32[8,16]{1,0:T(8,128)S(1)}, s32[8,16]{1,0:T(8,128)S(1)}, u32[]{:S(2)}, u32[]{:S(2)}) collective-permute-start(s32[8,16]{1,0:T(8,128)S(1)} %bitcast.50), channel_id=1, source_target_pairs={{0,4},{4,0},{1,5},{5,1},{2,6},{6,2},{3,7},{7,3},{8,12},{12,8},{9,1... | collective-permute-start | bytes 1544 | tf_op jit(solution)/shard_map/ppermute | solution.py:432
  12.8 0.1 collective-permute-start.1
  12.9 0.8 constant_dynamic-update-slice_fusion.1
  14.4 0.1 div.39
  14.5 0.1 reshape.525
  14.7 0.1 pad_add_fusion.5.order_ref
  14.7 0.1 pad_add_fusion.4.order_ref
  14.8 0.0 collective-permute-done
  14.8 0.2 convert_reduce_fusion.3
  15.0 0.2 select_add_fusion
  15.1 0.2 convert_reduce_fusion
  15.4 0.1 copy.30
  15.4 0.1 copy.29
  15.5 0.1 copy.26
  15.6 0.2 select_reduce_fusion
  15.8 0.1 fusion.11
  15.9 0.1 fusion.12
  16.0 0.1 select_reduce_fusion.2
  16.1 0.1 pad_add_fusion.1
  16.2 0.6 collective-permute-done.1
  16.8 1.5 %collective-permute-start.3 = (bf16[64,384]{1,0:T(8,128)(2,1)S(1)}, bf16[64,384]{1,0:T(8,128)(2,1)S(1)}, u32[]{:S(2)}, u32[]{:S(2)}) collective-permute-start(bf16[64,384]{1,0:T(8,128)(2,1)S(1)} %constant_dynamic-update-slice_fusion), channel_id=1, source_target_pairs={{0,8},{8,0},{16,24},{24,16},{1,9},{9,1},{17,25},{25,17},{2,10},{10... | collective-permute-start | bytes 147464 | tf_op jit(solution)/shard_map/ppermute | solution.py:427
  18.3 1.4 collective-permute-start.9
  19.7 1.0 wide_queries.2.q_ref
  20.7 2.6 %collective-permute-start.2 = (bf16[320,512]{1,0:T(8,128)(2,1)S(1)}, bf16[320,512]{1,0:T(8,128)(2,1)S(1)}, u32[]{:S(2)}, u32[]{:S(2)}) collective-permute-start(bf16[320,512]{1,0:T(8,128)(2,1)S(1)} %bitcast.46), channel_id=1, source_target_pairs={{0,4},{1,5},{2,6},{3,7},{8,12},{9,13},{10,14},{11,15},{16,20},{17,... | collective-permute-start | bytes 983048 | tf_op jit(solution)/shard_map/ppermute | solution.py:474
  23.3 16.7 %collective-permute-done.3 = bf16[64,384]{1,0:T(8,128)(2,1)S(1)} collective-permute-done((bf16[64,384]{1,0:T(8,128)(2,1)S(1)}, bf16[64,384]{1,0:T(8,128)(2,1)S(1)}, u32[]{:S(2)}, u32[]{:S(2)}) %collective-permute-start.3) | collective-permute-done | bytes 49184 | tf_op jit(solution)/shard_map/ppermute | solution.py:427
  40.0 3.9 %collective-permute-start.6 = (bf16[128,384]{1,0:T(8,128)(2,1)S(1)}, bf16[128,384]{1,0:T(8,128)(2,1)S(1)}, u32[]{:S(2)}, u32[]{:S(2)}) collective-permute-start(bf16[128,384]{1,0:T(8,128)(2,1)S(1)} %constant_dynamic-update-slice_fusion.2), channel_id=1, source_target_pairs={{0,16},{8,24},{16,0},{24,8},{1,17},{9,25},{17,1},{25,9},{2,18},{10... | collective-permute-start | bytes 294920 | tf_op jit(solution)/shard_map/ppermute | solution.py:427
  43.9 1.3 collective-permute-start.7
  45.2 0.7 collective-permute-start.8
  45.9 9.1 %stage.5 = (f32[8,2,512]{2,1,0:T(2,128)S(1)}, f32[8,128,512]{2,1,0:T(8,128)S(1)}) custom-call(s32[8,17]{1,0:T(8,128)S(1)} %get-tuple-element.62.list_ref, bf16[8,512,256]{2,1,0:T(8,128)(2,1)S(1)} %wide_queries.2.q_ref, bf16[5120,128]{1,0:T(8,128)(2,1)S(1)} %copy-done.1, bf16[5120,128]{1,0:T(8,128)(2,1)} %collective-permute-done.4.refs_1_, ...), custom_call_target="tpu_custom_call" | custom-call | flops 8999999488 | tf_op jit(solution)/shard_map/stage/pallas_call | solution.py:282
  55.1 1.0 wide_queries.3.q_ref
  56.1 12.1 %stage.7 = (f32[8,2,512]{2,1,0:T(2,128)S(1)}, f32[8,128,512]{2,1,0:T(8,128)S(1)}) custom-call(s32[8,17]{1,0:T(8,128)S(1)} %get-tuple-element.61.list_ref, bf16[8,512,256]{2,1,0:T(8,128)(2,1)S(1)} %wide_queries.3.q_ref, bf16[5120,128]{1,0:T(8,128)(2,1)S(1)} %copy-done.1, bf16[5120,128]{1,0:T(8,128)(2,1)} %collective-permute-done.4.refs_1_, ...), custom_call_target="tpu_custom_call" | custom-call | flops 8999999488 | tf_op jit(solution)/shard_map/stage/pallas_call | solution.py:282
  68.2 7.6 %collective-permute-done.7.refs_0_ = bf16[5120,128]{1,0:T(8,128)(2,1)S(1)} collective-permute-done((bf16[5120,128]{1,0:T(8,128)(2,1)}, bf16[5120,128]{1,0:T(8,128)(2,1)S(1)}, u32[]{:S(2)}, u32[]{:S(2)}) %collective-permute-start.7) | collective-permute-done | bytes 1310752 | tf_op jit(solution)/shard_map/ppermute | solution.py:452
  75.8 1.3 collective-permute-start.10
  77.1 0.9 collective-permute-start.11
  78.0 5.4 %stage.8 = (f32[8,2,512]{2,1,0:T(2,128)S(1)}, f32[8,128,512]{2,1,0:T(8,128)S(1)}) custom-call(s32[8,17]{1,0:T(8,128)S(1)} %get-tuple-element.63.list_ref, bf16[8,512,256]{2,1,0:T(8,128)(2,1)S(1)} %wide_queries.3.q_ref, bf16[5120,128]{1,0:T(8,128)(2,1)S(1)} %collective-permute-done.7.refs_0_, ...), custom_call_target="tpu_custom_call", output_to_operand_aliasing={{0}: (4, {}), {1}: (5, {})} | custom-call | flops 8999999488 | tf_op jit(solution)/shard_map/stage/pallas_call | solution.py:282
  83.5 4.2 %stage.6 = (f32[8,2,512]{2,1,0:T(2,128)S(1)}, f32[8,128,512]{2,1,0:T(8,128)S(1)}) custom-call(s32[8,17]{1,0:T(8,128)S(1)} %get-tuple-element.64.list_ref, bf16[8,512,256]{2,1,0:T(8,128)(2,1)S(1)} %wide_queries.2.q_ref, bf16[5120,128]{1,0:T(8,128)(2,1)S(1)} %collective-permute-done.7.refs_0_, ...), custom_call_target="tpu_custom_call", output_to_operand_aliasing={{0}: (4, {}), {1}: (5, {})} | custom-call | flops 8999999488 | tf_op jit(solution)/shard_map/stage/pallas_call | solution.py:282
  87.7 11.7 %near.1.near_ref = f32[8,128,512]{2,1,0:T(8,128)S(1)} custom-call(s32[1]{0:T(128)} %bitcast.4.begin_ref, bf16[8,512,256]{2,1,0:T(8,128)(2,1)S(1)} %wide_queries.2.q_ref, bf16[320,512]{1,0:T(8,128)(2,1)S(1)} %collective-permute-done.2.far_ref, bf16[320,512]{1,0:T(8,128)(2,1)S(1)} %bitcast.47, bf16[256,384]{1,0:T(8,128)(2,1)S(1)} %pad_maximum_fusion.comp_ref, ...), custom_call_target="tpu_custom_call" | custom-call | flops 14000000000 | tf_op jit(solution)/shard_map/near/pallas_call | solution.py:179
  99.4 6.7 %collective-permute-done.10.refs_0_ = bf16[5120,128]{1,0:T(8,128)(2,1)S(1)} collective-permute-done((bf16[5120,128]{1,0:T(8,128)(2,1)S(1)}, bf16[5120,128]{1,0:T(8,128)(2,1)S(1)}, u32[]{:S(2)}, u32[]{:S(2)}) %collective-permute-start.10) | collective-permute-done | bytes 1310752 | tf_op jit(solution)/shard_map/ppermute | solution.py:452
  106.1 3.5 %part_stage.3 = bf16[528,512]{1,0:T(8,128)(2,1)S(1)} custom-call(s32[4]{0:T(128)S(1)} %pad_add_fusion.5.order_ref, s32[8,17]{1,0:T(8,128)S(1)} %get-tuple-element.68.list_ref, bf16[8,512,256]{2,1,0:T(8,128)(2,1)S(1)} %wide_queries.3.q_ref, bf16[5120,128]{1,0:T(8,128)(2,1)S(1)} %collective-permute-done.10.refs_0_, ...), custom_call_target="tpu_custom_call" | custom-call | flops 4000000000 | tf_op jit(solution)/shard_map/part_stage/pallas_call | solution.py:341
  109.6 1.6 %collective-permute-start.12 = (bf16[528,512]{1,0:T(8,128)(2,1)S(1)}, bf16[528,512]{1,0:T(8,128)(2,1)S(1)}, u32[]{:S(2)}, u32[]{:S(2)}) collective-permute-start(bf16[528,512]{1,0:T(8,128)(2,1)S(1)} %part_stage.3), channel_id=1, source_target_pairs={{0,4},{4,0},{1,5},{5,1},{2,6},{6,2},{3,7},{7,3},{8,12},{12,8},{9,1... | collective-permute-start | bytes 1622024 | tf_op jit(solution)/shard_map/ppermute | solution.py:432
  111.1 2.9 %part_stage.2 = bf16[528,512]{1,0:T(8,128)(2,1)S(1)} custom-call(s32[4]{0:T(128)S(1)} %pad_add_fusion.4.order_ref, s32[8,17]{1,0:T(8,128)S(1)} %get-tuple-element.68.list_ref, bf16[8,512,256]{2,1,0:T(8,128)(2,1)S(1)} %wide_queries.3.q_ref, bf16[5120,128]{1,0:T(8,128)(2,1)S(1)} %collective-permute-done.10.refs_0_, ...), custom_call_target="tpu_custom_call" | custom-call | flops 4000000000 | tf_op jit(solution)/shard_map/part_stage/pallas_call | solution.py:341
  114.0 0.0 slice-start.1
  114.0 5.4 %stage.9 = (f32[8,2,512]{2,1,0:T(2,128)S(1)}, f32[8,128,512]{2,1,0:T(8,128)S(1)}) custom-call(s32[8,17]{1,0:T(8,128)S(1)} %get-tuple-element.43.list_ref, bf16[8,512,256]{2,1,0:T(8,128)(2,1)S(1)} %wide_queries.2.q_ref, bf16[5120,128]{1,0:T(8,128)(2,1)S(1)} %collective-permute-done.10.refs_0_, ...), custom_call_target="tpu_custom_call", output_to_operand_aliasing={{0}: (4, {}), {1}: (5, {})} | custom-call | flops 8999999488 | tf_op jit(solution)/shard_map/stage/pallas_call | solution.py:282
  119.5 1.8 %collective-permute-done.12.refs_0_ = bf16[528,512]{1,0:T(8,128)(2,1)S(1)} collective-permute-done((bf16[528,512]{1,0:T(8,128)(2,1)S(1)}, bf16[528,512]{1,0:T(8,128)(2,1)S(1)}, u32[]{:S(2)}, u32[]{:S(2)}) %collective-permute-start.12) | collective-permute-done | bytes 540704 | tf_op jit(solution)/shard_map/ppermute | solution.py:432
  121.3 1.2 last_stage.2
  122.5 1.5 %fusion.15 = (bf16[256,2560]{1,0:T(8,128)(2,1)S(1)}, f32[256,2560]{1,0:T(8,128)S(1)}) fusion(bf16[256,1024]{1,0:T(8,128)(2,1)S(1)} %last_stage.2, bf16[1024,2560]{1,0:T(8,128)(2,1)S(1)} %bitcast.49), kind=kOutput, calls=%fused_computation.74 | convolution fusion | flops 1342832640 | bytes 9699328 | tf_op jit(solution)/shard_map/dot_general | solution.py:529
  124.1 0.1 collective-permute-start.13
  124.2 0.5 collective-permute-start.14
  124.7 0.8 collective-permute-start.15
  125.5 0.3 collective-permute-done.13
  125.8 0.5 collective-permute-done.14
  126.3 0.1 fusion.2
  126.4 0.3 collective-permute-start.18
  126.7 12.3 %collective-permute-done.15.refs_0_ = bf16[528,512]{1,0:T(8,128)(2,1)S(1)} collective-permute-done((bf16[528,512]{1,0:T(8,128)(2,1)S(1)}, bf16[528,512]{1,0:T(8,128)(2,1)S(1)}, u32[]{:S(2)}, u32[]{:S(2)}) %collective-permute-start.15) | collective-permute-done | bytes 540704 | tf_op jit(solution)/shard_map/ppermute | solution.py:432
  138.9 1.2 last_stage.3
  140.2 1.5 %fusion.16 = (bf16[256,2560]{1,0:T(8,128)(2,1)S(1)}, f32[256,2560]{1,0:T(8,128)S(1)}) fusion(bf16[256,1024]{1,0:T(8,128)(2,1)S(1)} %last_stage.3, bf16[1024,2560]{1,0:T(8,128)(2,1)S(1)} %bitcast.49), kind=kOutput, calls=%fused_computation.75 | convolution fusion | flops 1342832640 | bytes 9699328 | tf_op jit(solution)/shard_map/dot_general | solution.py:529
  141.8 0.1 collective-permute-start.16
  141.8 0.5 collective-permute-start.17
  142.3 1.1 collective-permute-done.16
  143.4 0.5 collective-permute-done.17
  143.9 1.1 fusion.3
  (39 shorter events, 0.3 us)
Async XLA Ops:
  0.0 10.8 %copy-start.4 = (s32[1,8,1,16]{3,2,1,0:T(1,128)S(1)}, s32[1,8,1,16]{3,2,1,0:T(1,128)}, u32[]{:S(2)}) copy-start(s32[1,8,1,16]{3,2,1,0:T(1,128)} %param.13) | copy-start | bytes 1540
  0.0 14.3 %copy-start.3 = (f32[1,512,1,24]{1,3,2,0:T(8,128)S(1)}, f32[1,512,1,24]{1,3,2,0:T(8,128)}, u32[]{:S(2)}) copy-start(f32[1,512,1,24]{1,3,2,0:T(8,128)} %param.12) | copy-start | bytes 147460
  0.0 18.3 %copy-start = (bf16[1,512,1,1536]{3,1,2,0:T(8,128)(2,1)S(1)}, bf16[1,512,1,1536]{3,1,2,0:T(8,128)(2,1)}, u32[]{:S(2)}) copy-start(bf16[1,512,1,1536]{3,1,2,0:T(8,128)(2,1)} %param.8) | copy-start | bytes 4718596
  3.8 36.1 %collective-permute-start.4 = (bf16[5120,128]{1,0:T(8,128)(2,1)}, bf16[5120,128]{1,0:T(8,128)(2,1)}, u32[]{:S(2)}, u32[]{:S(2)}) collective-permute-start(bf16[5120,128]{1,0:T(8,128)(2,1)} %get-tuple-element.29.refs_0_), channel_id=1, source_target_pairs={{8,0},{16,8},{24,16},{9,1},{17,9},{25,17},{10,2},{18,10},{26,18},{... | collective-permute-start | bytes 3932168 | tf_op jit(solution)/shard_map/ppermute | solution.py:452
  5.1 34.9 %collective-permute-start.5 = (bf16[5120,128]{1,0:T(8,128)(2,1)}, bf16[5120,128]{1,0:T(8,128)(2,1)S(1)}, u32[]{:S(2)}, u32[]{:S(2)}) collective-permute-start(bf16[5120,128]{1,0:T(8,128)(2,1)} %get-tuple-element.29.refs_0_), channel_id=1, source_target_pairs={{0,8},{8,16},{16,24},{1,9},{9,17},{17,25},{2,10},{10,18},{18,26},{... | collective-permute-start | bytes 3932168 | tf_op jit(solution)/shard_map/ppermute | solution.py:452
  10.8 4.0 %collective-permute-start = (s32[8,16]{1,0:T(8,128)S(1)}, s32[8,16]{1,0:T(8,128)S(1)}, u32[]{:S(2)}, u32[]{:S(2)}) collective-permute-start(s32[8,16]{1,0:T(8,128)S(1)} %bitcast.50), channel_id=1, source_target_pairs={{0,4},{4,0},{1,5},{5,1},{2,6},{6,2},{3,7},{7,3},{8,12},{12,8},{9,1... | collective-permute-start | bytes 1544 | tf_op jit(solution)/shard_map/ppermute | solution.py:432
  12.8 4.0 %collective-permute-start.1 = (bf16[32,384]{1,0:T(8,128)(2,1)}, bf16[32,384]{1,0:T(8,128)(2,1)S(1)}, u32[]{:S(2)}, u32[]{:S(2)}) collective-permute-start(bf16[32,384]{1,0:T(8,128)(2,1)} %get-tuple-element.26), channel_id=1, source_target_pairs={{0,4},{4,0},{1,5},{5,1},{2,6},{6,2},{3,7},{7,3},{8,12},{12,8},{9,1... | collective-permute-start | bytes 73736 | tf_op jit(solution)/shard_map/ppermute | solution.py:427
  16.8 23.1 %collective-permute-start.3 = (bf16[64,384]{1,0:T(8,128)(2,1)S(1)}, bf16[64,384]{1,0:T(8,128)(2,1)S(1)}, u32[]{:S(2)}, u32[]{:S(2)}) collective-permute-start(bf16[64,384]{1,0:T(8,128)(2,1)S(1)} %constant_dynamic-update-slice_fusion), channel_id=1, source_target_pairs={{0,8},{8,0},{16,24},{24,16},{1,9},{9,1},{17,25},{25,17},{2,10},{10... | collective-permute-start | bytes 147464 | tf_op jit(solution)/shard_map/ppermute | solution.py:427
  18.3 2.4 %copy-start.2 = (bf16[1,512,1,320]{1,3,2,0:T(8,128)(2,1)S(1)}, bf16[1,512,1,320]{1,3,2,0:T(8,128)(2,1)}, u32[]{:S(2)}) copy-start(bf16[1,512,1,320]{1,3,2,0:T(8,128)(2,1)} %param.9) | copy-start | bytes 983044
  18.3 27.6 %copy-start.1 = (bf16[5120,128]{1,0:T(8,128)(2,1)S(1)}, bf16[5120,128]{1,0:T(8,128)(2,1)}, u32[]{:S(2)}) copy-start(bf16[5120,128]{1,0:T(8,128)(2,1)} %get-tuple-element.29.refs_0_) | copy-start | bytes 3932164
  18.3 36.7 %collective-permute-start.9 = (bf16[512,1536]{1,0:T(8,128)(2,1)S(1)}, bf16[512,1536]{1,0:T(8,128)(2,1)S(1)}, u32[]{:S(2)}, u32[]{:S(2)}) collective-permute-start(bf16[512,1536]{1,0:T(8,128)(2,1)S(1)} %bitcast.44), channel_id=1, source_target_pairs={{0,4},{4,0},{1,5},{5,1},{2,6},{6,2},{3,7},{7,3},{8,12},{12,8},{9,1... | collective-permute-start | bytes 4718600 | tf_op jit(solution)/shard_map/ppermute | solution.py:432
  20.7 66.9 %collective-permute-start.2 = (bf16[320,512]{1,0:T(8,128)(2,1)S(1)}, bf16[320,512]{1,0:T(8,128)(2,1)S(1)}, u32[]{:S(2)}, u32[]{:S(2)}) collective-permute-start(bf16[320,512]{1,0:T(8,128)(2,1)S(1)} %bitcast.46), channel_id=1, source_target_pairs={{0,4},{1,5},{2,6},{3,7},{8,12},{9,13},{10,14},{11,15},{16,20},{17,... | collective-permute-start | bytes 983048 | tf_op jit(solution)/shard_map/ppermute | solution.py:474
  40.0 47.6 %collective-permute-start.6 = (bf16[128,384]{1,0:T(8,128)(2,1)S(1)}, bf16[128,384]{1,0:T(8,128)(2,1)S(1)}, u32[]{:S(2)}, u32[]{:S(2)}) collective-permute-start(bf16[128,384]{1,0:T(8,128)(2,1)S(1)} %constant_dynamic-update-slice_fusion.2), channel_id=1, source_target_pairs={{0,16},{8,24},{16,0},{24,8},{1,17},{9,25},{17,1},{25,9},{2,18},{10... | collective-permute-start | bytes 294920 | tf_op jit(solution)/shard_map/ppermute | solution.py:427
  43.9 31.9 %collective-permute-start.7 = (bf16[5120,128]{1,0:T(8,128)(2,1)}, bf16[5120,128]{1,0:T(8,128)(2,1)S(1)}, u32[]{:S(2)}, u32[]{:S(2)}) collective-permute-start(bf16[5120,128]{1,0:T(8,128)(2,1)} %collective-permute-done.4.refs_1_), channel_id=1, source_target_pairs={{8,0},{16,8},{9,1},{17,9},{10,2},{18,10},{11,3},{19,11},{12,4},{20... | collective-permute-start | bytes 3932168 | tf_op jit(solution)/shard_map/ppermute | solution.py:452
  45.2 31.9 %collective-permute-start.8 = (bf16[5120,128]{1,0:T(8,128)(2,1)S(1)}, bf16[5120,128]{1,0:T(8,128)(2,1)S(1)}, u32[]{:S(2)}, u32[]{:S(2)}) collective-permute-start(bf16[5120,128]{1,0:T(8,128)(2,1)S(1)} %collective-permute-done.5.refs_2_), channel_id=1, source_target_pairs={{8,16},{16,24},{9,17},{17,25},{10,18},{18,26},{11,19},{19,27},{12,... | collective-permute-start | bytes 3932168 | tf_op jit(solution)/shard_map/ppermute | solution.py:452
  75.8 30.3 %collective-permute-start.10 = (bf16[5120,128]{1,0:T(8,128)(2,1)S(1)}, bf16[5120,128]{1,0:T(8,128)(2,1)S(1)}, u32[]{:S(2)}, u32[]{:S(2)}) collective-permute-start(bf16[5120,128]{1,0:T(8,128)(2,1)S(1)} %collective-permute-done.7.refs_0_), channel_id=1, source_target_pairs={{8,0},{9,1},{10,2},{11,3},{12,4},{13,5},{14,6},{15,7}} | collective-permute-start | bytes 3932168 | tf_op jit(solution)/shard_map/ppermute | solution.py:452
  77.1 29.0 %collective-permute-start.11 = (bf16[5120,128]{1,0:T(8,128)(2,1)S(1)}, bf16[5120,128]{1,0:T(8,128)(2,1)S(1)}, u32[]{:S(2)}, u32[]{:S(2)}) collective-permute-start(bf16[5120,128]{1,0:T(8,128)(2,1)S(1)} %collective-permute-done.8.refs_1_), channel_id=1, source_target_pairs={{16,24},{17,25},{18,26},{19,27},{20,28},{21,29},{22,30},{23,31}} | collective-permute-start | bytes 3932168 | tf_op jit(solution)/shard_map/ppermute | solution.py:452
  109.6 11.7 %collective-permute-start.12 = (bf16[528,512]{1,0:T(8,128)(2,1)S(1)}, bf16[528,512]{1,0:T(8,128)(2,1)S(1)}, u32[]{:S(2)}, u32[]{:S(2)}) collective-permute-start(bf16[528,512]{1,0:T(8,128)(2,1)S(1)} %part_stage.3), channel_id=1, source_target_pairs={{0,4},{4,0},{1,5},{5,1},{2,6},{6,2},{3,7},{7,3},{8,12},{12,8},{9,1... | collective-permute-start | bytes 1622024 | tf_op jit(solution)/shard_map/ppermute | solution.py:432
  111.1 11.4 %slice-start = ((s8[5242880]{0:T(1024)(128)(4,1)}), s8[4194304]{0:T(1024)(128)(4,1)S(1)}, s32[]{:S(2)}) async-start(s8[5242880]{0:T(1024)(128)(4,1)} %bitcast.48), calls=%async_computation | async-start | bytes 8388608
  114.0 8.5 %slice-start.1 = ((s8[5242880]{0:T(1024)(128)(4,1)}), s8[1048576]{0:T(1024)(128)(4,1)S(1)}, s32[]{:S(2)}) async-start(s8[5242880]{0:T(1024)(128)(4,1)} %bitcast.48), calls=%async_computation.1 | async-start | bytes 2097152
  124.1 1.7 %collective-permute-start.13 = (bf16[64,2560]{1,0:T(8,128)(2,1)S(1)}, bf16[64,2560]{1,0:T(8,128)(2,1)S(1)}, u32[]{:S(2)}, u32[]{:S(2)}) collective-permute-start(bf16[64,2560]{1,0:T(8,128)(2,1)S(1)} %get-tuple-element.59), channel_id=1, source_target_pairs={{0,1},{1,0},{2,3},{3,2},{4,5},{5,4},{6,7},{7,6},{8,9},{9,8},{10,11... | collective-permute-start | bytes 983048 | tf_op jit(solution)/shard_map/ppermute | solution.py:427
  124.2 2.1 %collective-permute-start.14 = (bf16[64,2560]{1,0:T(8,128)(2,1)S(1)}, bf16[64,2560]{1,0:T(8,128)(2,1)S(1)}, u32[]{:S(2)}, u32[]{:S(2)}) collective-permute-start(bf16[64,2560]{1,0:T(8,128)(2,1)S(1)} %get-tuple-element.60), channel_id=1, source_target_pairs={{0,1},{1,0},{2,3},{3,2},{4,5},{5,4},{6,7},{7,6},{8,9},{9,8},{10,11... | collective-permute-start | bytes 983048 | tf_op jit(solution)/shard_map/ppermute | solution.py:427
  124.7 14.3 %collective-permute-start.15 = (bf16[528,512]{1,0:T(8,128)(2,1)S(1)}, bf16[528,512]{1,0:T(8,128)(2,1)S(1)}, u32[]{:S(2)}, u32[]{:S(2)}) collective-permute-start(bf16[528,512]{1,0:T(8,128)(2,1)S(1)} %part_stage.2), channel_id=1, source_target_pairs={{0,4},{4,0},{1,5},{5,1},{2,6},{6,2},{3,7},{7,3},{8,12},{12,8},{9,1... | collective-permute-start | bytes 1622024 | tf_op jit(solution)/shard_map/ppermute | solution.py:432
  126.4 17.5 %collective-permute-start.18 = (bf16[128,2560]{1,0:T(8,128)(2,1)S(1)}, bf16[128,2560]{1,0:T(8,128)(2,1)S(1)}, u32[]{:S(2)}, u32[]{:S(2)}) collective-permute-start(bf16[128,2560]{1,0:T(8,128)(2,1)S(1)} %fusion.2), channel_id=1, source_target_pairs={{0,2},{1,3},{2,0},{3,1},{4,6},{5,7},{6,4},{7,5},{8,10},{9,11},{10,... | collective-permute-start | bytes 1966088 | tf_op jit(solution)/shard_map/ppermute | solution.py:427
  141.8 1.7 %collective-permute-start.16 = (bf16[64,2560]{1,0:T(8,128)(2,1)S(1)}, bf16[64,2560]{1,0:T(8,128)(2,1)S(1)}, u32[]{:S(2)}, u32[]{:S(2)}) collective-permute-start(bf16[64,2560]{1,0:T(8,128)(2,1)S(1)} %get-tuple-element.57), channel_id=1, source_target_pairs={{0,1},{1,0},{2,3},{3,2},{4,5},{5,4},{6,7},{7,6},{8,9},{9,8},{10,11... | collective-permute-start | bytes 983048 | tf_op jit(solution)/shard_map/ppermute | solution.py:427
  141.8 2.1 %collective-permute-start.17 = (bf16[64,2560]{1,0:T(8,128)(2,1)S(1)}, bf16[64,2560]{1,0:T(8,128)(2,1)S(1)}, u32[]{:S(2)}, u32[]{:S(2)}) collective-permute-start(bf16[64,2560]{1,0:T(8,128)(2,1)S(1)} %get-tuple-element.58), channel_id=1, source_target_pairs={{0,1},{1,0},{2,3},{3,2},{4,5},{5,4},{6,7},{7,6},{8,9},{9,8},{10,11... | collective-permute-start | bytes 983048 | tf_op jit(solution)/shard_map/ppermute | solution.py:427

commit v6 on v5

--- a/solution.py
+++ b/solution.py
@@ -476,7 +476,7 @@
     hops = [[(packed, 0)]] + spread(packed, "sib", wraps)
     for number, bit in enumerate(1 << k for k in range((sib_count - 1).bit_length())):
         got = swap(comp, "sib", bit)
-        behind = [a for a, _ in hops[min(number + 1, len(hops) - 1)]]
+        behind = [a for a, _ in hops[min(number + 1, len(hops) - 1)]][:1]
         comp, got = lax.optimization_barrier((comp, got, behind))[:2]
         comp = jnp.concatenate([comp, got], axis=0)
 

time: 145 us -> 145 us (level)
  Pallas kernels: 62.6 us -> 59 us
  starting transfers between devices: 26.4 us -> 29.3 us
    ppermute x6, waiting for transfers between devices: 14.3 us -> 18.5 us  [spread(): held[side] = lax.ppermute(held[side], axis, pairs)]
    pallas_call x5, Pallas kernels: 36.3 us -> 32.7 us  [stage(): pl.pallas_call(functools.partial(stage_kernel, first, len(kvs), unit), gr...]
    ppermute x4, waiting for transfers between devices: 14.1 us -> 11 us  [shift(): lax.ppermute(value, axis, [(i, (i + steps) % count) for i in range(count)])]
    ppermute x8, starting transfers between devices: 6.89 us -> 8.89 us  [swap(): lax.ppermute(value, axis, [(i, i ^ bit) for i in range(lax.axis_size(axis...]
  transfers between devices with their start and end apart: 19 -> 19, of which waited for: 10 -> 8; matrix products, arithmetic and copies ran while one was open for 3% -> 3% of each run, Pallas kernels for 37% -> 35%
where the time goes in v6:
time: 145 us
  Pallas kernels  59 us (41%)
  waiting for transfers between devices  48.4 us (33%)
  starting transfers between devices  29.3 us (20%)
  matrix products  3.04 us (2%)
  other arithmetic  2.53 us (2%)
    pallas_call x5, Pallas kernels, stage(): pl.pallas_call(functools.partial(stage_kernel, first, len(kvs), unit), gr...  32.7 us
    ppermute x8, waiting for transfers between devices, swap(): lax.ppermute(value, axis, [(i, i ^ bit) for i in range(lax.axis_size(axis...  18.9 us
    ppermute x6, waiting for transfers between devices, spread(): held[side] = lax.ppermute(held[side], axis, pairs)  18.5 us
    pallas_call x1, Pallas kernels, near_parts(): pl.pallas_call(near_kernel, grid_spec=pltpu.PrefetchScalarGridSpec(num_sc...  11.7 us
    ppermute x6, starting transfers between devices, spread(): held[side] = lax.ppermute(held[side], axis, pairs)  11.2 us
    ppermute x4, waiting for transfers between devices, shift(): lax.ppermute(value, axis, [(i, (i + steps) % count) for i in range(count)])  11 us
    ppermute x8, starting transfers between devices, swap(): lax.ppermute(value, axis, [(i, i ^ bit) for i in range(lax.axis_size(axis...  8.89 us
    ppermute x4, starting transfers between devices, shift(): lax.ppermute(value, axis, [(i, (i + steps) % count) for i in range(count)])  6.68 us
  transfers between devices with their start and end apart: 19, of which 8 were waited for; matrix products, arithmetic and copies ran while one was open for 3% of the time, Pallas kernels for 35%

profile of v6, /device:TPU:0, one launch (start us, length us, event | category | flops | bytes accessed | tf_op | source)
XLA Modules:
  0.0 144.7 jit_solution(698909441381953678)
XLA Ops:
  0.0 3.8 %pack.1 = (bf16[5120,128]{1,0:T(8,128)(2,1)}, bf16[32,384]{1,0:T(8,128)(2,1)}) custom-call(bf16[320,2048]{1,0:T(8,128)(2,1)} %bitcast.58, f32[2,64]{1,0:T(2,128)} %pool_ref.1), custom_call_target="tpu_custom_call" | custom-call | flops 5000000000 | tf_op jit(solution)/shard_map/pack/pallas_call | solution.py:76
  3.8 1.3 collective-permute-start.4
  5.1 5.6 %collective-permute-start.7 = (bf16[5120,128]{1,0:T(8,128)(2,1)}, bf16[5120,128]{1,0:T(8,128)(2,1)S(1)}, u32[]{:S(2)}, u32[]{:S(2)}) collective-permute-start(bf16[5120,128]{1,0:T(8,128)(2,1)} %get-tuple-element.29.refs_0_), channel_id=1, source_target_pairs={{0,8},{8,16},{16,24},{1,9},{9,17},{17,25},{2,10},{10,18},{18,26},{... | collective-permute-start | bytes 3932168 | tf_op jit(solution)/shard_map/ppermute | solution.py:452
  10.8 2.0 %collective-permute-start = (s32[8,16]{1,0:T(8,128)S(1)}, s32[8,16]{1,0:T(8,128)S(1)}, u32[]{:S(2)}, u32[]{:S(2)}) collective-permute-start(s32[8,16]{1,0:T(8,128)S(1)} %bitcast.50), channel_id=1, source_target_pairs={{0,4},{4,0},{1,5},{5,1},{2,6},{6,2},{3,7},{7,3},{8,12},{12,8},{9,1... | collective-permute-start | bytes 1544 | tf_op jit(solution)/shard_map/ppermute | solution.py:432
  12.8 0.1 collective-permute-start.1
  12.9 0.8 constant_dynamic-update-slice_fusion.1
  14.4 0.1 div.39
  14.5 0.1 reshape.525
  14.7 0.1 pad_add_fusion.5.order_ref
  14.7 0.1 pad_add_fusion.4.order_ref
  14.8 0.0 collective-permute-done
  14.8 0.2 convert_reduce_fusion.3
  15.0 0.2 select_add_fusion
  15.1 0.2 convert_reduce_fusion
  15.4 0.1 copy.30
  15.4 0.1 copy.29
  15.5 0.1 copy.26
  15.6 0.2 select_reduce_fusion
  15.8 0.1 fusion.11
  15.9 0.1 fusion.12
  16.0 0.1 select_reduce_fusion.2
  16.1 0.1 pad_add_fusion.1
  16.2 0.6 collective-permute-done.1
  16.8 1.5 %collective-permute-start.3 = (bf16[64,384]{1,0:T(8,128)(2,1)S(1)}, bf16[64,384]{1,0:T(8,128)(2,1)S(1)}, u32[]{:S(2)}, u32[]{:S(2)}) collective-permute-start(bf16[64,384]{1,0:T(8,128)(2,1)S(1)} %constant_dynamic-update-slice_fusion), channel_id=1, source_target_pairs={{0,8},{8,0},{16,24},{24,16},{1,9},{9,1},{17,25},{25,17},{2,10},{10... | collective-permute-start | bytes 147464 | tf_op jit(solution)/shard_map/ppermute | solution.py:427
  18.3 1.4 collective-permute-start.9
  19.7 1.0 wide_queries.2.q_ref
  20.7 2.6 %collective-permute-start.2 = (bf16[320,512]{1,0:T(8,128)(2,1)S(1)}, bf16[320,512]{1,0:T(8,128)(2,1)S(1)}, u32[]{:S(2)}, u32[]{:S(2)}) collective-permute-start(bf16[320,512]{1,0:T(8,128)(2,1)S(1)} %bitcast.46), channel_id=1, source_target_pairs={{0,4},{1,5},{2,6},{3,7},{8,12},{9,13},{10,14},{11,15},{16,20},{17,... | collective-permute-start | bytes 983048 | tf_op jit(solution)/shard_map/ppermute | solution.py:474
  23.3 16.7 %collective-permute-done.3 = bf16[64,384]{1,0:T(8,128)(2,1)S(1)} collective-permute-done((bf16[64,384]{1,0:T(8,128)(2,1)S(1)}, bf16[64,384]{1,0:T(8,128)(2,1)S(1)}, u32[]{:S(2)}, u32[]{:S(2)}) %collective-permute-start.3) | collective-permute-done | bytes 49184 | tf_op jit(solution)/shard_map/ppermute | solution.py:427
  40.0 0.0 collective-permute-done.4.refs_1_
  40.0 3.9 %collective-permute-start.5 = (bf16[128,384]{1,0:T(8,128)(2,1)S(1)}, bf16[128,384]{1,0:T(8,128)(2,1)S(1)}, u32[]{:S(2)}, u32[]{:S(2)}) collective-permute-start(bf16[128,384]{1,0:T(8,128)(2,1)S(1)} %constant_dynamic-update-slice_fusion.2), channel_id=1, source_target_pairs={{0,16},{8,24},{16,0},{24,8},{1,17},{9,25},{17,1},{25,9},{2,18},{10... | collective-permute-start | bytes 294920 | tf_op jit(solution)/shard_map/ppermute | solution.py:427
  43.9 1.3 collective-permute-start.6
  45.2 0.0 collective-permute-done.7.refs_2_
  45.2 0.7 collective-permute-start.8
  45.9 9.1 %stage.5 = (f32[8,2,512]{2,1,0:T(2,128)S(1)}, f32[8,128,512]{2,1,0:T(8,128)S(1)}) custom-call(s32[8,17]{1,0:T(8,128)S(1)} %get-tuple-element.62.list_ref, bf16[8,512,256]{2,1,0:T(8,128)(2,1)S(1)} %wide_queries.2.q_ref, bf16[5120,128]{1,0:T(8,128)(2,1)S(1)} %copy-done.1, bf16[5120,128]{1,0:T(8,128)(2,1)} %collective-permute-done.4.refs_1_, ...), custom_call_target="tpu_custom_call" | custom-call | flops 8999999488 | tf_op jit(solution)/shard_map/stage/pallas_call | solution.py:282
  55.1 1.0 wide_queries.3.q_ref
  56.1 9.1 %stage.7 = (f32[8,2,512]{2,1,0:T(2,128)S(1)}, f32[8,128,512]{2,1,0:T(8,128)S(1)}) custom-call(s32[8,17]{1,0:T(8,128)S(1)} %get-tuple-element.61.list_ref, bf16[8,512,256]{2,1,0:T(8,128)(2,1)S(1)} %wide_queries.3.q_ref, bf16[5120,128]{1,0:T(8,128)(2,1)S(1)} %copy-done.1, bf16[5120,128]{1,0:T(8,128)(2,1)} %collective-permute-done.4.refs_1_, ...), custom_call_target="tpu_custom_call" | custom-call | flops 8999999488 | tf_op jit(solution)/shard_map/stage/pallas_call | solution.py:282
  65.2 10.5 %collective-permute-done.6.refs_0_ = bf16[5120,128]{1,0:T(8,128)(2,1)S(1)} collective-permute-done((bf16[5120,128]{1,0:T(8,128)(2,1)}, bf16[5120,128]{1,0:T(8,128)(2,1)S(1)}, u32[]{:S(2)}, u32[]{:S(2)}) %collective-permute-start.6) | collective-permute-done | bytes 1310752 | tf_op jit(solution)/shard_map/ppermute | solution.py:452
  75.8 1.3 collective-permute-start.10
  77.1 0.9 collective-permute-start.11
  78.0 4.8 %stage.8 = (f32[8,2,512]{2,1,0:T(2,128)S(1)}, f32[8,128,512]{2,1,0:T(8,128)S(1)}) custom-call(s32[8,17]{1,0:T(8,128)S(1)} %get-tuple-element.63.list_ref, bf16[8,512,256]{2,1,0:T(8,128)(2,1)S(1)} %wide_queries.3.q_ref, bf16[5120,128]{1,0:T(8,128)(2,1)S(1)} %collective-permute-done.6.refs_0_, ...), custom_call_target="tpu_custom_call", output_to_operand_aliasing={{0}: (4, {}), {1}: (5, {})} | custom-call | flops 8999999488 | tf_op jit(solution)/shard_map/stage/pallas_call | solution.py:282
  82.8 3.5 %stage.6 = (f32[8,2,512]{2,1,0:T(2,128)S(1)}, f32[8,128,512]{2,1,0:T(8,128)S(1)}) custom-call(s32[8,17]{1,0:T(8,128)S(1)} %get-tuple-element.64.list_ref, bf16[8,512,256]{2,1,0:T(8,128)(2,1)S(1)} %wide_queries.2.q_ref, bf16[5120,128]{1,0:T(8,128)(2,1)S(1)} %collective-permute-done.6.refs_0_, ...), custom_call_target="tpu_custom_call", output_to_operand_aliasing={{0}: (4, {}), {1}: (5, {})} | custom-call | flops 8999999488 | tf_op jit(solution)/shard_map/stage/pallas_call | solution.py:282
  86.4 11.7 %near.1.near_ref = f32[8,128,512]{2,1,0:T(8,128)S(1)} custom-call(s32[1]{0:T(128)} %bitcast.4.begin_ref, bf16[8,512,256]{2,1,0:T(8,128)(2,1)S(1)} %wide_queries.2.q_ref, bf16[320,512]{1,0:T(8,128)(2,1)S(1)} %collective-permute-done.2.far_ref, bf16[320,512]{1,0:T(8,128)(2,1)S(1)} %bitcast.47, bf16[256,384]{1,0:T(8,128)(2,1)S(1)} %pad_maximum_fusion.comp_ref, ...), custom_call_target="tpu_custom_call" | custom-call | flops 14000000000 | tf_op jit(solution)/shard_map/near/pallas_call | solution.py:179
  98.1 8.0 %collective-permute-done.10.refs_0_ = bf16[5120,128]{1,0:T(8,128)(2,1)S(1)} collective-permute-done((bf16[5120,128]{1,0:T(8,128)(2,1)S(1)}, bf16[5120,128]{1,0:T(8,128)(2,1)S(1)}, u32[]{:S(2)}, u32[]{:S(2)}) %collective-permute-start.10) | collective-permute-done | bytes 1310752 | tf_op jit(solution)/shard_map/ppermute | solution.py:452
  106.1 3.5 %part_stage.3 = bf16[528,512]{1,0:T(8,128)(2,1)S(1)} custom-call(s32[4]{0:T(128)S(1)} %pad_add_fusion.5.order_ref, s32[8,17]{1,0:T(8,128)S(1)} %get-tuple-element.68.list_ref, bf16[8,512,256]{2,1,0:T(8,128)(2,1)S(1)} %wide_queries.3.q_ref, bf16[5120,128]{1,0:T(8,128)(2,1)S(1)} %collective-permute-done.10.refs_0_, ...), custom_call_target="tpu_custom_call" | custom-call | flops 4000000000 | tf_op jit(solution)/shard_map/part_stage/pallas_call | solution.py:341
  109.6 1.6 %collective-permute-start.12 = (bf16[528,512]{1,0:T(8,128)(2,1)S(1)}, bf16[528,512]{1,0:T(8,128)(2,1)S(1)}, u32[]{:S(2)}, u32[]{:S(2)}) collective-permute-start(bf16[528,512]{1,0:T(8,128)(2,1)S(1)} %part_stage.3), channel_id=1, source_target_pairs={{0,4},{4,0},{1,5},{5,1},{2,6},{6,2},{3,7},{7,3},{8,12},{12,8},{9,1... | collective-permute-start | bytes 1622024 | tf_op jit(solution)/shard_map/ppermute | solution.py:432
  111.1 2.9 %part_stage.2 = bf16[528,512]{1,0:T(8,128)(2,1)S(1)} custom-call(s32[4]{0:T(128)S(1)} %pad_add_fusion.4.order_ref, s32[8,17]{1,0:T(8,128)S(1)} %get-tuple-element.68.list_ref, bf16[8,512,256]{2,1,0:T(8,128)(2,1)S(1)} %wide_queries.3.q_ref, bf16[5120,128]{1,0:T(8,128)(2,1)S(1)} %collective-permute-done.10.refs_0_, ...), custom_call_target="tpu_custom_call" | custom-call | flops 4000000000 | tf_op jit(solution)/shard_map/part_stage/pallas_call | solution.py:341
  114.0 0.0 slice-start.1
  114.0 6.1 %stage.9 = (f32[8,2,512]{2,1,0:T(2,128)S(1)}, f32[8,128,512]{2,1,0:T(8,128)S(1)}) custom-call(s32[8,17]{1,0:T(8,128)S(1)} %get-tuple-element.43.list_ref, bf16[8,512,256]{2,1,0:T(8,128)(2,1)S(1)} %wide_queries.2.q_ref, bf16[5120,128]{1,0:T(8,128)(2,1)S(1)} %collective-permute-done.10.refs_0_, ...), custom_call_target="tpu_custom_call", output_to_operand_aliasing={{0}: (4, {}), {1}: (5, {})} | custom-call | flops 8999999488 | tf_op jit(solution)/shard_map/stage/pallas_call | solution.py:282
  120.1 0.9 collective-permute-done.12.refs_0_
  121.0 1.2 last_stage.2
  122.3 1.5 %fusion.15 = (bf16[256,2560]{1,0:T(8,128)(2,1)S(1)}, f32[256,2560]{1,0:T(8,128)S(1)}) fusion(bf16[256,1024]{1,0:T(8,128)(2,1)S(1)} %last_stage.2, bf16[1024,2560]{1,0:T(8,128)(2,1)S(1)} %bitcast.49), kind=kOutput, calls=%fused_computation.74 | convolution fusion | flops 1342832640 | bytes 9699328 | tf_op jit(solution)/shard_map/dot_general | solution.py:529
  123.9 0.1 collective-permute-start.13
  123.9 0.5 collective-permute-start.14
  124.4 1.7 %collective-permute-start.15 = (bf16[528,512]{1,0:T(8,128)(2,1)S(1)}, bf16[528,512]{1,0:T(8,128)(2,1)S(1)}, u32[]{:S(2)}, u32[]{:S(2)}) collective-permute-start(bf16[528,512]{1,0:T(8,128)(2,1)S(1)} %part_stage.2), channel_id=1, source_target_pairs={{0,4},{4,0},{1,5},{5,1},{2,6},{6,2},{3,7},{7,3},{8,12},{12,8},{9,1... | collective-permute-start | bytes 1622024 | tf_op jit(solution)/shard_map/ppermute | solution.py:432
  126.2 0.1 fusion.2
  126.3 2.3 %collective-permute-start.18 = (bf16[128,2560]{1,0:T(8,128)(2,1)S(1)}, bf16[128,2560]{1,0:T(8,128)(2,1)S(1)}, u32[]{:S(2)}, u32[]{:S(2)}) collective-permute-start(bf16[128,2560]{1,0:T(8,128)(2,1)S(1)} %fusion.2), channel_id=1, source_target_pairs={{0,2},{1,3},{2,0},{3,1},{4,6},{5,7},{6,4},{7,5},{8,10},{9,11},{10,... | collective-permute-start | bytes 1966088 | tf_op jit(solution)/shard_map/ppermute | solution.py:427
  128.6 10.1 %collective-permute-done.15.refs_0_ = bf16[528,512]{1,0:T(8,128)(2,1)S(1)} collective-permute-done((bf16[528,512]{1,0:T(8,128)(2,1)S(1)}, bf16[528,512]{1,0:T(8,128)(2,1)S(1)}, u32[]{:S(2)}, u32[]{:S(2)}) %collective-permute-start.15) | collective-permute-done | bytes 540704 | tf_op jit(solution)/shard_map/ppermute | solution.py:432
  138.7 1.2 last_stage.3
  139.9 1.5 %fusion.16 = (bf16[256,2560]{1,0:T(8,128)(2,1)S(1)}, f32[256,2560]{1,0:T(8,128)S(1)}) fusion(bf16[256,1024]{1,0:T(8,128)(2,1)S(1)} %last_stage.3, bf16[1024,2560]{1,0:T(8,128)(2,1)S(1)} %bitcast.49), kind=kOutput, calls=%fused_computation.75 | convolution fusion | flops 1342832640 | bytes 9699328 | tf_op jit(solution)/shard_map/dot_general | solution.py:529
  141.5 0.1 collective-permute-start.16
  141.6 0.5 collective-permute-start.17
  142.1 1.1 collective-permute-done.16
  143.2 0.5 collective-permute-done.17
  143.7 1.1 fusion.3
  (39 shorter events, 0.3 us)
Async XLA Ops:
  0.0 10.8 %copy-start.4 = (s32[1,8,1,16]{3,2,1,0:T(1,128)S(1)}, s32[1,8,1,16]{3,2,1,0:T(1,128)}, u32[]{:S(2)}) copy-start(s32[1,8,1,16]{3,2,1,0:T(1,128)} %param.13) | copy-start | bytes 1540
  0.0 14.3 %copy-start.3 = (f32[1,512,1,24]{1,3,2,0:T(8,128)S(1)}, f32[1,512,1,24]{1,3,2,0:T(8,128)}, u32[]{:S(2)}) copy-start(f32[1,512,1,24]{1,3,2,0:T(8,128)} %param.12) | copy-start | bytes 147460
  0.0 18.3 %copy-start = (bf16[1,512,1,1536]{3,1,2,0:T(8,128)(2,1)S(1)}, bf16[1,512,1,1536]{3,1,2,0:T(8,128)(2,1)}, u32[]{:S(2)}) copy-start(bf16[1,512,1,1536]{3,1,2,0:T(8,128)(2,1)} %param.8) | copy-start | bytes 4718596
  3.8 36.1 %collective-permute-start.4 = (bf16[5120,128]{1,0:T(8,128)(2,1)}, bf16[5120,128]{1,0:T(8,128)(2,1)}, u32[]{:S(2)}, u32[]{:S(2)}) collective-permute-start(bf16[5120,128]{1,0:T(8,128)(2,1)} %get-tuple-element.29.refs_0_), channel_id=1, source_target_pairs={{8,0},{16,8},{24,16},{9,1},{17,9},{25,17},{10,2},{18,10},{26,18},{... | collective-permute-start | bytes 3932168 | tf_op jit(solution)/shard_map/ppermute | solution.py:452
  5.1 40.0 %collective-permute-start.7 = (bf16[5120,128]{1,0:T(8,128)(2,1)}, bf16[5120,128]{1,0:T(8,128)(2,1)S(1)}, u32[]{:S(2)}, u32[]{:S(2)}) collective-permute-start(bf16[5120,128]{1,0:T(8,128)(2,1)} %get-tuple-element.29.refs_0_), channel_id=1, source_target_pairs={{0,8},{8,16},{16,24},{1,9},{9,17},{17,25},{2,10},{10,18},{18,26},{... | collective-permute-start | bytes 3932168 | tf_op jit(solution)/shard_map/ppermute | solution.py:452
  10.8 4.0 %collective-permute-start = (s32[8,16]{1,0:T(8,128)S(1)}, s32[8,16]{1,0:T(8,128)S(1)}, u32[]{:S(2)}, u32[]{:S(2)}) collective-permute-start(s32[8,16]{1,0:T(8,128)S(1)} %bitcast.50), channel_id=1, source_target_pairs={{0,4},{4,0},{1,5},{5,1},{2,6},{6,2},{3,7},{7,3},{8,12},{12,8},{9,1... | collective-permute-start | bytes 1544 | tf_op jit(solution)/shard_map/ppermute | solution.py:432
  12.8 4.0 %collective-permute-start.1 = (bf16[32,384]{1,0:T(8,128)(2,1)}, bf16[32,384]{1,0:T(8,128)(2,1)S(1)}, u32[]{:S(2)}, u32[]{:S(2)}) collective-permute-start(bf16[32,384]{1,0:T(8,128)(2,1)} %get-tuple-element.26), channel_id=1, source_target_pairs={{0,4},{4,0},{1,5},{5,1},{2,6},{6,2},{3,7},{7,3},{8,12},{12,8},{9,1... | collective-permute-start | bytes 73736 | tf_op jit(solution)/shard_map/ppermute | solution.py:427
  16.8 23.1 %collective-permute-start.3 = (bf16[64,384]{1,0:T(8,128)(2,1)S(1)}, bf16[64,384]{1,0:T(8,128)(2,1)S(1)}, u32[]{:S(2)}, u32[]{:S(2)}) collective-permute-start(bf16[64,384]{1,0:T(8,128)(2,1)S(1)} %constant_dynamic-update-slice_fusion), channel_id=1, source_target_pairs={{0,8},{8,0},{16,24},{24,16},{1,9},{9,1},{17,25},{25,17},{2,10},{10... | collective-permute-start | bytes 147464 | tf_op jit(solution)/shard_map/ppermute | solution.py:427
  18.3 2.4 %copy-start.2 = (bf16[1,512,1,320]{1,3,2,0:T(8,128)(2,1)S(1)}, bf16[1,512,1,320]{1,3,2,0:T(8,128)(2,1)}, u32[]{:S(2)}) copy-start(bf16[1,512,1,320]{1,3,2,0:T(8,128)(2,1)} %param.9) | copy-start | bytes 983044
  18.3 27.6 %copy-start.1 = (bf16[5120,128]{1,0:T(8,128)(2,1)S(1)}, bf16[5120,128]{1,0:T(8,128)(2,1)}, u32[]{:S(2)}) copy-start(bf16[5120,128]{1,0:T(8,128)(2,1)} %get-tuple-element.29.refs_0_) | copy-start | bytes 3932164
  18.3 36.7 %collective-permute-start.9 = (bf16[512,1536]{1,0:T(8,128)(2,1)S(1)}, bf16[512,1536]{1,0:T(8,128)(2,1)S(1)}, u32[]{:S(2)}, u32[]{:S(2)}) collective-permute-start(bf16[512,1536]{1,0:T(8,128)(2,1)S(1)} %bitcast.44), channel_id=1, source_target_pairs={{0,4},{4,0},{1,5},{5,1},{2,6},{6,2},{3,7},{7,3},{8,12},{12,8},{9,1... | collective-permute-start | bytes 4718600 | tf_op jit(solution)/shard_map/ppermute | solution.py:432
  20.7 65.6 %collective-permute-start.2 = (bf16[320,512]{1,0:T(8,128)(2,1)S(1)}, bf16[320,512]{1,0:T(8,128)(2,1)S(1)}, u32[]{:S(2)}, u32[]{:S(2)}) collective-permute-start(bf16[320,512]{1,0:T(8,128)(2,1)S(1)} %bitcast.46), channel_id=1, source_target_pairs={{0,4},{1,5},{2,6},{3,7},{8,12},{9,13},{10,14},{11,15},{16,20},{17,... | collective-permute-start | bytes 983048 | tf_op jit(solution)/shard_map/ppermute | solution.py:474
  40.0 46.3 %collective-permute-start.5 = (bf16[128,384]{1,0:T(8,128)(2,1)S(1)}, bf16[128,384]{1,0:T(8,128)(2,1)S(1)}, u32[]{:S(2)}, u32[]{:S(2)}) collective-permute-start(bf16[128,384]{1,0:T(8,128)(2,1)S(1)} %constant_dynamic-update-slice_fusion.2), channel_id=1, source_target_pairs={{0,16},{8,24},{16,0},{24,8},{1,17},{9,25},{17,1},{25,9},{2,18},{10... | collective-permute-start | bytes 294920 | tf_op jit(solution)/shard_map/ppermute | solution.py:427
  43.9 31.9 %collective-permute-start.6 = (bf16[5120,128]{1,0:T(8,128)(2,1)}, bf16[5120,128]{1,0:T(8,128)(2,1)S(1)}, u32[]{:S(2)}, u32[]{:S(2)}) collective-permute-start(bf16[5120,128]{1,0:T(8,128)(2,1)} %collective-permute-done.4.refs_1_), channel_id=1, source_target_pairs={{8,0},{16,8},{9,1},{17,9},{10,2},{18,10},{11,3},{19,11},{12,4},{20... | collective-permute-start | bytes 3932168 | tf_op jit(solution)/shard_map/ppermute | solution.py:452
  45.2 31.9 %collective-permute-start.8 = (bf16[5120,128]{1,0:T(8,128)(2,1)S(1)}, bf16[5120,128]{1,0:T(8,128)(2,1)S(1)}, u32[]{:S(2)}, u32[]{:S(2)}) collective-permute-start(bf16[5120,128]{1,0:T(8,128)(2,1)S(1)} %collective-permute-done.7.refs_2_), channel_id=1, source_target_pairs={{8,16},{16,24},{9,17},{17,25},{10,18},{18,26},{11,19},{19,27},{12,... | collective-permute-start | bytes 3932168 | tf_op jit(solution)/shard_map/ppermute | solution.py:452
  75.8 30.3 %collective-permute-start.10 = (bf16[5120,128]{1,0:T(8,128)(2,1)S(1)}, bf16[5120,128]{1,0:T(8,128)(2,1)S(1)}, u32[]{:S(2)}, u32[]{:S(2)}) collective-permute-start(bf16[5120,128]{1,0:T(8,128)(2,1)S(1)} %collective-permute-done.6.refs_0_), channel_id=1, source_target_pairs={{8,0},{9,1},{10,2},{11,3},{12,4},{13,5},{14,6},{15,7}} | collective-permute-start | bytes 3932168 | tf_op jit(solution)/shard_map/ppermute | solution.py:452
  77.1 29.0 %collective-permute-start.11 = (bf16[5120,128]{1,0:T(8,128)(2,1)S(1)}, bf16[5120,128]{1,0:T(8,128)(2,1)S(1)}, u32[]{:S(2)}, u32[]{:S(2)}) collective-permute-start(bf16[5120,128]{1,0:T(8,128)(2,1)S(1)} %collective-permute-done.8.refs_1_), channel_id=1, source_target_pairs={{16,24},{17,25},{18,26},{19,27},{20,28},{21,29},{22,30},{23,31}} | collective-permute-start | bytes 3932168 | tf_op jit(solution)/shard_map/ppermute | solution.py:452
  109.6 11.4 %collective-permute-start.12 = (bf16[528,512]{1,0:T(8,128)(2,1)S(1)}, bf16[528,512]{1,0:T(8,128)(2,1)S(1)}, u32[]{:S(2)}, u32[]{:S(2)}) collective-permute-start(bf16[528,512]{1,0:T(8,128)(2,1)S(1)} %part_stage.3), channel_id=1, source_target_pairs={{0,4},{4,0},{1,5},{5,1},{2,6},{6,2},{3,7},{7,3},{8,12},{12,8},{9,1... | collective-permute-start | bytes 1622024 | tf_op jit(solution)/shard_map/ppermute | solution.py:432
  111.1 11.1 %slice-start = ((s8[5242880]{0:T(1024)(128)(4,1)}), s8[4194304]{0:T(1024)(128)(4,1)S(1)}, s32[]{:S(2)}) async-start(s8[5242880]{0:T(1024)(128)(4,1)} %bitcast.48), calls=%async_computation | async-start | bytes 8388608
  114.0 8.2 %slice-start.1 = ((s8[5242880]{0:T(1024)(128)(4,1)}), s8[1048576]{0:T(1024)(128)(4,1)S(1)}, s32[]{:S(2)}) async-start(s8[5242880]{0:T(1024)(128)(4,1)} %bitcast.48), calls=%async_computation.1 | async-start | bytes 2097152
  123.9 2.3 %collective-permute-start.13 = (bf16[64,2560]{1,0:T(8,128)(2,1)S(1)}, bf16[64,2560]{1,0:T(8,128)(2,1)S(1)}, u32[]{:S(2)}, u32[]{:S(2)}) collective-permute-start(bf16[64,2560]{1,0:T(8,128)(2,1)S(1)} %get-tuple-element.59), channel_id=1, source_target_pairs={{0,1},{1,0},{2,3},{3,2},{4,5},{5,4},{6,7},{7,6},{8,9},{9,8},{10,11... | collective-permute-start | bytes 983048 | tf_op jit(solution)/shard_map/ppermute | solution.py:427
  123.9 2.2 %collective-permute-start.14 = (bf16[64,2560]{1,0:T(8,128)(2,1)S(1)}, bf16[64,2560]{1,0:T(8,128)(2,1)S(1)}, u32[]{:S(2)}, u32[]{:S(2)}) collective-permute-start(bf16[64,2560]{1,0:T(8,128)(2,1)S(1)} %get-tuple-element.60), channel_id=1, source_target_pairs={{0,1},{1,0},{2,3},{3,2},{4,5},{5,4},{6,7},{7,6},{8,9},{9,8},{10,11... | collective-permute-start | bytes 983048 | tf_op jit(solution)/shard_map/ppermute | solution.py:427
  124.4 14.3 %collective-permute-start.15 = (bf16[528,512]{1,0:T(8,128)(2,1)S(1)}, bf16[528,512]{1,0:T(8,128)(2,1)S(1)}, u32[]{:S(2)}, u32[]{:S(2)}) collective-permute-start(bf16[528,512]{1,0:T(8,128)(2,1)S(1)} %part_stage.2), channel_id=1, source_target_pairs={{0,4},{4,0},{1,5},{5,1},{2,6},{6,2},{3,7},{7,3},{8,12},{12,8},{9,1... | collective-permute-start | bytes 1622024 | tf_op jit(solution)/shard_map/ppermute | solution.py:432
  126.3 17.4 %collective-permute-start.18 = (bf16[128,2560]{1,0:T(8,128)(2,1)S(1)}, bf16[128,2560]{1,0:T(8,128)(2,1)S(1)}, u32[]{:S(2)}, u32[]{:S(2)}) collective-permute-start(bf16[128,2560]{1,0:T(8,128)(2,1)S(1)} %fusion.2), channel_id=1, source_target_pairs={{0,2},{1,3},{2,0},{3,1},{4,6},{5,7},{6,4},{7,5},{8,10},{9,11},{10,... | collective-permute-start | bytes 1966088 | tf_op jit(solution)/shard_map/ppermute | solution.py:427
  141.5 1.7 %collective-permute-start.16 = (bf16[64,2560]{1,0:T(8,128)(2,1)S(1)}, bf16[64,2560]{1,0:T(8,128)(2,1)S(1)}, u32[]{:S(2)}, u32[]{:S(2)}) collective-permute-start(bf16[64,2560]{1,0:T(8,128)(2,1)S(1)} %get-tuple-element.57), channel_id=1, source_target_pairs={{0,1},{1,0},{2,3},{3,2},{4,5},{5,4},{6,7},{7,6},{8,9},{9,8},{10,11... | collective-permute-start | bytes 983048 | tf_op jit(solution)/shard_map/ppermute | solution.py:427
  141.6 2.1 %collective-permute-start.17 = (bf16[64,2560]{1,0:T(8,128)(2,1)S(1)}, bf16[64,2560]{1,0:T(8,128)(2,1)S(1)}, u32[]{:S(2)}, u32[]{:S(2)}) collective-permute-start(bf16[64,2560]{1,0:T(8,128)(2,1)S(1)} %get-tuple-element.58), channel_id=1, source_target_pairs={{0,1},{1,0},{2,3},{3,2},{4,5},{5,4},{6,7},{7,6},{8,9},{9,8},{10,11... | collective-permute-start | bytes 983048 | tf_op jit(solution)/shard_map/ppermute | solution.py:427
